TPU v7x, 512 devices: a whole 4x8x8 slice. The times are simulated.
512 devices in a mesh: section: 16 (over y, x_lo), expert: 16 (over z, x_hi), tensor: 2 (over core).
Axes of the slice: x: 4 (x_hi: 2, x_lo: 2; x = x_hi * 2 + x_lo), y: 8, z: 8, core: 2. Of those that a mesh axis runs over, the one named last changes fastest.
Arguments:
- activations: bfloat16 [16, 2048, 2560], P('section', 'expert', 'tensor'), may hold values from -6 to 6
- norm_gain: bfloat16 [16, 2560], P('section'), may hold values from 0.099609375 to 1.8984375
- w_gate: bfloat16 [16, 2560, 8192], P('section', None, ('expert', 'tensor')), may hold values from -0.125 to 0.125
- w_up: bfloat16 [16, 2560, 8192], P('section', None, ('expert', 'tensor')), may hold values from -0.125 to 0.125
- w_down: bfloat16 [16, 8192, 2560], P('section', ('expert', 'tensor')), may hold values from -0.1875 to 0.1875
- route_ids: int32 [2, 16, 2048, 6], P(None, 'section', 'expert'), may hold values from 0 to 159, all different within a row; in each aligned block of 128 rows (0 to 127, 128 to 255, ..., all dimensions but the last counted through in order) at most 8 rows name the same one
- route_weights: float32 [2, 16, 2048, 6], P(None, 'section', 'expert'), may hold values from 0.25 to 2.5
Outputs:
- advanced: bfloat16 [16, 2048, 2560], P('section', 'expert', 'tensor')
Inputs may be any that keep to these rules, and one draw needn't show every extreme that they name: `route_ids`: each row names 6 different experts. Within the rows of one device (aligned blocks of 128 rows, for each tick and section) no expert is named by more than 8 rows, and in some blocks one expert is named by exactly 8.
All inputs are finite; a program needn't handle non-finite values.
Results may differ from a plain program's by a relative error of at most 0.01.
Values may be sent and summed in bfloat16 or wider, within the bound.
No kernel may reach another device: no remote copies, remote signals or barrier semaphores. Data moves between devices by JAX's collectives and lax.ppermute only.
A program may use at most 64 MiB of HBM per device.

v0:
```python
import jax
import jax.numpy as jnp
from jax import lax
from jax.sharding import PartitionSpec as P

TICKS = 2


NORM_EPS = 1e-06


def from_behind(array, axis, by):
    devices = lax.axis_size(axis)
    return lax.ppermute(array, axis, [(i, (i + by) % devices) for i in range(devices)])


def route_tables(block_ids, block_weights, window, capacity):
    tok_count = block_ids.shape[0]
    ids_major = block_ids.T
    weights_major = block_weights.T
    experts_col = jnp.arange(window, dtype=jnp.int32)[None, :, None]
    member = ids_major[:, None, :] == experts_col
    named = jnp.sum(member.astype(jnp.float32), axis=0)
    gate_of = jnp.sum(jnp.where(member, weights_major[:, None, :], 0.0), axis=0)
    row_pos = jnp.arange(tok_count, dtype=jnp.int32)
    strictly = (row_pos[:, None] < row_pos[None, :]).astype(jnp.bfloat16)
    earlier = jnp.dot(named.astype(jnp.bfloat16), strictly, preferred_element_type=jnp.float32)
    slot_col = jnp.arange(capacity, dtype=jnp.float32)[None, :, None]
    filled = named[:, None, :] * (earlier[:, None, :] == slot_col).astype(jnp.float32)
    dispatch_table = filled.reshape(window * capacity, tok_count)
    combine_table = (filled * gate_of[:, None, :]).reshape(window * capacity, tok_count)
    return (dispatch_table.astype(jnp.bfloat16), combine_table)


def local(activations, norm_gain, w_gate, w_up, w_down, route_ids, route_weights):
    current = activations[0]
    tok_rows = current.shape[0]
    half_width = current.shape[1]
    full_width = half_width * lax.axis_size("tensor")
    expert_count = lax.axis_size("expert")
    window = expert_count // 2
    capacity = tok_rows // 16
    gain_row = norm_gain[0].astype(jnp.float32)
    gate_w = w_gate[0]
    up_w = w_up[0]
    down_w = w_down[0]
    for tick_index in range(TICKS):
        current = from_behind(current, "section", 1)
        as_float = current.astype(jnp.float32)
        full_rows = lax.all_gather(current, "tensor", axis=1, tiled=True).astype(jnp.float32)
        rms_scale = jnp.sqrt(jnp.mean(full_rows * full_rows, axis=1, keepdims=True) + NORM_EPS)
        normed = (full_rows / rms_scale * gain_row).astype(jnp.bfloat16)
        row_width = normed.shape[1]
        dispatch_table, combine_table = route_tables(
            route_ids[tick_index, 0], route_weights[tick_index, 0], window, capacity
        )
        slot_rows = jnp.dot(dispatch_table, normed, preferred_element_type=jnp.float32).astype(
            jnp.bfloat16
        )
        slot_rows = slot_rows.reshape(window, capacity, row_width)
        outgoing = jnp.repeat(slot_rows, 2, axis=0)
        arrived = lax.all_to_all(outgoing, "expert", split_axis=0, concat_axis=0, tiled=True)
        flat_rows = arrived.reshape(expert_count * capacity, full_width)
        gate_act = jnp.dot(flat_rows, gate_w, preferred_element_type=jnp.float32)
        up_act = jnp.dot(flat_rows, up_w, preferred_element_type=jnp.float32)
        hidden = (jax.nn.silu(gate_act) * up_act).astype(jnp.bfloat16)
        partial_out = jnp.dot(hidden, down_w, preferred_element_type=jnp.float32).reshape(
            expert_count, capacity, full_width
        )
        summed = lax.psum_scatter(
            partial_out.astype(jnp.bfloat16), "tensor", scatter_dimension=2, tiled=True
        ).astype(jnp.float32)
        returned_rows = lax.all_to_all(
            summed.astype(jnp.bfloat16), "expert", split_axis=0, concat_axis=0, tiled=True
        ).astype(summed.dtype)
        expert_out = jnp.sum(returned_rows.reshape(window, 2, capacity, half_width), axis=1)
        moe_sum = lax.dot_general(
            combine_table,
            expert_out.reshape(window * capacity, half_width),
            (((0,), (0,)), ((), ())),
            precision=lax.Precision.HIGHEST,
            preferred_element_type=jnp.float32,
        )
        current = (as_float + moe_sum).astype(jnp.bfloat16)
    return current[None]


def solution(mesh):
    in_specs = (
        P("section", "expert", "tensor"),
        P("section", None),
        P("section", None, ("expert", "tensor")),
        P("section", None, ("expert", "tensor")),
        P("section", ("expert", "tensor"), None),
        P(None, "section", "expert", None),
        P(None, "section", "expert", None),
    )
    out_specs = P("section", "expert", "tensor")
    return jax.shard_map(local, mesh=mesh, in_specs=in_specs, out_specs=out_specs, check_vma=False)
```

profile of v0, /device:TPU:8, one launch (start us, length us, event | category | flops | bytes accessed | tf_op | source)
XLA Modules:
  0.0 186.6 jit_solution(1134317320348397802)
XLA Ops:
  6.5 0.0 copy-start
  6.5 0.0 reduce-scatter.3.cloned.1.call-start
  6.5 3.5 %collective-permute-start = (bf16[128,1280]{1,0:T(8,128)(2,1)}, bf16[128,1280]{1,0:T(8,128)(2,1)S(1)}, u32[]{:S(2)}, u32[]{:S(2)}) collective-permute-start(bf16[128,1280]{1,0:T(8,128)(2,1)} %bitcast.115), channel_id=1, source_target_pairs={{0,32},{32,64},{64,96},{96,128},{128,160},{160,192},{192,224},{224... | collective-permute-start | bytes 983048 | tf_op jit(solution)/shard_map/ppermute | solution.py:14
  10.1 0.7 fusion.100
  10.8 0.7 fusion.99
  11.5 0.7 convert_reduce_fusion.4
  12.2 0.1 eq.82
  12.3 0.1 fusion.62
  12.5 6.7 %collective-permute-done = bf16[128,1280]{1,0:T(8,128)(2,1)S(1)} collective-permute-done((bf16[128,1280]{1,0:T(8,128)(2,1)}, bf16[128,1280]{1,0:T(8,128)(2,1)S(1)}, u32[]{:S(2)}, u32[]{:S(2)}) %collective-permute-start) | collective-permute-done | bytes 327712 | tf_op jit(solution)/shard_map/ppermute | solution.py:14
  19.1 0.0 copy-start.4
  19.1 2.3 %all_gather.6 = bf16[128,2560]{1,0:T(8,128)(2,1)S(1)} all-gather(bf16[128,1280]{1,0:T(8,128)(2,1)S(1)} %collective-permute-done), channel_id=1, replica_groups=mesh['section'=16,'expert'=16,'tensor'=2] {'tensor'}, dimensions={1}, use_global_device_ids=true | all-gather | bytes 983040 | tf_op jit(solution)/shard_map/all_gather | solution.py:50
  21.4 0.2 fusion.2
  21.6 0.4 fusion
  22.0 0.0 copy-done.4
  22.0 0.0 copy-start.2
  22.1 35.5 %all_to_all.20 = bf16[16,8,2560]{2,1,0:T(8,128)(2,1)S(1)} all-to-all(bf16[16,8,2560]{2,1,0:T(8,128)(2,1)S(1)} %bitcast.113), channel_id=1, replica_groups=mesh['section'=16,'expert'=16,'tensor'=2] {'expert'}, dimensions={0} | all-to-all | bytes 1310720 | tf_op jit(solution)/shard_map/all_to_all | solution.py:62
  57.5 0.0 copy-done.2
  57.6 0.0 copy-start.1
  57.6 0.3 fusion.16
  57.9 0.0 copy-done
  57.9 1.0 copy-done.1
  58.9 1.7 convolution_convert_fusion.1
  60.6 0.0 reduce-scatter.3.cloned.1.call-update
  60.6 0.0 reduce-scatter.5.cloned.1.call-start
  60.7 11.4 %reduce-scatter.3.cloned.1.call-done = bf16[16,8,1280]{2,1,0:T(8,128)(2,1)} async-done(((bf16[16,8,2560]{2,1,0:T(8,128)(2,1)}), bf16[16,8,1280]{2,1,0:T(8,128)(2,1)}) %reduce-scatter.3.cloned.1.call-update) | async-done | bytes 327696 | tf_op jit(solution)/shard_map/reduce_scatter | solution.py:70
  72.1 0.0 copy-start.5
  72.1 25.5 %all_to_all.21 = bf16[16,8,1280]{2,1,0:T(8,128)(2,1)S(1)} all-to-all(bf16[16,8,1280]{2,1,0:T(8,128)(2,1)} %reduce-scatter.3.cloned.1.call-done), channel_id=1, replica_groups=mesh['section'=16,'expert'=16,'tensor'=2] {'expert'}, dimensions={0} | all-to-all | bytes 655360 | tf_op jit(solution)/shard_map/all_to_all | solution.py:73
  97.6 0.0 copy-done.5
  97.6 0.7 add_convert_fusion.1
  98.4 2.5 %collective-permute-start.1 = (bf16[128,1280]{1,0:T(8,128)(2,1)S(1)}, bf16[128,1280]{1,0:T(8,128)(2,1)S(1)}, u32[]{:S(2)}, u32[]{:S(2)}) collective-permute-start(bf16[128,1280]{1,0:T(8,128)(2,1)S(1)} %add_convert_fusion.1), channel_id=1, source_target_pairs={{0,32},{32,64},{64,96},{96,128},{128,160},{160,192},{192,224},{224... | collective-permute-start | bytes 983048 | tf_op jit(solution)/shard_map/ppermute | solution.py:14
  100.9 0.1 fusion.61
  101.0 8.4 %collective-permute-done.1 = bf16[128,1280]{1,0:T(8,128)(2,1)S(1)} collective-permute-done((bf16[128,1280]{1,0:T(8,128)(2,1)S(1)}, bf16[128,1280]{1,0:T(8,128)(2,1)S(1)}, u32[]{:S(2)}, u32[]{:S(2)}) %collective-permute-start.1) | collective-permute-done | bytes 327712 | tf_op jit(solution)/shard_map/ppermute | solution.py:14
  109.4 0.0 copy-start.6
  109.4 0.7 copy-done.6
  110.1 2.3 %all_gather.7 = bf16[128,2560]{1,0:T(8,128)(2,1)S(1)} all-gather(bf16[128,1280]{1,0:T(8,128)(2,1)S(1)} %collective-permute-done.1), channel_id=1, replica_groups=mesh['section'=16,'expert'=16,'tensor'=2] {'tensor'}, dimensions={1}, use_global_device_ids=true | all-gather | bytes 983040 | tf_op jit(solution)/shard_map/all_gather | solution.py:50
  112.3 0.2 fusion.5
  112.6 0.4 fusion.1
  113.0 0.0 copy-start.3
  113.0 26.6 %all_to_all.22 = bf16[16,8,2560]{2,1,0:T(8,128)(2,1)S(1)} all-to-all(bf16[16,8,2560]{2,1,0:T(8,128)(2,1)S(1)} %bitcast.114), channel_id=1, replica_groups=mesh['section'=16,'expert'=16,'tensor'=2] {'expert'}, dimensions={0} | all-to-all | bytes 1310720 | tf_op jit(solution)/shard_map/all_to_all | solution.py:62
  139.7 0.0 copy-done.3
  139.7 0.3 fusion.14
  140.0 1.7 convolution_convert_fusion
  141.8 0.0 copy-start.7
  141.8 0.0 reduce-scatter.5.cloned.1.call-update
  141.8 11.2 %reduce-scatter.5.cloned.1.call-done = bf16[16,8,1280]{2,1,0:T(8,128)(2,1)} async-done(((bf16[16,8,2560]{2,1,0:T(8,128)(2,1)}), bf16[16,8,1280]{2,1,0:T(8,128)(2,1)}) %reduce-scatter.5.cloned.1.call-update) | async-done | bytes 327696 | tf_op jit(solution)/shard_map/reduce_scatter | solution.py:70
  153.0 25.3 %all_to_all.23 = bf16[16,8,1280]{2,1,0:T(8,128)(2,1)S(1)} all-to-all(bf16[16,8,1280]{2,1,0:T(8,128)(2,1)} %reduce-scatter.5.cloned.1.call-done), channel_id=1, replica_groups=mesh['section'=16,'expert'=16,'tensor'=2] {'expert'}, dimensions={0} | all-to-all | bytes 655360 | tf_op jit(solution)/shard_map/all_to_all | solution.py:73
  178.3 0.0 copy-done.7
  178.3 1.5 fusion.48
  (11 shorter events, 0.2 us)
Async XLA Ops:
  6.5 51.4 %copy-start = (bf16[1,256,2560]{2,1,0:T(8,128)(2,1)S(1)}, bf16[1,256,2560]{2,1,0:T(8,128)(2,1)}, u32[]{:S(2)}) copy-start(bf16[1,256,2560]{2,1,0:T(8,128)(2,1)} %param.11) | copy-start | bytes 3932164
  6.5 65.6 %reduce-scatter.3.cloned.1.call-start = ((), (), s32[]{:S(2)}) async-start(), calls=%async_computation.6 | async-start | bytes 983040 | tf_op jit(solution)/shard_map/reduce_scatter | solution.py:70
  6.5 12.6 %collective-permute-start = (bf16[128,1280]{1,0:T(8,128)(2,1)}, bf16[128,1280]{1,0:T(8,128)(2,1)S(1)}, u32[]{:S(2)}, u32[]{:S(2)}) collective-permute-start(bf16[128,1280]{1,0:T(8,128)(2,1)} %bitcast.115), channel_id=1, source_target_pairs={{0,32},{32,64},{64,96},{96,128},{128,160},{160,192},{192,224},{224... | collective-permute-start | bytes 983048 | tf_op jit(solution)/shard_map/ppermute | solution.py:14
  19.1 2.9 %copy-start.4 = (bf16[128,1280]{1,0:T(8,128)(2,1)}, bf16[128,1280]{1,0:T(8,128)(2,1)S(1)}, u32[]{:S(2)}) copy-start(bf16[128,1280]{1,0:T(8,128)(2,1)S(1)} %collective-permute-done) | copy-start | bytes 983044
  22.0 35.5 %copy-start.2 = (bf16[1,2560,256]{2,1,0:T(8,128)(2,1)S(1)}, bf16[1,2560,256]{2,1,0:T(8,128)(2,1)}, u32[]{:S(2)}) copy-start(bf16[1,2560,256]{2,1,0:T(8,128)(2,1)} %param.9) | copy-start | bytes 3932164
  57.6 1.3 copy-start.1
  60.6 92.3 %reduce-scatter.5.cloned.1.call-start = ((), (), s32[]{:S(2)}) async-start(), calls=%async_computation.7 | async-start | bytes 983040 | tf_op jit(solution)/shard_map/reduce_scatter | solution.py:70
  72.1 25.5 %copy-start.5 = (bf16[128,1280]{1,0:T(8,128)(2,1)S(1)}, bf16[128,1280]{1,0:T(8,128)(2,1)}, u32[]{:S(2)}) copy-start(bf16[128,1280]{1,0:T(8,128)(2,1)} %copy-done.4) | copy-start | bytes 983044
  98.4 11.0 %collective-permute-start.1 = (bf16[128,1280]{1,0:T(8,128)(2,1)S(1)}, bf16[128,1280]{1,0:T(8,128)(2,1)S(1)}, u32[]{:S(2)}, u32[]{:S(2)}) collective-permute-start(bf16[128,1280]{1,0:T(8,128)(2,1)S(1)} %add_convert_fusion.1), channel_id=1, source_target_pairs={{0,32},{32,64},{64,96},{96,128},{128,160},{160,192},{192,224},{224... | collective-permute-start | bytes 983048 | tf_op jit(solution)/shard_map/ppermute | solution.py:14
  109.4 0.7 copy-start.6
  113.0 26.7 %copy-start.3 = (bf16[1,2560,256]{2,1,0:T(8,128)(2,1)S(1)}, bf16[1,2560,256]{2,1,0:T(8,128)(2,1)}, u32[]{:S(2)}) copy-start(bf16[1,2560,256]{2,1,0:T(8,128)(2,1)} %param.9) | copy-start | bytes 3932164
  141.8 36.6 %copy-start.7 = (bf16[128,1280]{1,0:T(8,128)(2,1)S(1)}, bf16[128,1280]{1,0:T(8,128)(2,1)}, u32[]{:S(2)}) copy-start(bf16[128,1280]{1,0:T(8,128)(2,1)} %copy-done.6) | copy-start | bytes 983044
Sparse Core Ops, SparseCore 0:
  60.8 11.3 reduce-scatter.2
  141.9 11.0 reduce-scatter.4
where the time goes:
time: 187 us
  blocking collectives  117 us (63%)
  waiting for transfers between devices  37.6 us (20%)
  between operations  13.5 us (7%)
  matrix products  7.46 us (4%)
  starting transfers between devices  6.04 us (3%)
  local copies, waits for them, and re-layouts  3.29 us (2%)
    all_to_all x2, blocking collectives, local(): lax.all_to_all(outgoing, 'expert', split_axis=0, concat_axis=0, tiled=True)  62.1 us
    all_to_all x2, blocking collectives, local(): lax.all_to_all(summed.astype(jnp.bfloat16), 'expert', split_axis=0, conca...  50.8 us
    reduce_scatter x2, waiting for transfers between devices, local(): lax.psum_scatter(partial_out.astype(jnp.bfloat16), 'tensor', scatter_dime...  22.6 us
    ppermute x2, waiting for transfers between devices, from_behind(): lax.ppermute(array, axis, [(i, (i + by) % devices) for i in range(devices)])  15 us
    ppermute x2, starting transfers between devices, from_behind(): lax.ppermute(array, axis, [(i, (i + by) % devices) for i in range(devices)])  6 us
    all_gather x2, blocking collectives, local(): lax.all_gather(current, 'tensor', axis=1, tiled=True).astype(jnp.float32)  4.52 us
  transfers between devices with their start and end apart: 4, of which 4 were waited for; matrix products, arithmetic and copies ran while one was open for 1% of the time, Pallas kernels for 0%

commit v1 on v0

--- a/solution.py
+++ b/solution.py
@@ -43,37 +43,41 @@
     gain_row = norm_gain[0].astype(jnp.float32)
     gate_w = w_gate[0]
     up_w = w_up[0]
-    down_w = w_down[0]
+    down_w = lax.all_to_all(w_down[0], "tensor", split_axis=1, concat_axis=0, tiled=True)
     for tick_index in range(TICKS):
         current = from_behind(current, "section", 1)
-        as_float = current.astype(jnp.float32)
-        full_rows = lax.all_gather(current, "tensor", axis=1, tiled=True).astype(jnp.float32)
-        rms_scale = jnp.sqrt(jnp.mean(full_rows * full_rows, axis=1, keepdims=True) + NORM_EPS)
-        normed = (full_rows / rms_scale * gain_row).astype(jnp.bfloat16)
-        row_width = normed.shape[1]
         dispatch_table, combine_table = route_tables(
             route_ids[tick_index, 0], route_weights[tick_index, 0], window, capacity
         )
-        slot_rows = jnp.dot(dispatch_table, normed, preferred_element_type=jnp.float32).astype(
+        dispatch_twice = jnp.repeat(
+            dispatch_table.reshape(window, capacity, tok_rows), 2, axis=0
+        ).reshape(expert_count * capacity, tok_rows)
+        outgoing = jnp.dot(dispatch_twice, current, preferred_element_type=jnp.float32).astype(
             jnp.bfloat16
         )
-        slot_rows = slot_rows.reshape(window, capacity, row_width)
-        outgoing = jnp.repeat(slot_rows, 2, axis=0)
-        arrived = lax.all_to_all(outgoing, "expert", split_axis=0, concat_axis=0, tiled=True)
-        flat_rows = arrived.reshape(expert_count * capacity, full_width)
-        gate_act = jnp.dot(flat_rows, gate_w, preferred_element_type=jnp.float32)
-        up_act = jnp.dot(flat_rows, up_w, preferred_element_type=jnp.float32)
+        arrived = lax.all_to_all(
+            outgoing.reshape(expert_count, capacity, half_width),
+            "expert",
+            split_axis=0,
+            concat_axis=0,
+            tiled=True,
+        ).reshape(expert_count * capacity, half_width)
+        rows = lax.all_gather(arrived, "tensor", axis=1, tiled=True).astype(jnp.float32)
+        rms_scale = jnp.sqrt(jnp.mean(rows * rows, axis=1, keepdims=True) + NORM_EPS)
+        normed = (rows / rms_scale * gain_row).astype(jnp.bfloat16)
+        gate_act = jnp.dot(normed, gate_w, preferred_element_type=jnp.float32)
+        up_act = jnp.dot(normed, up_w, preferred_element_type=jnp.float32)
         hidden = (jax.nn.silu(gate_act) * up_act).astype(jnp.bfloat16)
-        partial_out = jnp.dot(hidden, down_w, preferred_element_type=jnp.float32).reshape(
-            expert_count, capacity, full_width
-        )
-        summed = lax.psum_scatter(
-            partial_out.astype(jnp.bfloat16), "tensor", scatter_dimension=2, tiled=True
+        hidden = lax.all_gather(hidden, "tensor", axis=1, tiled=True)
+        partial_out = jnp.dot(hidden, down_w, preferred_element_type=jnp.float32)
+        returned = lax.all_to_all(
+            partial_out.astype(jnp.bfloat16).reshape(expert_count, capacity, half_width),
+            "expert",
+            split_axis=0,
+            concat_axis=0,
+            tiled=True,
         ).astype(jnp.float32)
-        returned_rows = lax.all_to_all(
-            summed.astype(jnp.bfloat16), "expert", split_axis=0, concat_axis=0, tiled=True
-        ).astype(summed.dtype)
-        expert_out = jnp.sum(returned_rows.reshape(window, 2, capacity, half_width), axis=1)
+        expert_out = jnp.sum(returned.reshape(window, 2, capacity, half_width), axis=1)
         moe_sum = lax.dot_general(
             combine_table,
             expert_out.reshape(window * capacity, half_width),
@@ -81,7 +85,7 @@
             precision=lax.Precision.HIGHEST,
             preferred_element_type=jnp.float32,
         )
-        current = (as_float + moe_sum).astype(jnp.bfloat16)
+        current = (current.astype(jnp.float32) + moe_sum).astype(jnp.bfloat16)
     return current[None]
 
 

time: 187 us -> 126 us (0.67)
  the two profiles are of different devices: /device:TPU:8 before, /device:TPU:32 now
where the time goes in v1:
time: 126 us
  blocking collectives  44.8 us (36%)
  waiting for transfers between devices  41.9 us (33%)
  starting transfers between devices  25.6 us (20%)
  matrix products  6.65 us (5%)
  local copies, waits for them, and re-layouts  5.93 us (5%)
    all_to_all x1, blocking collectives, local(): lax.all_to_all(partial_out.astype(jnp.bfloat16).reshape(expert_count, cap...  18.5 us
    all_to_all x1, blocking collectives, local(): lax.all_to_all(outgoing.reshape(expert_count, capacity, half_width), 'exp...  17.9 us
    all_to_all x1, waiting for transfers between devices, local(): lax.all_to_all(partial_out.astype(jnp.bfloat16).reshape(expert_count, cap...  15.9 us
    ppermute x2, waiting for transfers between devices, from_behind(): lax.ppermute(array, axis, [(i, (i + by) % devices) for i in range(devices)])  13.6 us
    all_to_all x1, starting transfers between devices, local(): lax.all_to_all(outgoing.reshape(expert_count, capacity, half_width), 'exp...  12.9 us
    all_to_all x1, waiting for transfers between devices, local(): lax.all_to_all(outgoing.reshape(expert_count, capacity, half_width), 'exp...  12.4 us
    ppermute x2, starting transfers between devices, from_behind(): lax.ppermute(array, axis, [(i, (i + by) % devices) for i in range(devices)])  5.44 us
    all_gather x2, blocking collectives, local(): lax.all_gather(arrived, 'tensor', axis=1, tiled=True).astype(jnp.float32)  4.53 us
  transfers between devices with their start and end apart: 5, of which 4 were waited for; matrix products, arithmetic and copies ran while one was open for 4% of the time, Pallas kernels for 0%

profile of v1, /device:TPU:32, one launch (start us, length us, event | category | flops | bytes accessed | tf_op | source)
XLA Modules:
  0.0 125.8 jit_solution(13811037970939792285)
XLA Ops:
  0.0 0.0 copy-start
  0.0 3.5 %collective-permute-start = (bf16[128,1280]{1,0:T(8,128)(2,1)}, bf16[128,1280]{1,0:T(8,128)(2,1)S(1)}, u32[]{:S(2)}, u32[]{:S(2)}) collective-permute-start(bf16[128,1280]{1,0:T(8,128)(2,1)} %bitcast.84), channel_id=1, source_target_pairs={{0,32},{32,64},{64,96},{96,128},{128,160},{160,192},{192,224},{224... | collective-permute-start | bytes 983048 | tf_op jit(solution)/shard_map/ppermute | solution.py:14
  3.5 2.4 %copy.10 = bf16[1,256,2560]{1,2,0:T(8,128)(2,1)} copy(bf16[1,256,2560]{2,1,0:T(8,128)(2,1)} %param.11) | data formatting | bytes 2621440 | tf_op args[4]
  6.0 0.0 copy-start.3
  6.0 0.0 copy-start.4
  6.0 3.8 %all-to-all-start.1 = ((bf16[256,2,1280]{0,2,1:T(8,128)(2,1)}), bf16[256,2,1280]{0,2,1:T(8,128)(2,1)S(1)}, u32[]{:S(2)}, u32[]{:S(2)}) async-start(bf16[256,2,1280]{0,2,1:T(8,128)(2,1)} %bitcast.79), calls=%async_computation.1 | async-start | bytes 2621440 | tf_op jit(solution)/shard_map/all_to_all | solution.py:46
  9.7 0.0 copy-done.3
  9.8 0.0 copy-done.4
  9.8 0.1 fusion.32
  10.0 3.8 %collective-permute-done = bf16[128,1280]{1,0:T(8,128)(2,1)S(1)} collective-permute-done((bf16[128,1280]{1,0:T(8,128)(2,1)}, bf16[128,1280]{1,0:T(8,128)(2,1)S(1)}, u32[]{:S(2)}, u32[]{:S(2)}) %collective-permute-start) | collective-permute-done | bytes 327712 | tf_op jit(solution)/shard_map/ppermute | solution.py:14
  13.8 1.0 fusion
  14.8 0.0 all-to-all-done.1
  14.8 0.0 copy-start.1
  14.8 12.9 %all-to-all-start = ((bf16[16,8,1280]{2,1,0:T(8,128)(2,1)}), bf16[16,8,1280]{2,1,0:T(8,128)(2,1)S(1)}, u32[]{:S(2)}, u32[]{:S(2)}) async-start(bf16[16,8,1280]{2,1,0:T(8,128)(2,1)} %fusion), calls=%async_computation | async-start | bytes 655360 | tf_op jit(solution)/shard_map/all_to_all | solution.py:58
  27.6 0.0 copy-done.1
  27.7 0.0 copy-start.2
  27.7 1.6 %copy.11 = bf16[2,256,1280]{2,1,0:T(8,128)(2,1)S(1)} copy(bf16[2,256,1280]{1,2,0:T(8,128)(2,1)} %bitcast.78) | data formatting | bytes 2621440 | tf_op jit(solution)/shard_map/all_to_all | solution.py:46
  29.3 0.0 copy-done.2
  29.3 12.4 %all-to-all-done = bf16[16,8,1280]{2,1,0:T(8,128)(2,1)S(1)} async-done(((bf16[16,8,1280]{2,1,0:T(8,128)(2,1)}), bf16[16,8,1280]{2,1,0:T(8,128)(2,1)S(1)}, u32[]{:S(2)}, u32[]{:S(2)}) %all-to-all-start) | async-done | bytes 327712 | tf_op jit(solution)/shard_map/all_to_all | solution.py:58
  41.7 2.3 %all_gather.12 = bf16[128,2560]{1,0:T(8,128)(2,1)S(1)} all-gather(bf16[128,1280]{1,0:T(8,128)(2,1)S(1)} %bitcast.80), channel_id=1, replica_groups=mesh['section'=16,'expert'=16,'tensor'=2] {'tensor'}, dimensions={1}, use_global_device_ids=true | all-gather | bytes 983040 | tf_op jit(solution)/shard_map/all_gather | solution.py:65
  44.0 0.2 fusion.4
  44.2 0.0 copy-done
  44.2 0.0 copy-start.5
  44.2 0.4 fusion.16
  44.6 0.9 copy-done.5
  45.5 0.4 fusion.27
  45.9 1.9 %all_gather.13 = bf16[128,512]{1,0:T(8,128)(2,1)S(1)} all-gather(bf16[128,256]{1,0:T(8,128)(2,1)S(1)} %fusion.27), channel_id=1, replica_groups=mesh['section'=16,'expert'=16,'tensor'=2] {'tensor'}, dimensions={1}, use_global_device_ids=true | all-gather | bytes 196608 | tf_op jit(solution)/shard_map/all_gather | solution.py:71
  47.8 1.1 fusion.2
  48.9 3.5 %all-to-all-start.2 = ((bf16[16,8,1280]{2,1,0:T(8,128)(2,1)}), bf16[16,8,1280]{2,1,0:T(8,128)(2,1)S(1)}, u32[]{:S(2)}, u32[]{:S(2)}) async-start(bf16[16,8,1280]{2,1,0:T(8,128)(2,1)} %fusion.2), calls=%async_computation.2 | async-start | bytes 655360 | tf_op jit(solution)/shard_map/all_to_all | solution.py:73
  52.5 15.9 %all-to-all-done.2 = bf16[16,8,1280]{2,1,0:T(8,128)(2,1)S(1)} async-done(((bf16[16,8,1280]{2,1,0:T(8,128)(2,1)}), bf16[16,8,1280]{2,1,0:T(8,128)(2,1)S(1)}, u32[]{:S(2)}, u32[]{:S(2)}) %all-to-all-start.2) | async-done | bytes 327712 | tf_op jit(solution)/shard_map/all_to_all | solution.py:73
  68.4 0.7 add_convert_fusion.1
  69.2 1.9 %collective-permute-start.1 = (bf16[128,1280]{1,0:T(8,128)(2,1)S(1)}, bf16[128,1280]{1,0:T(8,128)(2,1)S(1)}, u32[]{:S(2)}, u32[]{:S(2)}) collective-permute-start(bf16[128,1280]{1,0:T(8,128)(2,1)S(1)} %add_convert_fusion.1), channel_id=1, source_target_pairs={{0,32},{32,64},{64,96},{96,128},{128,160},{160,192},{192,224},{224... | collective-permute-start | bytes 983048 | tf_op jit(solution)/shard_map/ppermute | solution.py:14
  71.1 0.1 fusion.31
  71.2 9.8 %collective-permute-done.1 = bf16[128,1280]{1,0:T(8,128)(2,1)S(1)} collective-permute-done((bf16[128,1280]{1,0:T(8,128)(2,1)S(1)}, bf16[128,1280]{1,0:T(8,128)(2,1)S(1)}, u32[]{:S(2)}, u32[]{:S(2)}) %collective-permute-start.1) | collective-permute-done | bytes 327712 | tf_op jit(solution)/shard_map/ppermute | solution.py:14
  81.1 0.2 fusion.1
  81.3 17.9 %all_to_all.39 = bf16[16,8,1280]{2,1,0:T(8,128)(2,1)S(1)} all-to-all(bf16[16,8,1280]{2,1,0:T(8,128)(2,1)S(1)} %fusion.1), channel_id=1, replica_groups=mesh['section'=16,'expert'=16,'tensor'=2] {'expert'}, dimensions={0} | all-to-all | bytes 655360 | tf_op jit(solution)/shard_map/all_to_all | solution.py:58
  99.2 2.3 %all_gather.14 = bf16[128,2560]{1,0:T(8,128)(2,1)S(1)} all-gather(bf16[128,1280]{1,0:T(8,128)(2,1)S(1)} %bitcast.81), channel_id=1, replica_groups=mesh['section'=16,'expert'=16,'tensor'=2] {'tensor'}, dimensions={1}, use_global_device_ids=true | all-gather | bytes 983040 | tf_op jit(solution)/shard_map/all_gather | solution.py:65
  101.5 0.2 fusion.7
  101.7 0.0 copy-start.6
  101.7 0.4 fusion.14
  102.1 0.9 copy-done.6
  103.0 0.4 fusion.24
  103.4 1.9 %all_gather.15 = bf16[128,512]{1,0:T(8,128)(2,1)S(1)} all-gather(bf16[128,256]{1,0:T(8,128)(2,1)S(1)} %fusion.24), channel_id=1, replica_groups=mesh['section'=16,'expert'=16,'tensor'=2] {'tensor'}, dimensions={1}, use_global_device_ids=true | all-gather | bytes 196608 | tf_op jit(solution)/shard_map/all_gather | solution.py:71
  105.3 0.3 fusion.3
  105.7 18.5 %all_to_all.40 = bf16[16,8,1280]{2,1,0:T(8,128)(2,1)S(1)} all-to-all(bf16[16,8,1280]{2,1,0:T(8,128)(2,1)S(1)} %fusion.3), channel_id=1, replica_groups=mesh['section'=16,'expert'=16,'tensor'=2] {'expert'}, dimensions={0} | all-to-all | bytes 655360 | tf_op jit(solution)/shard_map/all_to_all | solution.py:73
  124.3 1.5 %fusion.30 = bf16[1,128,1280]{2,1,0:T(8,128)(2,1)} fusion(bf16[128,1280]{1,0:T(8,128)(2,1)S(1)} %collective-permute-done.1, f32[8,8,1280]{2,1,0:T(8,128)S(1)} %convert_reduce_fusion, f32[8,128]{1,0:T(8,128)S(1)} %get-tuple-element.5, f32[8,128]{1,0:T(8,128)S(1)} %get-tuple-element.6, f32[8,128]{1,0:T(8,128)S(1)} %fusion.31), kind=kOutput, calls=%fused_computation.36 | convolution fusion | flops 126345216 | bytes 995328 | tf_op jit(solution)/shard_map/dot_general | solution.py:81
  (15 shorter events, 0.2 us)
Async XLA Ops:
  0.0 44.2 %copy-start = (bf16[1,2560,256]{2,1,0:T(8,128)(2,1)S(1)}, bf16[1,2560,256]{2,1,0:T(8,128)(2,1)}, u32[]{:S(2)}) copy-start(bf16[1,2560,256]{2,1,0:T(8,128)(2,1)} %param.9) | copy-start | bytes 3932164
  0.0 13.8 %collective-permute-start = (bf16[128,1280]{1,0:T(8,128)(2,1)}, bf16[128,1280]{1,0:T(8,128)(2,1)S(1)}, u32[]{:S(2)}, u32[]{:S(2)}) collective-permute-start(bf16[128,1280]{1,0:T(8,128)(2,1)} %bitcast.84), channel_id=1, source_target_pairs={{0,32},{32,64},{64,96},{96,128},{128,160},{160,192},{192,224},{224... | collective-permute-start | bytes 983048 | tf_op jit(solution)/shard_map/ppermute | solution.py:14
  6.0 3.8 %copy-start.3 = (f32[2,1,128,6]{2,1,3,0:T(1,128)S(1)}, f32[2,1,128,6]{2,1,3,0:T(1,128)}, u32[]{:S(2)}) copy-start(f32[2,1,128,6]{2,1,3,0:T(1,128)} %param.13) | copy-start | bytes 18436
  6.0 3.8 %copy-start.4 = (s32[2,1,128,6]{2,1,3,0:T(1,128)S(1)}, s32[2,1,128,6]{2,1,3,0:T(1,128)}, u32[]{:S(2)}) copy-start(s32[2,1,128,6]{2,1,3,0:T(1,128)} %param.12) | copy-start | bytes 18436
  6.0 8.8 %all-to-all-start.1 = ((bf16[256,2,1280]{0,2,1:T(8,128)(2,1)}), bf16[256,2,1280]{0,2,1:T(8,128)(2,1)S(1)}, u32[]{:S(2)}, u32[]{:S(2)}) async-start(bf16[256,2,1280]{0,2,1:T(8,128)(2,1)} %bitcast.79), calls=%async_computation.1 | async-start | bytes 2621440 | tf_op jit(solution)/shard_map/all_to_all | solution.py:46
  14.8 12.9 %copy-start.1 = (bf16[256,2,1280]{0,2,1:T(8,128)(2,1)}, bf16[256,2,1280]{0,2,1:T(8,128)(2,1)S(1)}, u32[]{:S(2)}) copy-start(bf16[256,2,1280]{0,2,1:T(8,128)(2,1)S(1)} %all-to-all-done.1) | copy-start | bytes 3932164
  14.8 26.9 %all-to-all-start = ((bf16[16,8,1280]{2,1,0:T(8,128)(2,1)}), bf16[16,8,1280]{2,1,0:T(8,128)(2,1)S(1)}, u32[]{:S(2)}, u32[]{:S(2)}) async-start(bf16[16,8,1280]{2,1,0:T(8,128)(2,1)} %fusion), calls=%async_computation | async-start | bytes 655360 | tf_op jit(solution)/shard_map/all_to_all | solution.py:58
  27.7 1.6 %copy-start.2 = (bf16[1,2560]{1,0:T(2,128)(2,1)S(1)}, bf16[1,2560]{1,0:T(2,128)(2,1)}, u32[]{:S(2)}) copy-start(bf16[1,2560]{1,0:T(2,128)(2,1)} %param.8) | copy-start | bytes 15364
  44.2 1.3 %copy-start.5 = (bf16[1,2560,256]{2,1,0:T(8,128)(2,1)S(1)}, bf16[1,2560,256]{2,1,0:T(8,128)(2,1)}, u32[]{:S(2)}) copy-start(bf16[1,2560,256]{2,1,0:T(8,128)(2,1)} %param.10) | copy-start | bytes 3932164
  48.9 19.5 %all-to-all-start.2 = ((bf16[16,8,1280]{2,1,0:T(8,128)(2,1)}), bf16[16,8,1280]{2,1,0:T(8,128)(2,1)S(1)}, u32[]{:S(2)}, u32[]{:S(2)}) async-start(bf16[16,8,1280]{2,1,0:T(8,128)(2,1)} %fusion.2), calls=%async_computation.2 | async-start | bytes 655360 | tf_op jit(solution)/shard_map/all_to_all | solution.py:73
  69.2 11.9 %collective-permute-start.1 = (bf16[128,1280]{1,0:T(8,128)(2,1)S(1)}, bf16[128,1280]{1,0:T(8,128)(2,1)S(1)}, u32[]{:S(2)}, u32[]{:S(2)}) collective-permute-start(bf16[128,1280]{1,0:T(8,128)(2,1)S(1)} %add_convert_fusion.1), channel_id=1, source_target_pairs={{0,32},{32,64},{64,96},{96,128},{128,160},{160,192},{192,224},{224... | collective-permute-start | bytes 983048 | tf_op jit(solution)/shard_map/ppermute | solution.py:14
  101.7 1.3 %copy-start.6 = (bf16[1,2560,256]{2,1,0:T(8,128)(2,1)S(1)}, bf16[1,2560,256]{2,1,0:T(8,128)(2,1)}, u32[]{:S(2)}) copy-start(bf16[1,2560,256]{2,1,0:T(8,128)(2,1)} %param.10) | copy-start | bytes 3932164

commit v2 on v1

v2 whole, which is shorter than its diff:
```python
import jax
import jax.numpy as jnp
from jax import lax
from jax.sharding import PartitionSpec as P

NORM_EPS = 1e-06


def from_behind(array, by, flip=0):
    sections, experts = lax.axis_size("section"), lax.axis_size("expert")
    pairs = [
        (s * experts + e, (s + by) % sections * experts + (e ^ flip))
        for s in range(sections)
        for e in range(experts)
    ]
    return lax.ppermute(array, ("section", "expert"), pairs)


def slots_of(ids_major, window, capacity):
    tok_count = ids_major.shape[1]
    experts_col = jnp.arange(window, dtype=jnp.int32)[None, :, None]
    member = ids_major[:, None, :] == experts_col
    named = jnp.sum(member.astype(jnp.float32), axis=0)
    row_pos = jnp.arange(tok_count, dtype=jnp.int32)
    strictly = (row_pos[:, None] < row_pos[None, :]).astype(jnp.bfloat16)
    earlier = jnp.dot(named.astype(jnp.bfloat16), strictly, preferred_element_type=jnp.float32)
    slot_col = jnp.arange(capacity, dtype=jnp.float32)[None, :, None]
    filled = named[:, None, :] * (earlier[:, None, :] == slot_col).astype(jnp.float32)
    return filled, member


def dispatch_rows(ids_major, window, capacity):
    filled, _ = slots_of(ids_major, window, capacity)
    return filled.reshape(window * capacity, -1).astype(jnp.bfloat16)


def combine_rows(ids_major, weights_major, window, capacity):
    filled, member = slots_of(ids_major, window, capacity)
    gate_of = jnp.sum(jnp.where(member, weights_major[:, None, :], 0.0), axis=0)
    return (filled * gate_of[:, None, :]).reshape(window * capacity, -1)


def local(activations, norm_gain, w_gate, w_up, w_down, route_ids, route_weights):
    start = activations[0]
    tok_rows, half_width = start.shape
    expert_count = lax.axis_size("expert")
    window = expert_count // 2
    capacity = tok_rows // 16
    slots = expert_count * capacity
    gain_row = norm_gain[0].astype(jnp.float32)
    gate_w = w_gate[0]
    up_w = w_up[0]

    current = from_behind(start, 1)
    routes = jnp.concatenate(
        [route_ids[0, 0].T.astype(jnp.float32), route_weights[0, 0].T], axis=0
    )
    routes_on = from_behind(routes, 1)
    residual = from_behind(start, 2)
    down_w = lax.all_to_all(w_down[0], "tensor", split_axis=1, concat_axis=0, tiled=True)

    def dispatch(tokens, ids):
        table = dispatch_rows(ids, window, capacity)
        twice = jnp.repeat(table.reshape(window, capacity, tok_rows), 2, axis=0)
        outgoing = jnp.dot(
            twice.reshape(slots, tok_rows), tokens, preferred_element_type=jnp.float32
        ).astype(jnp.bfloat16)
        arrived = lax.all_to_all(
            outgoing.reshape(expert_count, capacity, half_width), "expert", 0, 0, tiled=True
        )
        return arrived.reshape(slots, half_width)

    def experts(arrived):
        rows = lax.all_gather(arrived, "tensor", axis=1, tiled=True).astype(jnp.float32)
        rms_scale = jnp.sqrt(jnp.mean(rows * rows, axis=1, keepdims=True) + NORM_EPS)
        normed = (rows / rms_scale * gain_row).astype(jnp.bfloat16)
        gate_act = jnp.dot(normed, gate_w, preferred_element_type=jnp.float32)
        up_act = jnp.dot(normed, up_w, preferred_element_type=jnp.float32)
        hidden = (jax.nn.silu(gate_act) * up_act).astype(jnp.bfloat16)
        hidden = lax.all_gather(hidden, "tensor", axis=1, tiled=True)
        return jnp.dot(hidden, down_w, preferred_element_type=jnp.float32).astype(jnp.bfloat16)

    def combine(tokens, rows, ids, weights):
        moe_sum = lax.dot_general(
            combine_rows(ids, weights, window, capacity),
            rows.astype(jnp.float32),
            (((0,), (0,)), ((), ())),
            precision=lax.Precision.HIGHEST,
            preferred_element_type=jnp.float32,
        )
        return (tokens.astype(jnp.float32) + moe_sum).astype(jnp.bfloat16)

    partial = experts(dispatch(current, route_ids[0, 0].T))
    by_side = partial.reshape(window, 2, capacity, half_width)
    side = lax.axis_index("expert") % 2
    straight = lax.dynamic_index_in_dim(by_side, side, 1, keepdims=False)
    crossed = lax.dynamic_index_in_dim(by_side, 1 - side, 1, keepdims=False)
    halves = from_behind(straight, 1).astype(jnp.float32) + from_behind(crossed, 1, 1).astype(
        jnp.float32
    )
    same_side = [[2 * z + x for z in range(window)] for x in range(2)]
    returned = lax.all_to_all(
        halves.astype(jnp.bfloat16), "expert", 0, 0, tiled=True, axis_index_groups=same_side
    ).reshape(window * capacity, half_width)
    ids_on = routes_on[:6].astype(jnp.int32)
    current = combine(residual, returned, ids_on, routes_on[6:])

    partial = experts(dispatch(current, route_ids[1, 0].T))
    returned = lax.all_to_all(
        partial.reshape(expert_count, capacity, half_width), "expert", 0, 0, tiled=True
    ).astype(jnp.float32)
    expert_out = jnp.sum(returned.reshape(window, 2, capacity, half_width), axis=1)
    current = combine(
        current,
        expert_out.reshape(window * capacity, half_width),
        route_ids[1, 0].T,
        route_weights[1, 0].T,
    )
    return current[None]


def solution(mesh):
    in_specs = (
        P("section", "expert", "tensor"),
        P("section", None),
        P("section", None, ("expert", "tensor")),
        P("section", None, ("expert", "tensor")),
        P("section", ("expert", "tensor"), None),
        P(None, "section", "expert", None),
        P(None, "section", "expert", None),
    )
    out_specs = P("section", "expert", "tensor")
    return jax.shard_map(local, mesh=mesh, in_specs=in_specs, out_specs=out_specs, check_vma=False)
```

time: 126 us -> 125 us (level)
  the two profiles are of different devices: /device:TPU:32 before, /device:TPU:16 now
where the time goes in v2:
time: 125 us; the launch traced here: 124 us
  blocking collectives  44 us (35%)
  starting transfers between devices  36.8 us (29%)
  waiting for transfers between devices  29.7 us (24%)
  local copies, waits for them, and re-layouts  5.95 us (5%)
  matrix products  5.79 us (5%)
  other arithmetic  1.31 us (1%)
    all_to_all x1, blocking collectives, local(): lax.all_to_all(partial.reshape(expert_count, capacity, half_width), 'expe...  18.5 us
    all_to_all x1, blocking collectives, dispatch(): lax.all_to_all(outgoing.reshape(expert_count, capacity, half_width), 'exp...  17.1 us
    ppermute x5, starting transfers between devices, from_behind(): return lax.ppermute(array, ('section', 'expert'), pairs)  16.8 us
    all_to_all x1, waiting for transfers between devices, dispatch(): lax.all_to_all(outgoing.reshape(expert_count, capacity, half_width), 'exp...  13.2 us
    all_to_all x1, starting transfers between devices, dispatch(): lax.all_to_all(outgoing.reshape(expert_count, capacity, half_width), 'exp...  12.9 us
    all_to_all x1, waiting for transfers between devices, local(): lax.all_to_all(halves.astype(jnp.bfloat16), 'expert', 0, 0, tiled=True, a...  9.2 us
    ppermute x5, waiting for transfers between devices, from_behind(): return lax.ppermute(array, ('section', 'expert'), pairs)  7.33 us
    all_gather x2, blocking collectives, experts(): lax.all_gather(arrived, 'tensor', axis=1, tiled=True).astype(jnp.float32)  4.53 us
  transfers between devices with their start and end apart: 8, of which 4 were waited for; matrix products, arithmetic and copies ran while one was open for 6% of the time, Pallas kernels for 0%

profile of v2, /device:TPU:16, one launch (start us, length us, event | category | flops | bytes accessed | tf_op | source)
XLA Modules:
  0.0 123.9 jit_solution(14301423249115048978)
XLA Ops:
  0.0 0.0 copy-start
  0.0 3.5 %collective-permute-start.2 = (bf16[128,1280]{1,0:T(8,128)(2,1)}, bf16[128,1280]{1,0:T(8,128)(2,1)S(1)}, u32[]{:S(2)}, u32[]{:S(2)}) collective-permute-start(bf16[128,1280]{1,0:T(8,128)(2,1)} %bitcast.92), channel_id=1, source_target_pairs={{0,32},{2,34},{4,36},{6,38},{8,40},{10,42},{12,44},{14,46},{16,48}... | collective-permute-start | bytes 983048 | tf_op jit(solution)/shard_map/ppermute | solution.py:16
  3.5 3.5 %collective-permute-start = (bf16[128,1280]{1,0:T(8,128)(2,1)}, bf16[128,1280]{1,0:T(8,128)(2,1)S(1)}, u32[]{:S(2)}, u32[]{:S(2)}) collective-permute-start(bf16[128,1280]{1,0:T(8,128)(2,1)} %bitcast.93), channel_id=1, source_target_pairs={{0,64},{2,66},{4,68},{6,70},{8,72},{10,74},{12,76},{14,78},{16,80}... | collective-permute-start | bytes 983048 | tf_op jit(solution)/shard_map/ppermute | solution.py:16
  7.0 2.4 %copy.14 = bf16[1,256,2560]{1,2,0:T(8,128)(2,1)} copy(bf16[1,256,2560]{2,1,0:T(8,128)(2,1)} %param.11) | data formatting | bytes 2621440 | tf_op args[4]
  9.5 3.8 %all-to-all-start.1 = ((bf16[256,2,1280]{0,2,1:T(8,128)(2,1)}), bf16[256,2,1280]{0,2,1:T(8,128)(2,1)S(1)}, u32[]{:S(2)}, u32[]{:S(2)}) async-start(bf16[256,2,1280]{0,2,1:T(8,128)(2,1)} %bitcast.84), calls=%async_computation.1 | async-start | bytes 2621440 | tf_op jit(solution)/shard_map/all_to_all | solution.py:60
  13.2 0.0 copy-done.3
  13.3 0.0 copy-done.4
  13.3 4.7 %collective-permute-start.1 = (f32[12,128]{1,0:T(8,128)S(1)}, f32[12,128]{1,0:T(8,128)S(1)}, u32[]{:S(2)}, u32[]{:S(2)}) collective-permute-start(f32[12,128]{1,0:T(8,128)S(1)} %pad_maximum_fusion), channel_id=1, source_target_pairs={{0,32},{2,34},{4,36},{6,38},{8,40},{10,42},{12,44},{14,46},{16,48}... | collective-permute-start | bytes 18440 | tf_op jit(solution)/shard_map/ppermute | solution.py:16
  18.0 0.1 fusion.31
  18.2 0.0 collective-permute-done.2
  18.2 1.0 fusion
  19.1 0.0 all-to-all-done.1
  19.2 12.9 %all-to-all-start = ((bf16[16,8,1280]{2,1,0:T(8,128)(2,1)}), bf16[16,8,1280]{2,1,0:T(8,128)(2,1)S(1)}, u32[]{:S(2)}, u32[]{:S(2)}) async-start(bf16[16,8,1280]{2,1,0:T(8,128)(2,1)} %fusion), calls=%async_computation | async-start | bytes 655360 | tf_op jit(solution)/shard_map/all_to_all | solution.py:68
  32.1 0.0 copy-done.1
  32.1 0.0 copy-start.2
  32.1 1.6 %copy.15 = bf16[2,256,1280]{2,1,0:T(8,128)(2,1)S(1)} copy(bf16[2,256,1280]{1,2,0:T(8,128)(2,1)} %bitcast.83) | data formatting | bytes 2621440 | tf_op jit(solution)/shard_map/all_to_all | solution.py:60
  33.8 0.1 fusion.30
  33.9 13.2 %all-to-all-done = bf16[16,8,1280]{2,1,0:T(8,128)(2,1)S(1)} async-done(((bf16[16,8,1280]{2,1,0:T(8,128)(2,1)}), bf16[16,8,1280]{2,1,0:T(8,128)(2,1)S(1)}, u32[]{:S(2)}, u32[]{:S(2)}) %all-to-all-start) | async-done | bytes 327712 | tf_op jit(solution)/shard_map/all_to_all | solution.py:68
  47.1 2.3 %all_gather.12 = bf16[128,2560]{1,0:T(8,128)(2,1)S(1)} all-gather(bf16[128,1280]{1,0:T(8,128)(2,1)S(1)} %bitcast.86), channel_id=1, replica_groups=mesh['section'=16,'expert'=16,'tensor'=2] {'tensor'}, dimensions={1}, use_global_device_ids=true | all-gather | bytes 983040 | tf_op jit(solution)/shard_map/all_gather | solution.py:74
  49.3 0.2 fusion.3
  49.6 0.0 copy-start.5
  49.6 0.4 fusion.15
  50.0 0.9 copy-done.5
  50.9 0.4 fusion.26
  51.3 1.9 %all_gather.13 = bf16[128,512]{1,0:T(8,128)(2,1)S(1)} all-gather(bf16[128,256]{1,0:T(8,128)(2,1)S(1)} %fusion.26), channel_id=1, replica_groups=mesh['section'=16,'expert'=16,'tensor'=2] {'tensor'}, dimensions={1}, use_global_device_ids=true | all-gather | bytes 196608 | tf_op jit(solution)/shard_map/all_gather | solution.py:80
  53.2 0.3 convolution_convert_fusion.2
  53.6 2.5 %collective-permute-start.3 = (bf16[8,8,1280]{2,1,0:T(8,128)(2,1)S(1)}, bf16[8,8,1280]{2,1,0:T(8,128)(2,1)S(1)}, u32[]{:S(2)}, u32[]{:S(2)}) collective-permute-start(bf16[8,8,1280]{2,1,0:T(8,128)(2,1)S(1)} %get-tuple-element.9), channel_id=1, source_target_pairs={{0,32},{2,34},{4,36},{6,38},{8,40},{10,42},{12,44},{14,46},{16,48}... | collective-permute-start | bytes 491528 | tf_op jit(solution)/shard_map/ppermute | solution.py:16
  56.1 2.6 %collective-permute-start.4 = (bf16[8,8,1280]{2,1,0:T(8,128)(2,1)S(1)}, bf16[8,8,1280]{2,1,0:T(8,128)(2,1)S(1)}, u32[]{:S(2)}, u32[]{:S(2)}) collective-permute-start(bf16[8,8,1280]{2,1,0:T(8,128)(2,1)S(1)} %get-tuple-element.10), channel_id=1, source_target_pairs={{0,34},{2,32},{4,38},{6,36},{8,42},{10,40},{12,46},{14,44},{16,50}... | collective-permute-start | bytes 491528 | tf_op jit(solution)/shard_map/ppermute | solution.py:16
  58.7 0.0 collective-permute-done.1
  58.8 4.7 %collective-permute-done.3 = bf16[8,8,1280]{2,1,0:T(8,128)(2,1)S(1)} collective-permute-done((bf16[8,8,1280]{2,1,0:T(8,128)(2,1)S(1)}, bf16[8,8,1280]{2,1,0:T(8,128)(2,1)S(1)}, u32[]{:S(2)}, u32[]{:S(2)}) %collective-permute-start.3) | collective-permute-done | bytes 163872 | tf_op jit(solution)/shard_map/ppermute | solution.py:16
  63.4 2.7 %collective-permute-done.4 = bf16[8,8,1280]{2,1,0:T(8,128)(2,1)S(1)} collective-permute-done((bf16[8,8,1280]{2,1,0:T(8,128)(2,1)S(1)}, bf16[8,8,1280]{2,1,0:T(8,128)(2,1)S(1)}, u32[]{:S(2)}, u32[]{:S(2)}) %collective-permute-start.4) | collective-permute-done | bytes 163872 | tf_op jit(solution)/shard_map/ppermute | solution.py:16
  66.1 0.7 add_convert_fusion.2
  66.8 3.4 %all-to-all-start.2 = ((bf16[8,8,1280]{2,1,0:T(8,128)(2,1)}), bf16[8,8,1280]{2,1,0:T(8,128)(2,1)S(1)}, u32[]{:S(2)}, u32[]{:S(2)}) async-start(bf16[8,8,1280]{2,1,0:T(8,128)(2,1)} %add_convert_fusion.2), calls=%async_computation.2 | async-start | bytes 327680 | tf_op jit(solution)/shard_map/all_to_all | solution.py:102
  70.2 0.1 fusion.32
  70.3 0.0 collective-permute-done
  70.3 9.2 %all-to-all-done.2 = bf16[8,8,1280]{2,1,0:T(8,128)(2,1)S(1)} async-done(((bf16[8,8,1280]{2,1,0:T(8,128)(2,1)}), bf16[8,8,1280]{2,1,0:T(8,128)(2,1)S(1)}, u32[]{:S(2)}, u32[]{:S(2)}) %all-to-all-start.2) | async-done | bytes 163872 | tf_op jit(solution)/shard_map/all_to_all | solution.py:102
  79.5 0.5 add_convert_fusion.1
  80.0 0.2 fusion.1
  80.3 17.1 %all_to_all.39 = bf16[16,8,1280]{2,1,0:T(8,128)(2,1)S(1)} all-to-all(bf16[16,8,1280]{2,1,0:T(8,128)(2,1)S(1)} %fusion.1), channel_id=1, replica_groups=mesh['section'=16,'expert'=16,'tensor'=2] {'expert'}, dimensions={0} | all-to-all | bytes 655360 | tf_op jit(solution)/shard_map/all_to_all | solution.py:68
  97.4 2.3 %all_gather.14 = bf16[128,2560]{1,0:T(8,128)(2,1)S(1)} all-gather(bf16[128,1280]{1,0:T(8,128)(2,1)S(1)} %bitcast.87), channel_id=1, replica_groups=mesh['section'=16,'expert'=16,'tensor'=2] {'tensor'}, dimensions={1}, use_global_device_ids=true | all-gather | bytes 983040 | tf_op jit(solution)/shard_map/all_gather | solution.py:74
  99.7 0.2 fusion.6
  99.9 0.4 fusion.13
  100.3 0.9 copy-done.6
  101.2 0.4 fusion.23
  101.6 1.9 %all_gather.15 = bf16[128,512]{1,0:T(8,128)(2,1)S(1)} all-gather(bf16[128,256]{1,0:T(8,128)(2,1)S(1)} %fusion.23), channel_id=1, replica_groups=mesh['section'=16,'expert'=16,'tensor'=2] {'tensor'}, dimensions={1}, use_global_device_ids=true | all-gather | bytes 196608 | tf_op jit(solution)/shard_map/all_gather | solution.py:80
  103.5 0.3 fusion.2
  103.9 18.5 %all_to_all.40 = bf16[16,8,1280]{2,1,0:T(8,128)(2,1)S(1)} all-to-all(bf16[16,8,1280]{2,1,0:T(8,128)(2,1)S(1)} %fusion.2), channel_id=1, replica_groups=mesh['section'=16,'expert'=16,'tensor'=2] {'expert'}, dimensions={0} | all-to-all | bytes 655360 | tf_op jit(solution)/shard_map/all_to_all | solution.py:109
  122.5 1.5 %fusion.29 = bf16[1,128,1280]{2,1,0:T(8,128)(2,1)} fusion(bf16[128,1280]{1,0:T(8,128)(2,1)S(1)} %add_convert_fusion.1, f32[8,8,1280]{2,1,0:T(8,128)S(1)} %convert_reduce_fusion, f32[8,128]{1,0:T(8,128)S(1)} %get-tuple-element.5, f32[8,128]{1,0:T(8,128)S(1)} %get-tuple-element.6, f32[8,128]{1,0:T(8,128)S(1)} %fusion.30), kind=kOutput, calls=%fused_computation.34 | convolution fusion | flops 126345216 | bytes 995328 | tf_op jit(solution)/shard_map/dot_general | solution.py:84
  (25 shorter events, 0.2 us)
Async XLA Ops:
  0.0 49.6 %copy-start = (bf16[1,2560,256]{2,1,0:T(8,128)(2,1)S(1)}, bf16[1,2560,256]{2,1,0:T(8,128)(2,1)}, u32[]{:S(2)}) copy-start(bf16[1,2560,256]{2,1,0:T(8,128)(2,1)} %param.9) | copy-start | bytes 3932164
  0.0 18.2 %collective-permute-start.2 = (bf16[128,1280]{1,0:T(8,128)(2,1)}, bf16[128,1280]{1,0:T(8,128)(2,1)S(1)}, u32[]{:S(2)}, u32[]{:S(2)}) collective-permute-start(bf16[128,1280]{1,0:T(8,128)(2,1)} %bitcast.92), channel_id=1, source_target_pairs={{0,32},{2,34},{4,36},{6,38},{8,40},{10,42},{12,44},{14,46},{16,48}... | collective-permute-start | bytes 983048 | tf_op jit(solution)/shard_map/ppermute | solution.py:16
  3.5 66.8 %collective-permute-start = (bf16[128,1280]{1,0:T(8,128)(2,1)}, bf16[128,1280]{1,0:T(8,128)(2,1)S(1)}, u32[]{:S(2)}, u32[]{:S(2)}) collective-permute-start(bf16[128,1280]{1,0:T(8,128)(2,1)} %bitcast.93), channel_id=1, source_target_pairs={{0,64},{2,66},{4,68},{6,70},{8,72},{10,74},{12,76},{14,78},{16,80}... | collective-permute-start | bytes 983048 | tf_op jit(solution)/shard_map/ppermute | solution.py:16
  9.5 3.8 %copy-start.3 = (s32[2,1,128,6]{2,1,3,0:T(1,128)S(1)}, s32[2,1,128,6]{2,1,3,0:T(1,128)}, u32[]{:S(2)}) copy-start(s32[2,1,128,6]{2,1,3,0:T(1,128)} %param.12) | copy-start | bytes 18436
  9.5 3.8 %copy-start.4 = (f32[2,1,128,6]{2,1,3,0:T(1,128)S(1)}, f32[2,1,128,6]{2,1,3,0:T(1,128)}, u32[]{:S(2)}) copy-start(f32[2,1,128,6]{2,1,3,0:T(1,128)} %param.13) | copy-start | bytes 18436
  9.5 9.7 %all-to-all-start.1 = ((bf16[256,2,1280]{0,2,1:T(8,128)(2,1)}), bf16[256,2,1280]{0,2,1:T(8,128)(2,1)S(1)}, u32[]{:S(2)}, u32[]{:S(2)}) async-start(bf16[256,2,1280]{0,2,1:T(8,128)(2,1)} %bitcast.84), calls=%async_computation.1 | async-start | bytes 2621440 | tf_op jit(solution)/shard_map/all_to_all | solution.py:60
  13.3 45.4 %collective-permute-start.1 = (f32[12,128]{1,0:T(8,128)S(1)}, f32[12,128]{1,0:T(8,128)S(1)}, u32[]{:S(2)}, u32[]{:S(2)}) collective-permute-start(f32[12,128]{1,0:T(8,128)S(1)} %pad_maximum_fusion), channel_id=1, source_target_pairs={{0,32},{2,34},{4,36},{6,38},{8,40},{10,42},{12,44},{14,46},{16,48}... | collective-permute-start | bytes 18440 | tf_op jit(solution)/shard_map/ppermute | solution.py:16
  19.1 12.9 %copy-start.1 = (bf16[256,2,1280]{0,2,1:T(8,128)(2,1)}, bf16[256,2,1280]{0,2,1:T(8,128)(2,1)S(1)}, u32[]{:S(2)}) copy-start(bf16[256,2,1280]{0,2,1:T(8,128)(2,1)S(1)} %all-to-all-done.1) | copy-start | bytes 3932164
  19.2 27.9 %all-to-all-start = ((bf16[16,8,1280]{2,1,0:T(8,128)(2,1)}), bf16[16,8,1280]{2,1,0:T(8,128)(2,1)S(1)}, u32[]{:S(2)}, u32[]{:S(2)}) async-start(bf16[16,8,1280]{2,1,0:T(8,128)(2,1)} %fusion), calls=%async_computation | async-start | bytes 655360 | tf_op jit(solution)/shard_map/all_to_all | solution.py:68
  32.1 1.6 %copy-start.2 = (bf16[1,2560]{1,0:T(2,128)(2,1)S(1)}, bf16[1,2560]{1,0:T(2,128)(2,1)}, u32[]{:S(2)}) copy-start(bf16[1,2560]{1,0:T(2,128)(2,1)} %param.8) | copy-start | bytes 15364
  49.6 1.3 %copy-start.5 = (bf16[1,2560,256]{2,1,0:T(8,128)(2,1)S(1)}, bf16[1,2560,256]{2,1,0:T(8,128)(2,1)}, u32[]{:S(2)}) copy-start(bf16[1,2560,256]{2,1,0:T(8,128)(2,1)} %param.10) | copy-start | bytes 3932164
  53.6 9.8 %collective-permute-start.3 = (bf16[8,8,1280]{2,1,0:T(8,128)(2,1)S(1)}, bf16[8,8,1280]{2,1,0:T(8,128)(2,1)S(1)}, u32[]{:S(2)}, u32[]{:S(2)}) collective-permute-start(bf16[8,8,1280]{2,1,0:T(8,128)(2,1)S(1)} %get-tuple-element.9), channel_id=1, source_target_pairs={{0,32},{2,34},{4,36},{6,38},{8,40},{10,42},{12,44},{14,46},{16,48}... | collective-permute-start | bytes 491528 | tf_op jit(solution)/shard_map/ppermute | solution.py:16
  56.1 10.0 %collective-permute-start.4 = (bf16[8,8,1280]{2,1,0:T(8,128)(2,1)S(1)}, bf16[8,8,1280]{2,1,0:T(8,128)(2,1)S(1)}, u32[]{:S(2)}, u32[]{:S(2)}) collective-permute-start(bf16[8,8,1280]{2,1,0:T(8,128)(2,1)S(1)} %get-tuple-element.10), channel_id=1, source_target_pairs={{0,34},{2,32},{4,38},{6,36},{8,42},{10,40},{12,46},{14,44},{16,50}... | collective-permute-start | bytes 491528 | tf_op jit(solution)/shard_map/ppermute | solution.py:16
  66.8 12.7 %all-to-all-start.2 = ((bf16[8,8,1280]{2,1,0:T(8,128)(2,1)}), bf16[8,8,1280]{2,1,0:T(8,128)(2,1)S(1)}, u32[]{:S(2)}, u32[]{:S(2)}) async-start(bf16[8,8,1280]{2,1,0:T(8,128)(2,1)} %add_convert_fusion.2), calls=%async_computation.2 | async-start | bytes 327680 | tf_op jit(solution)/shard_map/all_to_all | solution.py:102
  99.9 1.3 %copy-start.6 = (bf16[1,2560,256]{2,1,0:T(8,128)(2,1)S(1)}, bf16[1,2560,256]{2,1,0:T(8,128)(2,1)}, u32[]{:S(2)}) copy-start(bf16[1,2560,256]{2,1,0:T(8,128)(2,1)} %param.10) | copy-start | bytes 3932164

commit v3 on v2

v3 whole, which is shorter than its diff:
```python
import jax
import jax.numpy as jnp
from jax import lax
from jax.sharding import PartitionSpec as P

NORM_EPS = 1e-06


def send(array, by=0, flips=(0, 0)):
    sections, experts, cores = (lax.axis_size(name) for name in ("section", "expert", "tensor"))
    pairs = []
    for s in range(sections):
        for e in range(experts):
            for c in range(cores):
                there = ((s + by) % sections * experts + (e ^ flips[c])) * cores + c
                here = (s * experts + e) * cores + c
                if here != there:
                    pairs.append((here, there))
    return lax.ppermute(array, ("section", "expert", "tensor"), pairs)


def slots_of(ids_major, window, capacity):
    tok_count = ids_major.shape[1]
    experts_col = jnp.arange(window, dtype=jnp.int32)[None, :, None]
    member = ids_major[:, None, :] == experts_col
    named = jnp.sum(member.astype(jnp.float32), axis=0)
    row_pos = jnp.arange(tok_count, dtype=jnp.int32)
    strictly = (row_pos[:, None] < row_pos[None, :]).astype(jnp.bfloat16)
    earlier = jnp.dot(named.astype(jnp.bfloat16), strictly, preferred_element_type=jnp.float32)
    slot_col = jnp.arange(capacity, dtype=jnp.float32)[None, :, None]
    filled = named[:, None, :] * (earlier[:, None, :] == slot_col).astype(jnp.float32)
    return filled, member


def dispatch_rows(ids_major, window, capacity):
    filled, _ = slots_of(ids_major, window, capacity)
    return filled.reshape(window * capacity, -1).astype(jnp.bfloat16)


def combine_rows(ids_major, weights_major, window, capacity):
    filled, member = slots_of(ids_major, window, capacity)
    gate_of = jnp.sum(jnp.where(member, weights_major[:, None, :], 0.0), axis=0)
    return (filled * gate_of[:, None, :]).reshape(window * capacity, -1)


def local(activations, norm_gain, w_gate, w_up, w_down, route_ids, route_weights):
    start = activations[0]
    tok_rows, half_width = start.shape
    expert_count = lax.axis_size("expert")
    window = expert_count // 2
    capacity = tok_rows // 16
    slots = expert_count * capacity
    core = lax.axis_index("tensor")
    side = lax.axis_index("expert") % 2
    gain_row = norm_gain[0].astype(jnp.float32)

    def slot_rows(tokens, twice):
        outgoing = jnp.dot(twice, tokens, preferred_element_type=jnp.float32)
        return outgoing.astype(jnp.bfloat16).reshape(expert_count, capacity, half_width)

    def doubled(table):
        table = jnp.repeat(table.reshape(window, capacity, tok_rows), 2, axis=0)
        return table.reshape(slots, tok_rows)

    def experts(arrived, down_own, down_got):
        rows = lax.all_gather(arrived.reshape(slots, half_width), "tensor", axis=1, tiled=True)
        rows = rows.astype(jnp.float32)
        rms_scale = jnp.sqrt(jnp.mean(rows * rows, axis=1, keepdims=True) + NORM_EPS)
        normed = (rows / rms_scale * gain_row).astype(jnp.bfloat16)
        gate_act = jnp.dot(normed, w_gate[0], preferred_element_type=jnp.float32)
        up_act = jnp.dot(normed, w_up[0], preferred_element_type=jnp.float32)
        hidden = (jax.nn.silu(gate_act) * up_act).astype(jnp.bfloat16)
        hidden = lax.all_gather(hidden, "tensor", axis=0, tiled=False)
        total = jnp.dot(
            lax.dynamic_index_in_dim(hidden, core, 0, keepdims=False),
            down_own,
            preferred_element_type=jnp.float32,
        ) + jnp.dot(
            lax.dynamic_index_in_dim(hidden, 1 - core, 0, keepdims=False),
            down_got,
            preferred_element_type=jnp.float32,
        )
        return total.astype(jnp.bfloat16)

    def combine(tokens, rows, table):
        high = table.astype(jnp.bfloat16)
        low = (table - high.astype(jnp.float32)).astype(jnp.bfloat16)
        dims = (((0,), (0,)), ((), ()))
        moe_sum = lax.dot_general(high, rows, dims, preferred_element_type=jnp.float32)
        moe_sum += lax.dot_general(low, rows, dims, preferred_element_type=jnp.float32)
        return (tokens.astype(jnp.float32) + moe_sum).astype(jnp.bfloat16)

    ids = route_ids[0, 0].T
    outgoing = slot_rows(send(start, 1), doubled(dispatch_rows(ids, window, capacity)))
    routes = jnp.concatenate([ids.astype(jnp.float32), route_weights[0, 0].T], axis=0)
    down_own = lax.dynamic_slice_in_dim(w_down[0], core * half_width, half_width, 1)
    down_sent = lax.dynamic_slice_in_dim(w_down[0], (1 - core) * half_width, half_width, 1)
    outgoing, start, routes, down_sent, down_own = lax.optimization_barrier(
        (outgoing, start, routes, down_sent, down_own)
    )
    arrived = lax.all_to_all(outgoing, "expert", 0, 0, tiled=True)
    residual = send(start, 2)
    routes_on = send(routes, 1)
    down_got = lax.ppermute(down_sent, "tensor", [(0, 1), (1, 0)])
    partial = experts(arrived, down_own, down_got)
    by_side = partial.reshape(window, 2, capacity, half_width)
    straight = lax.dynamic_index_in_dim(by_side, side, 1, keepdims=False)
    crossed = lax.dynamic_index_in_dim(by_side, 1 - side, 1, keepdims=False)
    straight, crossed, residual, routes_on, ids, gates = lax.optimization_barrier(
        (straight, crossed, residual, routes_on, route_ids[1, 0], route_weights[1, 0])
    )
    halves = send(straight, 1).astype(jnp.float32) + send(crossed, 1, (1, 1)).astype(jnp.float32)
    dispatch_1 = doubled(dispatch_rows(ids.T, window, capacity))
    combine_0 = combine_rows(routes_on[:6].astype(jnp.int32), routes_on[6:], window, capacity)
    combine_1 = doubled(combine_rows(ids.T, gates.T, window, capacity))
    halves, combine_0, dispatch_1, combine_1 = lax.optimization_barrier(
        (halves.astype(jnp.bfloat16), combine_0, dispatch_1, combine_1)
    )
    same_side = [[2 * z + x for z in range(window)] for x in range(2)]
    returned = lax.all_to_all(
        halves, "expert", 0, 0, tiled=True, axis_index_groups=same_side
    ).reshape(window * capacity, half_width)
    current = combine(residual, returned, combine_0)

    arrived = lax.all_to_all(slot_rows(current, dispatch_1), "expert", 0, 0, tiled=True)
    partial = experts(arrived, down_own, down_got)
    returned = lax.all_to_all(
        partial.reshape(expert_count, capacity, half_width), "expert", 0, 0, tiled=True
    ).reshape(slots, half_width)
    return combine(current, returned, combine_1)[None]


def solution(mesh):
    in_specs = (
        P("section", "expert", "tensor"),
        P("section", None),
        P("section", None, ("expert", "tensor")),
        P("section", None, ("expert", "tensor")),
        P("section", ("expert", "tensor"), None),
        P(None, "section", "expert", None),
        P(None, "section", "expert", None),
    )
    out_specs = P("section", "expert", "tensor")
    return jax.shard_map(local, mesh=mesh, in_specs=in_specs, out_specs=out_specs, check_vma=False)
```

time: 125 us -> 118 us (0.944)
  the two profiles are of different devices: /device:TPU:16 before, /device:TPU:32 now
where the time goes in v3:
time: 118 us
  blocking collectives  56.1 us (48%)
  starting transfers between devices  26 us (22%)
  waiting for transfers between devices  24 us (20%)
  matrix products  6.05 us (5%)
  local copies, waits for them, and re-layouts  4.69 us (4%)
    all_to_all x1, blocking collectives, local(): lax.all_to_all(partial.reshape(expert_count, capacity, half_width), 'expe...  18.5 us
    all_to_all x1, blocking collectives, local(): lax.all_to_all(slot_rows(current, dispatch_1), 'expert', 0, 0, tiled=True)  16.8 us
    ppermute x5, waiting for transfers between devices, send(): return lax.ppermute(array, ('section', 'expert', 'tensor'), pairs)  15.9 us
    all_to_all x1, starting transfers between devices, local(): arrived = lax.all_to_all(outgoing, 'expert', 0, 0, tiled=True)  12.9 us
    all_to_all x1, blocking collectives, local(): lax.all_to_all(halves, 'expert', 0, 0, tiled=True, axis_index_groups=same...  12.5 us
    ppermute x5, starting transfers between devices, send(): return lax.ppermute(array, ('section', 'expert', 'tensor'), pairs)  11.2 us
    all_to_all x1, waiting for transfers between devices, local(): arrived = lax.all_to_all(outgoing, 'expert', 0, 0, tiled=True)  8.1 us
    all_gather x2, blocking collectives, experts(): lax.all_gather(arrived.reshape(slots, half_width), 'tensor', axis=1, tile...  4.53 us
  transfers between devices with their start and end apart: 7, of which 4 were waited for; matrix products, arithmetic and copies ran while one was open for 5% of the time, Pallas kernels for 0%

profile of v3, /device:TPU:32, one launch (start us, length us, event | category | flops | bytes accessed | tf_op | source)
XLA Modules:
  0.0 117.8 jit_solution(3218982883436426554)
XLA Ops:
  0.0 0.0 copy-start
  0.0 3.5 %collective-permute-start = (bf16[128,1280]{1,0:T(8,128)(2,1)}, bf16[128,1280]{1,0:T(8,128)(2,1)S(1)}, u32[]{:S(2)}, u32[]{:S(2)}) collective-permute-start(bf16[128,1280]{1,0:T(8,128)(2,1)} %bitcast.119), channel_id=1, source_target_pairs={{0,32},{1,33},{2,34},{3,35},{4,36},{5,37},{6,38},{7,39},{8,40},{9,... | collective-permute-start | bytes 983048 | tf_op jit(solution)/shard_map/ppermute | solution.py:19
  3.5 0.7 fusion.73
  4.3 0.1 fusion.52
  4.4 0.7 fusion.72
  5.1 2.2 %dynamic-slice_bitcast_fusion = (bf16[256,1280]{1,0:T(8,128)(2,1)S(1)}, bf16[256,1280]{1,0:T(8,128)(2,1)}) fusion(bf16[1,256,2560]{2,1,0:T(8,128)(2,1)} %param.11, s32[]{:T(128)S(6)} %select_n.37, s32[]{:T(128)S(6)} %select_n.36), kind=kLoop, calls=%fused_computation.37 | loop fusion | bytes 2621448 | tf_op jit(solution)/shard_map/dynamic_slice | solution.py:96
  7.3 6.4 %collective-permute-done = bf16[128,1280]{1,0:T(8,128)(2,1)S(1)} collective-permute-done((bf16[128,1280]{1,0:T(8,128)(2,1)}, bf16[128,1280]{1,0:T(8,128)(2,1)S(1)}, u32[]{:S(2)}, u32[]{:S(2)}) %collective-permute-start) | collective-permute-done | bytes 327712 | tf_op jit(solution)/shard_map/ppermute | solution.py:19
  13.8 1.0 fusion.4
  14.8 12.9 %all-to-all-start = ((bf16[16,8,1280]{2,1,0:T(8,128)(2,1)}), bf16[16,8,1280]{2,1,0:T(8,128)(2,1)S(1)}, u32[]{:S(2)}, u32[]{:S(2)}) async-start(bf16[16,8,1280]{2,1,0:T(8,128)(2,1)} %fusion.4), calls=%async_computation | async-start | bytes 655360 | tf_op jit(solution)/shard_map/all_to_all | solution.py:101
  27.7 0.1 eq.117
  27.8 1.9 %collective-permute-start.1 = (bf16[256,1280]{1,0:T(8,128)(2,1)}, bf16[256,1280]{1,0:T(8,128)(2,1)S(1)}, u32[]{:S(2)}, u32[]{:S(2)}) collective-permute-start(bf16[256,1280]{1,0:T(8,128)(2,1)} %get-tuple-element.22), channel_id=1, source_target_pairs={{0,1},{1,0},{2,3},{3,2},{4,5},{5,4},{6,7},{7,6},{8,9},{9,8},{10,11... | collective-permute-start | bytes 1966088 | tf_op jit(solution)/shard_map/ppermute | solution.py:104
  29.7 1.9 %collective-permute-start.2 = (bf16[128,1280]{1,0:T(8,128)(2,1)}, bf16[128,1280]{1,0:T(8,128)(2,1)S(1)}, u32[]{:S(2)}, u32[]{:S(2)}) collective-permute-start(bf16[128,1280]{1,0:T(8,128)(2,1)} %bitcast.120), channel_id=1, source_target_pairs={{0,64},{1,65},{2,66},{3,67},{4,68},{5,69},{6,70},{7,71},{8,72},{9,... | collective-permute-start | bytes 983048 | tf_op jit(solution)/shard_map/ppermute | solution.py:19
  31.7 1.9 %collective-permute-start.3 = (f32[12,128]{1,0:T(8,128)S(1)}, f32[12,128]{1,0:T(8,128)S(1)}, u32[]{:S(2)}, u32[]{:S(2)}) collective-permute-start(f32[12,128]{1,0:T(8,128)S(1)} %pad_maximum_fusion), channel_id=1, source_target_pairs={{0,32},{1,33},{2,34},{3,35},{4,36},{5,37},{6,38},{7,39},{8,40},{9,... | collective-permute-start | bytes 18440 | tf_op jit(solution)/shard_map/ppermute | solution.py:19
  33.6 8.1 %all-to-all-done = bf16[16,8,1280]{2,1,0:T(8,128)(2,1)S(1)} async-done(((bf16[16,8,1280]{2,1,0:T(8,128)(2,1)}), bf16[16,8,1280]{2,1,0:T(8,128)(2,1)S(1)}, u32[]{:S(2)}, u32[]{:S(2)}) %all-to-all-start) | async-done | bytes 327712 | tf_op jit(solution)/shard_map/all_to_all | solution.py:101
  41.7 2.3 %all_gather.18 = bf16[128,2560]{1,0:T(8,128)(2,1)S(1)} all-gather(bf16[128,1280]{1,0:T(8,128)(2,1)S(1)} %bitcast.105), channel_id=1, replica_groups=mesh['section'=16,'expert'=16,'tensor'=2] {'tensor'}, dimensions={1}, use_global_device_ids=true | all-gather | bytes 983040 | tf_op jit(solution)/shard_map/all_gather | solution.py:66
  44.0 0.2 fusion.8
  44.2 0.0 copy-start.2
  44.2 0.4 fusion.20
  44.6 0.9 copy-done.2
  45.5 0.4 fusion.31
  45.9 1.9 %all-gather = bf16[256,256]{1,0:T(8,128)(2,1)S(1)} all-gather(bf16[128,256]{1,0:T(8,128)(2,1)S(1)} %fusion.31), channel_id=2, replica_groups=mesh['section'=16,'expert'=16,'tensor'=2] {'tensor'}, dimensions={0}, use_global_device_ids=true | all-gather | bytes 196608 | tf_op jit(solution)/shard_map/all_gather | solution.py:73
  47.8 0.3 fusion.44
  48.1 0.0 collective-permute-done.1
  48.1 0.3 fusion.1
  48.4 0.0 collective-permute-done.3
  48.4 0.0 collective-permute-done.2
  48.4 0.1 fusion.50
  48.6 0.1 fusion.51
  48.7 1.9 %collective-permute-start.4 = (bf16[8,8,1280]{2,1,0:T(8,128)(2,1)S(1)}, bf16[8,8,1280]{2,1,0:T(8,128)(2,1)S(1)}, u32[]{:S(2)}, u32[]{:S(2)}) collective-permute-start(bf16[8,8,1280]{2,1,0:T(8,128)(2,1)S(1)} %get-tuple-element.26), channel_id=1, source_target_pairs={{0,32},{1,33},{2,34},{3,35},{4,36},{5,37},{6,38},{7,39},{8,40},{9,... | collective-permute-start | bytes 491528 | tf_op jit(solution)/shard_map/ppermute | solution.py:19
  50.7 1.9 %collective-permute-start.5 = (bf16[8,8,1280]{2,1,0:T(8,128)(2,1)S(1)}, bf16[8,8,1280]{2,1,0:T(8,128)(2,1)S(1)}, u32[]{:S(2)}, u32[]{:S(2)}) collective-permute-start(bf16[8,8,1280]{2,1,0:T(8,128)(2,1)S(1)} %get-tuple-element.27), channel_id=1, source_target_pairs={{0,34},{1,35},{2,32},{3,33},{4,38},{5,39},{6,36},{7,37},{8,42},{9,... | collective-permute-start | bytes 491528 | tf_op jit(solution)/shard_map/ppermute | solution.py:19
  52.6 0.1 bitcast_multiply_fusion
  52.7 7.1 %collective-permute-done.4 = bf16[8,8,1280]{2,1,0:T(8,128)(2,1)S(1)} collective-permute-done((bf16[8,8,1280]{2,1,0:T(8,128)(2,1)S(1)}, bf16[8,8,1280]{2,1,0:T(8,128)(2,1)S(1)}, u32[]{:S(2)}, u32[]{:S(2)}) %collective-permute-start.4) | collective-permute-done | bytes 163872 | tf_op jit(solution)/shard_map/ppermute | solution.py:19
  59.8 2.4 %collective-permute-done.5 = bf16[8,8,1280]{2,1,0:T(8,128)(2,1)S(1)} collective-permute-done((bf16[8,8,1280]{2,1,0:T(8,128)(2,1)S(1)}, bf16[8,8,1280]{2,1,0:T(8,128)(2,1)S(1)}, u32[]{:S(2)}, u32[]{:S(2)}) %collective-permute-start.5) | collective-permute-done | bytes 163872 | tf_op jit(solution)/shard_map/ppermute | solution.py:19
  62.2 12.5 %all_to_all.20 = bf16[8,8,1280]{2,1,0:T(8,128)(2,1)S(1)} all-to-all(bf16[8,8,1280]{2,1,0:T(8,128)(2,1)S(1)} %add_convert_fusion.1), channel_id=1, replica_groups={{0,4,8,12,16,20,24,28},{2,6,10,14,18,22,26,30},{1,5,9,13,17,21,25,29},{..., dimensions={0} | all-to-all | bytes 327680 | tf_op jit(solution)/shard_map/all_to_all | solution.py:120
  74.7 0.3 fusion.38
  75.0 0.3 add_convert_fusion
  75.3 0.2 fusion.5
  75.5 16.8 %all_to_all.21 = bf16[16,8,1280]{2,1,0:T(8,128)(2,1)S(1)} all-to-all(bf16[16,8,1280]{2,1,0:T(8,128)(2,1)S(1)} %fusion.5), channel_id=1, replica_groups=mesh['section'=16,'expert'=16,'tensor'=2] {'expert'}, dimensions={0} | all-to-all | bytes 655360 | tf_op jit(solution)/shard_map/all_to_all | solution.py:125
  92.3 2.3 %all_gather.21 = bf16[128,2560]{1,0:T(8,128)(2,1)S(1)} all-gather(bf16[128,1280]{1,0:T(8,128)(2,1)S(1)} %bitcast.107), channel_id=1, replica_groups=mesh['section'=16,'expert'=16,'tensor'=2] {'tensor'}, dimensions={1}, use_global_device_ids=true | all-gather | bytes 983040 | tf_op jit(solution)/shard_map/all_gather | solution.py:66
  94.5 0.2 fusion.11
  94.8 0.4 fusion.18
  95.2 0.4 fusion.28
  95.6 1.9 %all-gather.1 = bf16[256,256]{1,0:T(8,128)(2,1)S(1)} all-gather(bf16[128,256]{1,0:T(8,128)(2,1)S(1)} %fusion.28), channel_id=3, replica_groups=mesh['section'=16,'expert'=16,'tensor'=2] {'tensor'}, dimensions={0}, use_global_device_ids=true | all-gather | bytes 196608 | tf_op jit(solution)/shard_map/all_gather | solution.py:73
  97.5 0.3 fusion.41
  97.7 0.3 fusion.7
  98.0 18.5 %all_to_all.22 = bf16[16,8,1280]{2,1,0:T(8,128)(2,1)S(1)} all-to-all(bf16[16,8,1280]{2,1,0:T(8,128)(2,1)S(1)} %fusion.7), channel_id=1, replica_groups=mesh['section'=16,'expert'=16,'tensor'=2] {'expert'}, dimensions={0} | all-to-all | bytes 655360 | tf_op jit(solution)/shard_map/all_to_all | solution.py:127
  116.5 0.3 fusion.35
  116.8 1.0 fusion.6
  (24 shorter events, 0.3 us)
Async XLA Ops:
  0.0 44.2 %copy-start = (bf16[1,2560,256]{2,1,0:T(8,128)(2,1)S(1)}, bf16[1,2560,256]{2,1,0:T(8,128)(2,1)}, u32[]{:S(2)}) copy-start(bf16[1,2560,256]{2,1,0:T(8,128)(2,1)} %param.9) | copy-start | bytes 3932164
  0.0 13.8 %collective-permute-start = (bf16[128,1280]{1,0:T(8,128)(2,1)}, bf16[128,1280]{1,0:T(8,128)(2,1)S(1)}, u32[]{:S(2)}, u32[]{:S(2)}) collective-permute-start(bf16[128,1280]{1,0:T(8,128)(2,1)} %bitcast.119), channel_id=1, source_target_pairs={{0,32},{1,33},{2,34},{3,35},{4,36},{5,37},{6,38},{7,39},{8,40},{9,... | collective-permute-start | bytes 983048 | tf_op jit(solution)/shard_map/ppermute | solution.py:19
  7.3 20.4 %copy-start.1 = (bf16[1,2560]{1,0:T(2,128)(2,1)S(1)}, bf16[1,2560]{1,0:T(2,128)(2,1)}, u32[]{:S(2)}) copy-start(bf16[1,2560]{1,0:T(2,128)(2,1)} %param.8) | copy-start | bytes 15364
  14.8 26.9 %all-to-all-start = ((bf16[16,8,1280]{2,1,0:T(8,128)(2,1)}), bf16[16,8,1280]{2,1,0:T(8,128)(2,1)S(1)}, u32[]{:S(2)}, u32[]{:S(2)}) async-start(bf16[16,8,1280]{2,1,0:T(8,128)(2,1)} %fusion.4), calls=%async_computation | async-start | bytes 655360 | tf_op jit(solution)/shard_map/all_to_all | solution.py:101
  27.8 20.3 %collective-permute-start.1 = (bf16[256,1280]{1,0:T(8,128)(2,1)}, bf16[256,1280]{1,0:T(8,128)(2,1)S(1)}, u32[]{:S(2)}, u32[]{:S(2)}) collective-permute-start(bf16[256,1280]{1,0:T(8,128)(2,1)} %get-tuple-element.22), channel_id=1, source_target_pairs={{0,1},{1,0},{2,3},{3,2},{4,5},{5,4},{6,7},{7,6},{8,9},{9,8},{10,11... | collective-permute-start | bytes 1966088 | tf_op jit(solution)/shard_map/ppermute | solution.py:104
  29.7 18.7 %collective-permute-start.2 = (bf16[128,1280]{1,0:T(8,128)(2,1)}, bf16[128,1280]{1,0:T(8,128)(2,1)S(1)}, u32[]{:S(2)}, u32[]{:S(2)}) collective-permute-start(bf16[128,1280]{1,0:T(8,128)(2,1)} %bitcast.120), channel_id=1, source_target_pairs={{0,64},{1,65},{2,66},{3,67},{4,68},{5,69},{6,70},{7,71},{8,72},{9,... | collective-permute-start | bytes 983048 | tf_op jit(solution)/shard_map/ppermute | solution.py:19
  31.7 16.7 %collective-permute-start.3 = (f32[12,128]{1,0:T(8,128)S(1)}, f32[12,128]{1,0:T(8,128)S(1)}, u32[]{:S(2)}, u32[]{:S(2)}) collective-permute-start(f32[12,128]{1,0:T(8,128)S(1)} %pad_maximum_fusion), channel_id=1, source_target_pairs={{0,32},{1,33},{2,34},{3,35},{4,36},{5,37},{6,38},{7,39},{8,40},{9,... | collective-permute-start | bytes 18440 | tf_op jit(solution)/shard_map/ppermute | solution.py:19
  44.2 1.3 %copy-start.2 = (bf16[1,2560,256]{2,1,0:T(8,128)(2,1)S(1)}, bf16[1,2560,256]{2,1,0:T(8,128)(2,1)}, u32[]{:S(2)}) copy-start(bf16[1,2560,256]{2,1,0:T(8,128)(2,1)} %param.10) | copy-start | bytes 3932164
  48.7 11.0 %collective-permute-start.4 = (bf16[8,8,1280]{2,1,0:T(8,128)(2,1)S(1)}, bf16[8,8,1280]{2,1,0:T(8,128)(2,1)S(1)}, u32[]{:S(2)}, u32[]{:S(2)}) collective-permute-start(bf16[8,8,1280]{2,1,0:T(8,128)(2,1)S(1)} %get-tuple-element.26), channel_id=1, source_target_pairs={{0,32},{1,33},{2,34},{3,35},{4,36},{5,37},{6,38},{7,39},{8,40},{9,... | collective-permute-start | bytes 491528 | tf_op jit(solution)/shard_map/ppermute | solution.py:19
  50.7 11.5 %collective-permute-start.5 = (bf16[8,8,1280]{2,1,0:T(8,128)(2,1)S(1)}, bf16[8,8,1280]{2,1,0:T(8,128)(2,1)S(1)}, u32[]{:S(2)}, u32[]{:S(2)}) collective-permute-start(bf16[8,8,1280]{2,1,0:T(8,128)(2,1)S(1)} %get-tuple-element.27), channel_id=1, source_target_pairs={{0,34},{1,35},{2,32},{3,33},{4,38},{5,39},{6,36},{7,37},{8,42},{9,... | collective-permute-start | bytes 491528 | tf_op jit(solution)/shard_map/ppermute | solution.py:19

commit v4 on v3

--- a/solution.py
+++ b/solution.py
@@ -19,9 +19,13 @@
     return lax.ppermute(array, ("section", "expert", "tensor"), pairs)
 
 
+def round_trip(count):
+    return list(range(0, count, 2)) + list(range(count - 1, 0, -2))
+
+
 def slots_of(ids_major, window, capacity):
     tok_count = ids_major.shape[1]
-    experts_col = jnp.arange(window, dtype=jnp.int32)[None, :, None]
+    experts_col = jnp.array(round_trip(window), dtype=jnp.int32)[None, :, None]
     member = ids_major[:, None, :] == experts_col
     named = jnp.sum(member.astype(jnp.float32), axis=0)
     row_pos = jnp.arange(tok_count, dtype=jnp.int32)
@@ -40,7 +44,7 @@
 def combine_rows(ids_major, weights_major, window, capacity):
     filled, member = slots_of(ids_major, window, capacity)
     gate_of = jnp.sum(jnp.where(member, weights_major[:, None, :], 0.0), axis=0)
-    return (filled * gate_of[:, None, :]).reshape(window * capacity, -1)
+    return (filled * gate_of[:, None, :]).reshape(window * capacity, -1).astype(jnp.bfloat16)
 
 
 def local(activations, norm_gain, w_gate, w_up, w_down, route_ids, route_weights):
@@ -59,8 +63,13 @@
         return outgoing.astype(jnp.bfloat16).reshape(expert_count, capacity, half_width)
 
     def doubled(table):
-        table = jnp.repeat(table.reshape(window, capacity, tok_rows), 2, axis=0)
-        return table.reshape(slots, tok_rows)
+        return jnp.concatenate([table, table], axis=0)
+
+    same_side = [[2 * z + x for z in round_trip(window)] for x in range(2)]
+    both_sides = [same_side[0] + same_side[1]]
+
+    def exchange(chunks, groups):
+        return lax.all_to_all(chunks, "expert", 0, 0, tiled=True, axis_index_groups=groups)
 
     def experts(arrived, down_own, down_got):
         rows = lax.all_gather(arrived.reshape(slots, half_width), "tensor", axis=1, tiled=True)
@@ -83,11 +92,8 @@
         return total.astype(jnp.bfloat16)
 
     def combine(tokens, rows, table):
-        high = table.astype(jnp.bfloat16)
-        low = (table - high.astype(jnp.float32)).astype(jnp.bfloat16)
         dims = (((0,), (0,)), ((), ()))
-        moe_sum = lax.dot_general(high, rows, dims, preferred_element_type=jnp.float32)
-        moe_sum += lax.dot_general(low, rows, dims, preferred_element_type=jnp.float32)
+        moe_sum = lax.dot_general(table, rows, dims, preferred_element_type=jnp.float32)
         return (tokens.astype(jnp.float32) + moe_sum).astype(jnp.bfloat16)
 
     ids = route_ids[0, 0].T
@@ -98,14 +104,14 @@
     outgoing, start, routes, down_sent, down_own = lax.optimization_barrier(
         (outgoing, start, routes, down_sent, down_own)
     )
-    arrived = lax.all_to_all(outgoing, "expert", 0, 0, tiled=True)
+    arrived = exchange(outgoing, both_sides)
     residual = send(start, 2)
     routes_on = send(routes, 1)
     down_got = lax.ppermute(down_sent, "tensor", [(0, 1), (1, 0)])
     partial = experts(arrived, down_own, down_got)
-    by_side = partial.reshape(window, 2, capacity, half_width)
-    straight = lax.dynamic_index_in_dim(by_side, side, 1, keepdims=False)
-    crossed = lax.dynamic_index_in_dim(by_side, 1 - side, 1, keepdims=False)
+    by_side = partial.reshape(2, window, capacity, half_width)
+    straight = lax.dynamic_index_in_dim(by_side, side, 0, keepdims=False)
+    crossed = lax.dynamic_index_in_dim(by_side, 1 - side, 0, keepdims=False)
     straight, crossed, residual, routes_on, ids, gates = lax.optimization_barrier(
         (straight, crossed, residual, routes_on, route_ids[1, 0], route_weights[1, 0])
     )
@@ -116,17 +122,13 @@
     halves, combine_0, dispatch_1, combine_1 = lax.optimization_barrier(
         (halves.astype(jnp.bfloat16), combine_0, dispatch_1, combine_1)
     )
-    same_side = [[2 * z + x for z in range(window)] for x in range(2)]
-    returned = lax.all_to_all(
-        halves, "expert", 0, 0, tiled=True, axis_index_groups=same_side
-    ).reshape(window * capacity, half_width)
+    returned = exchange(halves, same_side).reshape(window * capacity, half_width)
     current = combine(residual, returned, combine_0)
 
-    arrived = lax.all_to_all(slot_rows(current, dispatch_1), "expert", 0, 0, tiled=True)
+    arrived = exchange(slot_rows(current, dispatch_1), both_sides)
     partial = experts(arrived, down_own, down_got)
-    returned = lax.all_to_all(
-        partial.reshape(expert_count, capacity, half_width), "expert", 0, 0, tiled=True
-    ).reshape(slots, half_width)
+    partial = partial.reshape(expert_count, capacity, half_width)
+    returned = exchange(partial, both_sides).reshape(slots, half_width)
     return combine(current, returned, combine_1)[None]
 
 

time: 118 us -> 115 us (0.975)
  the two profiles are of different devices: /device:TPU:32 before, /device:TPU:64 now
where the time goes in v4:
time: 115 us
  blocking collectives  54.4 us (47%)
  starting transfers between devices  26.3 us (23%)
  waiting for transfers between devices  21.6 us (19%)
  matrix products  5.52 us (5%)
  local copies, waits for them, and re-layouts  4.96 us (4%)
  other arithmetic  1.59 us (1%)
    all_to_all x3, blocking collectives, exchange(): lax.all_to_all(chunks, 'expert', 0, 0, tiled=True, axis_index_groups=groups)  46.1 us
    ppermute x5, waiting for transfers between devices, send(): return lax.ppermute(array, ('section', 'expert', 'tensor'), pairs)  14.6 us
    ppermute x5, starting transfers between devices, send(): return lax.ppermute(array, ('section', 'expert', 'tensor'), pairs)  12.2 us
    all_to_all x1, starting transfers between devices, exchange(): lax.all_to_all(chunks, 'expert', 0, 0, tiled=True, axis_index_groups=groups)  12.2 us
    all_to_all x1, waiting for transfers between devices, exchange(): lax.all_to_all(chunks, 'expert', 0, 0, tiled=True, axis_index_groups=groups)  6.94 us
    all_gather x2, blocking collectives, experts(): lax.all_gather(arrived.reshape(slots, half_width), 'tensor', axis=1, tile...  4.53 us
    all_gather x2, blocking collectives, experts(): hidden = lax.all_gather(hidden, 'tensor', axis=0, tiled=False)  3.8 us
  transfers between devices with their start and end apart: 7, of which 4 were waited for; matrix products, arithmetic and copies ran while one was open for 6% of the time, Pallas kernels for 0%

profile of v4, /device:TPU:64, one launch (start us, length us, event | category | flops | bytes accessed | tf_op | source)
XLA Modules:
  0.0 114.6 jit_solution(13757509570134277127)
XLA Ops:
  0.0 3.5 %collective-permute-start = (bf16[128,1280]{1,0:T(8,128)(2,1)}, bf16[128,1280]{1,0:T(8,128)(2,1)S(1)}, u32[]{:S(2)}, u32[]{:S(2)}) collective-permute-start(bf16[128,1280]{1,0:T(8,128)(2,1)} %bitcast.135), channel_id=1, source_target_pairs={{0,32},{1,33},{2,34},{3,35},{4,36},{5,37},{6,38},{7,39},{8,40},{9,... | collective-permute-start | bytes 983048 | tf_op jit(solution)/shard_map/ppermute | solution.py:19
  3.5 0.7 fusion.76
  4.2 0.7 convert_reduce_fusion
  5.0 0.1 fusion.50
  5.1 0.1 eq.138
  5.2 0.7 fusion.75
  5.9 0.1 fusion.57
  6.0 2.2 %dynamic-slice_bitcast_fusion = (bf16[256,1280]{1,0:T(8,128)(2,1)S(1)}, bf16[256,1280]{1,0:T(8,128)(2,1)}) fusion(bf16[1,256,2560]{2,1,0:T(8,128)(2,1)} %param.15, s32[]{:T(128)S(6)} %select_n.37, s32[]{:T(128)S(6)} %select_n.36), kind=kLoop, calls=%fused_computation.35 | loop fusion | bytes 2621448 | tf_op jit(solution)/shard_map/dynamic_slice | solution.py:102
  8.2 6.1 %collective-permute-done = bf16[128,1280]{1,0:T(8,128)(2,1)S(1)} collective-permute-done((bf16[128,1280]{1,0:T(8,128)(2,1)}, bf16[128,1280]{1,0:T(8,128)(2,1)S(1)}, u32[]{:S(2)}, u32[]{:S(2)}) %collective-permute-start) | collective-permute-done | bytes 327712 | tf_op jit(solution)/shard_map/ppermute | solution.py:19
  14.3 1.0 fusion.3
  15.3 12.2 %all-to-all-start = ((bf16[16,8,1280]{2,1,0:T(8,128)(2,1)}), bf16[16,8,1280]{2,1,0:T(8,128)(2,1)S(1)}, u32[]{:S(2)}, u32[]{:S(2)}) async-start(bf16[16,8,1280]{2,1,0:T(8,128)(2,1)} %fusion.3), calls=%async_computation | async-start | bytes 655360 | tf_op jit(solution)/shard_map/all_to_all | solution.py:72
  27.5 1.9 %collective-permute-start.1 = (bf16[256,1280]{1,0:T(8,128)(2,1)}, bf16[256,1280]{1,0:T(8,128)(2,1)S(1)}, u32[]{:S(2)}, u32[]{:S(2)}) collective-permute-start(bf16[256,1280]{1,0:T(8,128)(2,1)} %get-tuple-element.22), channel_id=1, source_target_pairs={{0,1},{1,0},{2,3},{3,2},{4,5},{5,4},{6,7},{7,6},{8,9},{9,8},{10,11... | collective-permute-start | bytes 1966088 | tf_op jit(solution)/shard_map/ppermute | solution.py:110
  29.5 2.0 %collective-permute-start.2 = (bf16[128,1280]{1,0:T(8,128)(2,1)}, bf16[128,1280]{1,0:T(8,128)(2,1)S(1)}, u32[]{:S(2)}, u32[]{:S(2)}) collective-permute-start(bf16[128,1280]{1,0:T(8,128)(2,1)} %bitcast.136), channel_id=1, source_target_pairs={{0,64},{1,65},{2,66},{3,67},{4,68},{5,69},{6,70},{7,71},{8,72},{9,... | collective-permute-start | bytes 983048 | tf_op jit(solution)/shard_map/ppermute | solution.py:19
  31.5 1.9 %collective-permute-start.3 = (f32[12,128]{1,0:T(8,128)S(1)}, f32[12,128]{1,0:T(8,128)S(1)}, u32[]{:S(2)}, u32[]{:S(2)}) collective-permute-start(f32[12,128]{1,0:T(8,128)S(1)} %pad_maximum_fusion.2), channel_id=1, source_target_pairs={{0,32},{1,33},{2,34},{3,35},{4,36},{5,37},{6,38},{7,39},{8,40},{9,... | collective-permute-start | bytes 18440 | tf_op jit(solution)/shard_map/ppermute | solution.py:19
  33.4 6.9 %all-to-all-done = bf16[16,8,1280]{2,1,0:T(8,128)(2,1)S(1)} async-done(((bf16[16,8,1280]{2,1,0:T(8,128)(2,1)}), bf16[16,8,1280]{2,1,0:T(8,128)(2,1)S(1)}, u32[]{:S(2)}, u32[]{:S(2)}) %all-to-all-start) | async-done | bytes 327712 | tf_op jit(solution)/shard_map/all_to_all | solution.py:72
  40.3 2.3 %all_gather.18 = bf16[128,2560]{1,0:T(8,128)(2,1)S(1)} all-gather(bf16[128,1280]{1,0:T(8,128)(2,1)S(1)} %bitcast.125), channel_id=1, replica_groups=mesh['section'=16,'expert'=16,'tensor'=2] {'tensor'}, dimensions={1}, use_global_device_ids=true | all-gather | bytes 983040 | tf_op jit(solution)/shard_map/all_gather | solution.py:75
  42.6 0.2 fusion.7
  42.8 0.0 copy-start.3
  42.9 0.4 fusion.19
  43.3 0.9 copy-done.3
  44.2 0.4 fusion.30
  44.6 1.9 %all-gather = bf16[256,256]{1,0:T(8,128)(2,1)S(1)} all-gather(bf16[128,256]{1,0:T(8,128)(2,1)S(1)} %fusion.30), channel_id=2, replica_groups=mesh['section'=16,'expert'=16,'tensor'=2] {'tensor'}, dimensions={0}, use_global_device_ids=true | all-gather | bytes 196608 | tf_op jit(solution)/shard_map/all_gather | solution.py:82
  46.5 0.3 fusion.42
  46.7 0.0 copy-start.2
  46.8 0.3 fusion
  47.1 0.3 copy-done.2
  47.4 0.1 fusion.61
  47.5 0.1 fusion.48
  47.6 0.1 fusion.49
  47.7 1.9 %collective-permute-start.4 = (bf16[8,8,1280]{2,1,0:T(8,128)(2,1)S(1)}, bf16[8,8,1280]{2,1,0:T(8,128)(2,1)S(1)}, u32[]{:S(2)}, u32[]{:S(2)}) collective-permute-start(bf16[8,8,1280]{2,1,0:T(8,128)(2,1)S(1)} %get-tuple-element.26), channel_id=1, source_target_pairs={{0,32},{1,33},{2,34},{3,35},{4,36},{5,37},{6,38},{7,39},{8,40},{9,... | collective-permute-start | bytes 491528 | tf_op jit(solution)/shard_map/ppermute | solution.py:19
  49.7 2.8 %collective-permute-start.5 = (bf16[8,8,1280]{2,1,0:T(8,128)(2,1)S(1)}, bf16[8,8,1280]{2,1,0:T(8,128)(2,1)S(1)}, u32[]{:S(2)}, u32[]{:S(2)}) collective-permute-start(bf16[8,8,1280]{2,1,0:T(8,128)(2,1)S(1)} %get-tuple-element.27), channel_id=1, source_target_pairs={{0,34},{1,35},{2,32},{3,33},{4,38},{5,39},{6,36},{7,37},{8,42},{9,... | collective-permute-start | bytes 491528 | tf_op jit(solution)/shard_map/ppermute | solution.py:19
  52.5 0.1 fusion.54
  52.6 0.1 fusion.55
  52.6 6.1 %collective-permute-done.4 = bf16[8,8,1280]{2,1,0:T(8,128)(2,1)S(1)} collective-permute-done((bf16[8,8,1280]{2,1,0:T(8,128)(2,1)S(1)}, bf16[8,8,1280]{2,1,0:T(8,128)(2,1)S(1)}, u32[]{:S(2)}, u32[]{:S(2)}) %collective-permute-start.4) | collective-permute-done | bytes 163872 | tf_op jit(solution)/shard_map/ppermute | solution.py:19
  58.8 2.4 %collective-permute-done.5 = bf16[8,8,1280]{2,1,0:T(8,128)(2,1)S(1)} collective-permute-done((bf16[8,8,1280]{2,1,0:T(8,128)(2,1)S(1)}, bf16[8,8,1280]{2,1,0:T(8,128)(2,1)S(1)}, u32[]{:S(2)}, u32[]{:S(2)}) %collective-permute-start.5) | collective-permute-done | bytes 163872 | tf_op jit(solution)/shard_map/ppermute | solution.py:19
  61.2 11.2 %all_to_all.20 = bf16[8,8,1280]{2,1,0:T(8,128)(2,1)S(1)} all-to-all(bf16[8,8,1280]{2,1,0:T(8,128)(2,1)S(1)} %add_convert_fusion.1), channel_id=1, replica_groups={{0,8,16,24,28,20,12,4},{2,10,18,26,30,22,14,6},{1,9,17,25,29,21,13,5},{..., dimensions={0} | all-to-all | bytes 327680 | tf_op jit(solution)/shard_map/all_to_all | solution.py:72
  72.4 0.3 add_convert_fusion
  72.7 0.2 fusion.4
  73.0 17.2 %all_to_all.21 = bf16[16,8,1280]{2,1,0:T(8,128)(2,1)S(1)} all-to-all(bf16[16,8,1280]{2,1,0:T(8,128)(2,1)S(1)} %fusion.4), channel_id=1, replica_groups={{0,8,16,24,28,20,12,4,2,10,18,26,30,22,14,6},{1,9,17,25,29,21,13,5,3,11..., dimensions={0} | all-to-all | bytes 655360 | tf_op jit(solution)/shard_map/all_to_all | solution.py:72
  90.2 2.3 %all_gather.21 = bf16[128,2560]{1,0:T(8,128)(2,1)S(1)} all-gather(bf16[128,1280]{1,0:T(8,128)(2,1)S(1)} %bitcast.127), channel_id=1, replica_groups=mesh['section'=16,'expert'=16,'tensor'=2] {'tensor'}, dimensions={1}, use_global_device_ids=true | all-gather | bytes 983040 | tf_op jit(solution)/shard_map/all_gather | solution.py:75
  92.4 0.2 fusion.10
  92.6 0.4 fusion.17
  93.1 0.4 fusion.27
  93.5 1.9 %all-gather.1 = bf16[256,256]{1,0:T(8,128)(2,1)S(1)} all-gather(bf16[128,256]{1,0:T(8,128)(2,1)S(1)} %fusion.27), channel_id=3, replica_groups=mesh['section'=16,'expert'=16,'tensor'=2] {'tensor'}, dimensions={0}, use_global_device_ids=true | all-gather | bytes 196608 | tf_op jit(solution)/shard_map/all_gather | solution.py:82
  95.4 0.3 fusion.39
  95.6 0.3 fusion.6
  95.9 17.7 %all_to_all.22 = bf16[16,8,1280]{2,1,0:T(8,128)(2,1)S(1)} all-to-all(bf16[16,8,1280]{2,1,0:T(8,128)(2,1)S(1)} %fusion.6), channel_id=1, replica_groups={{0,8,16,24,28,20,12,4,2,10,18,26,30,22,14,6},{1,9,17,25,29,21,13,5,3,11..., dimensions={0} | all-to-all | bytes 655360 | tf_op jit(solution)/shard_map/all_to_all | solution.py:72
  113.6 1.0 fusion.5
  (20 shorter events, 0.2 us)
Async XLA Ops:
  0.0 42.8 %copy-start = (bf16[1,2560,256]{2,1,0:T(8,128)(2,1)S(1)}, bf16[1,2560,256]{2,1,0:T(8,128)(2,1)}, u32[]{:S(2)}) copy-start(bf16[1,2560,256]{2,1,0:T(8,128)(2,1)} %param.13) | copy-start | bytes 3932164
  0.0 14.3 %collective-permute-start = (bf16[128,1280]{1,0:T(8,128)(2,1)}, bf16[128,1280]{1,0:T(8,128)(2,1)S(1)}, u32[]{:S(2)}, u32[]{:S(2)}) collective-permute-start(bf16[128,1280]{1,0:T(8,128)(2,1)} %bitcast.135), channel_id=1, source_target_pairs={{0,32},{1,33},{2,34},{3,35},{4,36},{5,37},{6,38},{7,39},{8,40},{9,... | collective-permute-start | bytes 983048 | tf_op jit(solution)/shard_map/ppermute | solution.py:19
  8.2 19.3 %copy-start.1 = (bf16[1,2560]{1,0:T(2,128)(2,1)S(1)}, bf16[1,2560]{1,0:T(2,128)(2,1)}, u32[]{:S(2)}) copy-start(bf16[1,2560]{1,0:T(2,128)(2,1)} %param.12) | copy-start | bytes 15364
  15.3 25.0 %all-to-all-start = ((bf16[16,8,1280]{2,1,0:T(8,128)(2,1)}), bf16[16,8,1280]{2,1,0:T(8,128)(2,1)S(1)}, u32[]{:S(2)}, u32[]{:S(2)}) async-start(bf16[16,8,1280]{2,1,0:T(8,128)(2,1)} %fusion.3), calls=%async_computation | async-start | bytes 655360 | tf_op jit(solution)/shard_map/all_to_all | solution.py:72
  27.5 19.2 %collective-permute-start.1 = (bf16[256,1280]{1,0:T(8,128)(2,1)}, bf16[256,1280]{1,0:T(8,128)(2,1)S(1)}, u32[]{:S(2)}, u32[]{:S(2)}) collective-permute-start(bf16[256,1280]{1,0:T(8,128)(2,1)} %get-tuple-element.22), channel_id=1, source_target_pairs={{0,1},{1,0},{2,3},{3,2},{4,5},{5,4},{6,7},{7,6},{8,9},{9,8},{10,11... | collective-permute-start | bytes 1966088 | tf_op jit(solution)/shard_map/ppermute | solution.py:110
  29.5 17.6 %collective-permute-start.2 = (bf16[128,1280]{1,0:T(8,128)(2,1)}, bf16[128,1280]{1,0:T(8,128)(2,1)S(1)}, u32[]{:S(2)}, u32[]{:S(2)}) collective-permute-start(bf16[128,1280]{1,0:T(8,128)(2,1)} %bitcast.136), channel_id=1, source_target_pairs={{0,64},{1,65},{2,66},{3,67},{4,68},{5,69},{6,70},{7,71},{8,72},{9,... | collective-permute-start | bytes 983048 | tf_op jit(solution)/shard_map/ppermute | solution.py:19
  31.5 15.6 %collective-permute-start.3 = (f32[12,128]{1,0:T(8,128)S(1)}, f32[12,128]{1,0:T(8,128)S(1)}, u32[]{:S(2)}, u32[]{:S(2)}) collective-permute-start(f32[12,128]{1,0:T(8,128)S(1)} %pad_maximum_fusion.2), channel_id=1, source_target_pairs={{0,32},{1,33},{2,34},{3,35},{4,36},{5,37},{6,38},{7,39},{8,40},{9,... | collective-permute-start | bytes 18440 | tf_op jit(solution)/shard_map/ppermute | solution.py:19
  42.8 1.3 %copy-start.3 = (bf16[1,2560,256]{2,1,0:T(8,128)(2,1)S(1)}, bf16[1,2560,256]{2,1,0:T(8,128)(2,1)}, u32[]{:S(2)}) copy-start(bf16[1,2560,256]{2,1,0:T(8,128)(2,1)} %param.14) | copy-start | bytes 3932164
  46.7 0.7 copy-start.2
  47.7 11.0 %collective-permute-start.4 = (bf16[8,8,1280]{2,1,0:T(8,128)(2,1)S(1)}, bf16[8,8,1280]{2,1,0:T(8,128)(2,1)S(1)}, u32[]{:S(2)}, u32[]{:S(2)}) collective-permute-start(bf16[8,8,1280]{2,1,0:T(8,128)(2,1)S(1)} %get-tuple-element.26), channel_id=1, source_target_pairs={{0,32},{1,33},{2,34},{3,35},{4,36},{5,37},{6,38},{7,39},{8,40},{9,... | collective-permute-start | bytes 491528 | tf_op jit(solution)/shard_map/ppermute | solution.py:19
  49.7 11.5 %collective-permute-start.5 = (bf16[8,8,1280]{2,1,0:T(8,128)(2,1)S(1)}, bf16[8,8,1280]{2,1,0:T(8,128)(2,1)S(1)}, u32[]{:S(2)}, u32[]{:S(2)}) collective-permute-start(bf16[8,8,1280]{2,1,0:T(8,128)(2,1)S(1)} %get-tuple-element.27), channel_id=1, source_target_pairs={{0,34},{1,35},{2,32},{3,33},{4,38},{5,39},{6,36},{7,37},{8,42},{9,... | collective-permute-start | bytes 491528 | tf_op jit(solution)/shard_map/ppermute | solution.py:19

commit v5 on v4

--- a/solution.py
+++ b/solution.py
@@ -25,7 +25,8 @@
 
 def slots_of(ids_major, window, capacity):
     tok_count = ids_major.shape[1]
-    experts_col = jnp.array(round_trip(window), dtype=jnp.int32)[None, :, None]
+    place = lax.broadcasted_iota(jnp.int32, (1, window, 1), 1)
+    experts_col = jnp.where(2 * place < window, 2 * place, 2 * window - 1 - 2 * place)
     member = ids_major[:, None, :] == experts_col
     named = jnp.sum(member.astype(jnp.float32), axis=0)
     row_pos = jnp.arange(tok_count, dtype=jnp.int32)
@@ -56,7 +57,6 @@
     slots = expert_count * capacity
     core = lax.axis_index("tensor")
     side = lax.axis_index("expert") % 2
-    gain_row = norm_gain[0].astype(jnp.float32)
 
     def slot_rows(tokens, twice):
         outgoing = jnp.dot(twice, tokens, preferred_element_type=jnp.float32)
@@ -97,14 +97,25 @@
         return (tokens.astype(jnp.float32) + moe_sum).astype(jnp.bfloat16)
 
     ids = route_ids[0, 0].T
-    outgoing = slot_rows(send(start, 1), doubled(dispatch_rows(ids, window, capacity)))
-    routes = jnp.concatenate([ids.astype(jnp.float32), route_weights[0, 0].T], axis=0)
-    down_own = lax.dynamic_slice_in_dim(w_down[0], core * half_width, half_width, 1)
+    shifted = send(start, 1, (0, 1))
+    pairs = [[2 * z, 2 * z + 1] for z in range(window)]
+    both_ids = lax.all_gather(ids, "expert", axis_index_groups=pairs)
+    ids_here = jnp.where(side == core, both_ids[0], both_ids[1])
+    outgoing = slot_rows(shifted, doubled(dispatch_rows(ids_here, window, capacity)))
     down_sent = lax.dynamic_slice_in_dim(w_down[0], (1 - core) * half_width, half_width, 1)
-    outgoing, start, routes, down_sent, down_own = lax.optimization_barrier(
-        (outgoing, start, routes, down_sent, down_own)
+    outgoing, start, gates, down_sent, down_all, gain = lax.optimization_barrier(
+        (outgoing, start, route_weights, down_sent, w_down[0], norm_gain)
     )
-    arrived = exchange(outgoing, both_sides)
+    gain_row = gain.astype(jnp.float32)
+    down_own = lax.dynamic_slice_in_dim(down_all, core * half_width, half_width, 1)
+    routes = jnp.concatenate([ids.astype(jnp.float32), gates[0, 0].T], axis=0)
+    orders = [
+        [2 * e for e in same_side[0] + same_side[1]],
+        [2 * e + 1 for e in same_side[1] + same_side[0]],
+    ]
+    arrived = lax.all_to_all(
+        outgoing, ("expert", "tensor"), 0, 0, tiled=True, axis_index_groups=orders
+    )
     residual = send(start, 2)
     routes_on = send(routes, 1)
     down_got = lax.ppermute(down_sent, "tensor", [(0, 1), (1, 0)])
@@ -113,7 +124,7 @@
     straight = lax.dynamic_index_in_dim(by_side, side, 0, keepdims=False)
     crossed = lax.dynamic_index_in_dim(by_side, 1 - side, 0, keepdims=False)
     straight, crossed, residual, routes_on, ids, gates = lax.optimization_barrier(
-        (straight, crossed, residual, routes_on, route_ids[1, 0], route_weights[1, 0])
+        (straight, crossed, residual, routes_on, route_ids[1, 0], gates[1, 0])
     )
     halves = send(straight, 1).astype(jnp.float32) + send(crossed, 1, (1, 1)).astype(jnp.float32)
     dispatch_1 = doubled(dispatch_rows(ids.T, window, capacity))

time: 115 us -> 114 us (level)
  blocking collectives: 54.4 us -> 62 us
  waiting for transfers between devices: 21.6 us -> 17.1 us
  local copies, waits for them, and re-layouts: 4.96 us -> 1.84 us
    all_gather x0 -> x1, blocking collectives: none -> 7.4 us  [local(): both_ids = lax.all_gather(ids, 'expert', axis_index_groups=pairs)]
    ppermute x5, waiting for transfers between devices: 14.6 us -> 10.9 us  [send(): return lax.ppermute(array, ('section', 'expert', 'tensor'), pairs)]
    dynamic_slice x1, local copies, waits for them, and re-layouts: 2.21 us -> 0.05 us  [local(): lax.dynamic_slice_in_dim(w_down[0], (1 - core) * half_width, half_width, 1)]
  transfers between devices with their start and end apart: 7 -> 7, of which waited for: 4 -> 4; matrix products, arithmetic and copies ran while one was open for 6% -> 3% of each run, Pallas kernels for 0% -> 0%
where the time goes in v5:
time: 114 us
  blocking collectives  62 us (54%)
  starting transfers between devices  26.2 us (23%)
  waiting for transfers between devices  17.1 us (15%)
  matrix products  5.46 us (5%)
  local copies, waits for them, and re-layouts  1.84 us (2%)
    all_to_all x3, blocking collectives, exchange(): lax.all_to_all(chunks, 'expert', 0, 0, tiled=True, axis_index_groups=groups)  46.1 us
    ppermute x5, starting transfers between devices, send(): return lax.ppermute(array, ('section', 'expert', 'tensor'), pairs)  12.5 us
    all_to_all x1, starting transfers between devices, local(): lax.all_to_all(outgoing, ('expert', 'tensor'), 0, 0, tiled=True, axis_ind...  11.7 us
    ppermute x5, waiting for transfers between devices, send(): return lax.ppermute(array, ('section', 'expert', 'tensor'), pairs)  10.9 us
    all_gather x1, blocking collectives, local(): both_ids = lax.all_gather(ids, 'expert', axis_index_groups=pairs)  7.4 us
    all_to_all x1, waiting for transfers between devices, local(): lax.all_to_all(outgoing, ('expert', 'tensor'), 0, 0, tiled=True, axis_ind...  6.2 us
    all_gather x2, blocking collectives, experts(): lax.all_gather(arrived.reshape(slots, half_width), 'tensor', axis=1, tile...  4.66 us
    all_gather x2, blocking collectives, experts(): hidden = lax.all_gather(hidden, 'tensor', axis=0, tiled=False)  3.8 us
  transfers between devices with their start and end apart: 7, of which 4 were waited for; matrix products, arithmetic and copies ran while one was open for 3% of the time, Pallas kernels for 0%

profile of v5, /device:TPU:64, one launch (start us, length us, event | category | flops | bytes accessed | tf_op | source)
XLA Modules:
  0.0 113.9 jit_solution(7752847441463983453)
XLA Ops:
  0.0 3.5 %collective-permute-start = (bf16[128,1280]{1,0:T(8,128)(2,1)}, bf16[128,1280]{1,0:T(8,128)(2,1)S(1)}, u32[]{:S(2)}, u32[]{:S(2)}) collective-permute-start(bf16[128,1280]{1,0:T(8,128)(2,1)} %bitcast.137), channel_id=1, source_target_pairs={{0,32},{1,35},{2,34},{3,33},{4,36},{5,39},{6,38},{7,37},{8,40},{9,... | collective-permute-start | bytes 983048 | tf_op jit(solution)/shard_map/ppermute | solution.py:19
  3.6 0.7 fusion.78
  4.3 7.4 %all-gather.3 = s32[2,6,128]{2,1,0:T(8,128)S(1)} all-gather(s32[1,6,128]{2,1,0:T(8,128)S(1)} %get-tuple-element.50), channel_id=2, replica_groups={{0,2},{4,6},{8,10},{12,14},{16,18},{20,22},{24,26},{28,30},{1,3},{5,7},..., dimensions={0}, use_global_device_ids=true | all-gather | bytes 9216 | tf_op jit(solution)/shard_map/all_gather | solution.py:102
  11.7 0.1 eq.126
  11.8 0.1 convert_reduce_fusion
  11.8 0.1 fusion.52
  12.0 0.1 fusion.59
  12.1 0.0 copy-done
  12.1 0.0 copy-start.2
  12.1 0.1 dynamic-slice_bitcast_fusion
  12.2 2.6 %collective-permute-done = bf16[128,1280]{1,0:T(8,128)(2,1)S(1)} collective-permute-done((bf16[128,1280]{1,0:T(8,128)(2,1)}, bf16[128,1280]{1,0:T(8,128)(2,1)S(1)}, u32[]{:S(2)}, u32[]{:S(2)}) %collective-permute-start) | collective-permute-done | bytes 327712 | tf_op jit(solution)/shard_map/ppermute | solution.py:19
  14.7 1.0 fusion.3
  15.7 11.7 %all-to-all-start = ((bf16[16,8,1280]{2,1,0:T(8,128)(2,1)}), bf16[16,8,1280]{2,1,0:T(8,128)(2,1)S(1)}, u32[]{:S(2)}, u32[]{:S(2)}) async-start(bf16[16,8,1280]{2,1,0:T(8,128)(2,1)} %fusion.3), calls=%async_computation | async-start | bytes 655360 | tf_op jit(solution)/shard_map/all_to_all | solution.py:116
  27.5 1.9 %collective-permute-start.1 = (bf16[256,1280]{1,0:T(8,128)(2,1)S(1)}, bf16[256,1280]{1,0:T(8,128)(2,1)S(1)}, u32[]{:S(2)}, u32[]{:S(2)}) collective-permute-start(bf16[256,1280]{1,0:T(8,128)(2,1)S(1)} %dynamic-slice_bitcast_fusion), channel_id=1, source_target_pairs={{0,1},{1,0},{2,3},{3,2},{4,5},{5,4},{6,7},{7,6},{8,9},{9,8},{10,11... | collective-permute-start | bytes 1966088 | tf_op jit(solution)/shard_map/ppermute | solution.py:121
  29.4 1.9 %collective-permute-start.2 = (bf16[128,1280]{1,0:T(8,128)(2,1)}, bf16[128,1280]{1,0:T(8,128)(2,1)S(1)}, u32[]{:S(2)}, u32[]{:S(2)}) collective-permute-start(bf16[128,1280]{1,0:T(8,128)(2,1)} %bitcast.138), channel_id=1, source_target_pairs={{0,64},{1,65},{2,66},{3,67},{4,68},{5,69},{6,70},{7,71},{8,72},{9,... | collective-permute-start | bytes 983048 | tf_op jit(solution)/shard_map/ppermute | solution.py:19
  31.4 2.0 %collective-permute-start.3 = (f32[12,128]{1,0:T(8,128)S(1)}, f32[12,128]{1,0:T(8,128)S(1)}, u32[]{:S(2)}, u32[]{:S(2)}) collective-permute-start(f32[12,128]{1,0:T(8,128)S(1)} %pad_maximum_fusion.2), channel_id=1, source_target_pairs={{0,32},{1,33},{2,34},{3,35},{4,36},{5,37},{6,38},{7,39},{8,40},{9,... | collective-permute-start | bytes 18440 | tf_op jit(solution)/shard_map/ppermute | solution.py:19
  33.5 6.2 %all-to-all-done = bf16[16,8,1280]{2,1,0:T(8,128)(2,1)S(1)} async-done(((bf16[16,8,1280]{2,1,0:T(8,128)(2,1)}), bf16[16,8,1280]{2,1,0:T(8,128)(2,1)S(1)}, u32[]{:S(2)}, u32[]{:S(2)}) %all-to-all-start) | async-done | bytes 327712 | tf_op jit(solution)/shard_map/all_to_all | solution.py:116
  39.7 2.4 %all_gather.26 = bf16[128,2560]{1,0:T(8,128)(2,1)S(1)} all-gather(bf16[128,1280]{1,0:T(8,128)(2,1)S(1)} %bitcast.128), channel_id=1, replica_groups=mesh['section'=16,'expert'=16,'tensor'=2] {'tensor'}, dimensions={1}, use_global_device_ids=true | all-gather | bytes 983040 | tf_op jit(solution)/shard_map/all_gather | solution.py:75
  42.1 0.2 fusion.7
  42.3 0.0 copy-start.4
  42.3 0.4 fusion.19
  42.7 0.9 copy-done.4
  43.6 0.4 fusion.30
  44.1 1.9 %all-gather.1 = bf16[256,256]{1,0:T(8,128)(2,1)S(1)} all-gather(bf16[128,256]{1,0:T(8,128)(2,1)S(1)} %fusion.30), channel_id=3, replica_groups=mesh['section'=16,'expert'=16,'tensor'=2] {'tensor'}, dimensions={0}, use_global_device_ids=true | all-gather | bytes 196608 | tf_op jit(solution)/shard_map/all_gather | solution.py:82
  46.0 0.2 fusion.35
  46.2 0.3 fusion
  46.5 1.9 %collective-permute-start.5 = (bf16[8,8,1280]{2,1,0:T(8,128)(2,1)S(1)}, bf16[8,8,1280]{2,1,0:T(8,128)(2,1)S(1)}, u32[]{:S(2)}, u32[]{:S(2)}) collective-permute-start(bf16[8,8,1280]{2,1,0:T(8,128)(2,1)S(1)} %get-tuple-element.29), channel_id=1, source_target_pairs={{0,34},{1,35},{2,32},{3,33},{4,38},{5,39},{6,36},{7,37},{8,42},{9,... | collective-permute-start | bytes 491528 | tf_op jit(solution)/shard_map/ppermute | solution.py:19
  48.5 3.1 %collective-permute-start.4 = (bf16[8,8,1280]{2,1,0:T(8,128)(2,1)S(1)}, bf16[8,8,1280]{2,1,0:T(8,128)(2,1)S(1)}, u32[]{:S(2)}, u32[]{:S(2)}) collective-permute-start(bf16[8,8,1280]{2,1,0:T(8,128)(2,1)S(1)} %get-tuple-element.28), channel_id=1, source_target_pairs={{0,32},{1,33},{2,34},{3,35},{4,36},{5,37},{6,38},{7,39},{8,40},{9,... | collective-permute-start | bytes 491528 | tf_op jit(solution)/shard_map/ppermute | solution.py:19
  51.6 0.1 fusion.63
  51.7 0.1 fusion.50
  51.8 0.1 fusion.51
  52.0 0.1 fusion.56
  52.1 0.1 fusion.57
  52.2 6.7 %collective-permute-done.5 = bf16[8,8,1280]{2,1,0:T(8,128)(2,1)S(1)} collective-permute-done((bf16[8,8,1280]{2,1,0:T(8,128)(2,1)S(1)}, bf16[8,8,1280]{2,1,0:T(8,128)(2,1)S(1)}, u32[]{:S(2)}, u32[]{:S(2)}) %collective-permute-start.5) | collective-permute-done | bytes 163872 | tf_op jit(solution)/shard_map/ppermute | solution.py:19
  58.8 1.7 %collective-permute-done.4 = bf16[8,8,1280]{2,1,0:T(8,128)(2,1)S(1)} collective-permute-done((bf16[8,8,1280]{2,1,0:T(8,128)(2,1)S(1)}, bf16[8,8,1280]{2,1,0:T(8,128)(2,1)S(1)}, u32[]{:S(2)}, u32[]{:S(2)}) %collective-permute-start.4) | collective-permute-done | bytes 163872 | tf_op jit(solution)/shard_map/ppermute | solution.py:19
  60.5 10.8 %all_to_all.20 = bf16[8,8,1280]{2,1,0:T(8,128)(2,1)S(1)} all-to-all(bf16[8,8,1280]{2,1,0:T(8,128)(2,1)S(1)} %add_convert_fusion.1), channel_id=1, replica_groups={{0,8,16,24,28,20,12,4},{2,10,18,26,30,22,14,6},{1,9,17,25,29,21,13,5},{..., dimensions={0} | all-to-all | bytes 327680 | tf_op jit(solution)/shard_map/all_to_all | solution.py:72
  71.4 0.3 add_convert_fusion
  71.7 0.2 fusion.4
  71.9 17.6 %all_to_all.21 = bf16[16,8,1280]{2,1,0:T(8,128)(2,1)S(1)} all-to-all(bf16[16,8,1280]{2,1,0:T(8,128)(2,1)S(1)} %fusion.4), channel_id=1, replica_groups={{0,8,16,24,28,20,12,4,2,10,18,26,30,22,14,6},{1,9,17,25,29,21,13,5,3,11..., dimensions={0} | all-to-all | bytes 655360 | tf_op jit(solution)/shard_map/all_to_all | solution.py:72
  89.5 2.3 %all_gather.29 = bf16[128,2560]{1,0:T(8,128)(2,1)S(1)} all-gather(bf16[128,1280]{1,0:T(8,128)(2,1)S(1)} %bitcast.130), channel_id=1, replica_groups=mesh['section'=16,'expert'=16,'tensor'=2] {'tensor'}, dimensions={1}, use_global_device_ids=true | all-gather | bytes 983040 | tf_op jit(solution)/shard_map/all_gather | solution.py:75
  91.7 0.2 fusion.10
  92.0 0.4 fusion.17
  92.4 0.4 fusion.27
  92.8 1.9 %all-gather.2 = bf16[256,256]{1,0:T(8,128)(2,1)S(1)} all-gather(bf16[128,256]{1,0:T(8,128)(2,1)S(1)} %fusion.27), channel_id=4, replica_groups=mesh['section'=16,'expert'=16,'tensor'=2] {'tensor'}, dimensions={0}, use_global_device_ids=true | all-gather | bytes 196608 | tf_op jit(solution)/shard_map/all_gather | solution.py:82
  94.7 0.2 fusion.33
  94.9 0.3 fusion.6
  95.2 17.7 %all_to_all.22 = bf16[16,8,1280]{2,1,0:T(8,128)(2,1)S(1)} all-to-all(bf16[16,8,1280]{2,1,0:T(8,128)(2,1)S(1)} %fusion.6), channel_id=1, replica_groups={{0,8,16,24,28,20,12,4,2,10,18,26,30,22,14,6},{1,9,17,25,29,21,13,5,3,11..., dimensions={0} | all-to-all | bytes 655360 | tf_op jit(solution)/shard_map/all_to_all | solution.py:72
  112.9 1.0 fusion.5
  (27 shorter events, 0.2 us)
Async XLA Ops:
  0.0 12.1 %copy-start = (bf16[1,256,2560]{2,1,0:T(8,128)(2,1)S(1)}, bf16[1,256,2560]{2,1,0:T(8,128)(2,1)}, u32[]{:S(2)}) copy-start(bf16[1,256,2560]{2,1,0:T(8,128)(2,1)} %param.11) | copy-start | bytes 3932164
  0.0 14.7 %collective-permute-start = (bf16[128,1280]{1,0:T(8,128)(2,1)}, bf16[128,1280]{1,0:T(8,128)(2,1)S(1)}, u32[]{:S(2)}, u32[]{:S(2)}) collective-permute-start(bf16[128,1280]{1,0:T(8,128)(2,1)} %bitcast.137), channel_id=1, source_target_pairs={{0,32},{1,35},{2,34},{3,33},{4,36},{5,39},{6,38},{7,37},{8,40},{9,... | collective-permute-start | bytes 983048 | tf_op jit(solution)/shard_map/ppermute | solution.py:19
  12.1 15.4 %copy-start.1 = (f32[2,1,128,6]{2,1,3,0:T(1,128)S(1)}, f32[2,1,128,6]{2,1,3,0:T(1,128)}, u32[]{:S(2)}) copy-start(f32[2,1,128,6]{2,1,3,0:T(1,128)} %param.13) | copy-start | bytes 18436
  12.1 21.3 %slice-start = ((f32[2,1,128,6]{2,1,3,0:T(1,128)}), f32[1,1,128,6]{2,1,3,0:T(1,128)S(1)}, s32[]{:S(2)}) async-start(f32[2,1,128,6]{2,1,3,0:T(1,128)} %param.13), calls=%async_computation.4 | async-start | bytes 6144 | tf_op jit(solution)/shard_map/slice | solution.py:127
  12.1 21.3 %copy-start.2 = (bf16[1,2560]{1,0:T(2,128)(2,1)S(1)}, bf16[1,2560]{1,0:T(2,128)(2,1)}, u32[]{:S(2)}) copy-start(bf16[1,2560]{1,0:T(2,128)(2,1)} %param.8) | copy-start | bytes 15364
  15.7 24.0 %all-to-all-start = ((bf16[16,8,1280]{2,1,0:T(8,128)(2,1)}), bf16[16,8,1280]{2,1,0:T(8,128)(2,1)S(1)}, u32[]{:S(2)}, u32[]{:S(2)}) async-start(bf16[16,8,1280]{2,1,0:T(8,128)(2,1)} %fusion.3), calls=%async_computation | async-start | bytes 655360 | tf_op jit(solution)/shard_map/all_to_all | solution.py:116
  27.5 18.7 %collective-permute-start.1 = (bf16[256,1280]{1,0:T(8,128)(2,1)S(1)}, bf16[256,1280]{1,0:T(8,128)(2,1)S(1)}, u32[]{:S(2)}, u32[]{:S(2)}) collective-permute-start(bf16[256,1280]{1,0:T(8,128)(2,1)S(1)} %dynamic-slice_bitcast_fusion), channel_id=1, source_target_pairs={{0,1},{1,0},{2,3},{3,2},{4,5},{5,4},{6,7},{7,6},{8,9},{9,8},{10,11... | collective-permute-start | bytes 1966088 | tf_op jit(solution)/shard_map/ppermute | solution.py:121
  29.4 17.1 %collective-permute-start.2 = (bf16[128,1280]{1,0:T(8,128)(2,1)}, bf16[128,1280]{1,0:T(8,128)(2,1)S(1)}, u32[]{:S(2)}, u32[]{:S(2)}) collective-permute-start(bf16[128,1280]{1,0:T(8,128)(2,1)} %bitcast.138), channel_id=1, source_target_pairs={{0,64},{1,65},{2,66},{3,67},{4,68},{5,69},{6,70},{7,71},{8,72},{9,... | collective-permute-start | bytes 983048 | tf_op jit(solution)/shard_map/ppermute | solution.py:19
  31.4 15.1 %collective-permute-start.3 = (f32[12,128]{1,0:T(8,128)S(1)}, f32[12,128]{1,0:T(8,128)S(1)}, u32[]{:S(2)}, u32[]{:S(2)}) collective-permute-start(f32[12,128]{1,0:T(8,128)S(1)} %pad_maximum_fusion.2), channel_id=1, source_target_pairs={{0,32},{1,33},{2,34},{3,35},{4,36},{5,37},{6,38},{7,39},{8,40},{9,... | collective-permute-start | bytes 18440 | tf_op jit(solution)/shard_map/ppermute | solution.py:19
  39.7 2.6 %copy-start.3 = (bf16[1,2560,256]{2,1,0:T(8,128)(2,1)S(1)}, bf16[1,2560,256]{2,1,0:T(8,128)(2,1)}, u32[]{:S(2)}) copy-start(bf16[1,2560,256]{2,1,0:T(8,128)(2,1)} %param.9) | copy-start | bytes 3932164
  42.3 1.3 %copy-start.4 = (bf16[1,2560,256]{2,1,0:T(8,128)(2,1)S(1)}, bf16[1,2560,256]{2,1,0:T(8,128)(2,1)}, u32[]{:S(2)}) copy-start(bf16[1,2560,256]{2,1,0:T(8,128)(2,1)} %param.10) | copy-start | bytes 3932164
  46.5 12.3 %collective-permute-start.5 = (bf16[8,8,1280]{2,1,0:T(8,128)(2,1)S(1)}, bf16[8,8,1280]{2,1,0:T(8,128)(2,1)S(1)}, u32[]{:S(2)}, u32[]{:S(2)}) collective-permute-start(bf16[8,8,1280]{2,1,0:T(8,128)(2,1)S(1)} %get-tuple-element.29), channel_id=1, source_target_pairs={{0,34},{1,35},{2,32},{3,33},{4,38},{5,39},{6,36},{7,37},{8,42},{9,... | collective-permute-start | bytes 491528 | tf_op jit(solution)/shard_map/ppermute | solution.py:19
  48.5 12.0 %collective-permute-start.4 = (bf16[8,8,1280]{2,1,0:T(8,128)(2,1)S(1)}, bf16[8,8,1280]{2,1,0:T(8,128)(2,1)S(1)}, u32[]{:S(2)}, u32[]{:S(2)}) collective-permute-start(bf16[8,8,1280]{2,1,0:T(8,128)(2,1)S(1)} %get-tuple-element.28), channel_id=1, source_target_pairs={{0,32},{1,33},{2,34},{3,35},{4,36},{5,37},{6,38},{7,39},{8,40},{9,... | collective-permute-start | bytes 491528 | tf_op jit(solution)/shard_map/ppermute | solution.py:19

commit v6 on v5

--- a/solution.py
+++ b/solution.py
@@ -20,13 +20,14 @@
 
 
 def round_trip(count):
-    return list(range(0, count, 2)) + list(range(count - 1, 0, -2))
+    return [-2 * i % count for i in range(count // 2)] + list(range(1, count, 2))
 
 
 def slots_of(ids_major, window, capacity):
     tok_count = ids_major.shape[1]
     place = lax.broadcasted_iota(jnp.int32, (1, window, 1), 1)
-    experts_col = jnp.where(2 * place < window, 2 * place, 2 * window - 1 - 2 * place)
+    experts_col = jnp.where(2 * place < window, window - 2 * place, 2 * place - window + 1)
+    experts_col = jnp.where(place == 0, 0, experts_col)
     member = ids_major[:, None, :] == experts_col
     named = jnp.sum(member.astype(jnp.float32), axis=0)
     row_pos = jnp.arange(tok_count, dtype=jnp.int32)

time: 114 us -> 114 us (level)
  the two profiles are of different devices: /device:TPU:64 before, /device:TPU:24 now
where the time goes in v6:
time: 114 us; the launch traced here: 113 us
  blocking collectives  64.3 us (56%)
  starting transfers between devices  33.7 us (30%)
  waiting for transfers between devices  6.84 us (6%)
  matrix products  5.46 us (5%)
  local copies, waits for them, and re-layouts  1.83 us (2%)
    all_to_all x3, blocking collectives, exchange(): lax.all_to_all(chunks, 'expert', 0, 0, tiled=True, axis_index_groups=groups)  48.5 us
    ppermute x5, starting transfers between devices, send(): return lax.ppermute(array, ('section', 'expert', 'tensor'), pairs)  20.2 us
    all_to_all x1, starting transfers between devices, local(): lax.all_to_all(outgoing, ('expert', 'tensor'), 0, 0, tiled=True, axis_ind...  11.6 us
    all_gather x1, blocking collectives, local(): both_ids = lax.all_gather(ids, 'expert', axis_index_groups=pairs)  7.4 us
    all_gather x2, blocking collectives, experts(): lax.all_gather(arrived.reshape(slots, half_width), 'tensor', axis=1, tile...  4.66 us
    ppermute x5, waiting for transfers between devices, send(): return lax.ppermute(array, ('section', 'expert', 'tensor'), pairs)  4.32 us
    all_gather x2, blocking collectives, experts(): hidden = lax.all_gather(hidden, 'tensor', axis=0, tiled=False)  3.8 us
    all_to_all x1, waiting for transfers between devices, local(): lax.all_to_all(outgoing, ('expert', 'tensor'), 0, 0, tiled=True, axis_ind...  2.52 us
  transfers between devices with their start and end apart: 7, of which 4 were waited for; matrix products, arithmetic and copies ran while one was open for 3% of the time, Pallas kernels for 0%

profile of v6, /device:TPU:24, one launch (start us, length us, event | category | flops | bytes accessed | tf_op | source)
XLA Modules:
  0.0 113.5 jit_solution(11009855974977222760)
XLA Ops:
  0.0 3.5 %collective-permute-start = (bf16[128,1280]{1,0:T(8,128)(2,1)}, bf16[128,1280]{1,0:T(8,128)(2,1)S(1)}, u32[]{:S(2)}, u32[]{:S(2)}) collective-permute-start(bf16[128,1280]{1,0:T(8,128)(2,1)} %bitcast.137), channel_id=1, source_target_pairs={{0,32},{1,35},{2,34},{3,33},{4,36},{5,39},{6,38},{7,37},{8,40},{9,... | collective-permute-start | bytes 983048 | tf_op jit(solution)/shard_map/ppermute | solution.py:19
  3.6 0.7 fusion.80
  4.3 7.4 %all-gather.3 = s32[2,6,128]{2,1,0:T(8,128)S(1)} all-gather(s32[1,6,128]{2,1,0:T(8,128)S(1)} %get-tuple-element.50), channel_id=2, replica_groups={{0,2},{4,6},{8,10},{12,14},{16,18},{20,22},{24,26},{28,30},{1,3},{5,7},..., dimensions={0}, use_global_device_ids=true | all-gather | bytes 9216 | tf_op jit(solution)/shard_map/all_gather | solution.py:103
  11.7 0.1 eq.142
  11.8 0.1 convert_reduce_fusion
  11.8 0.1 fusion.52
  12.0 0.1 fusion.59
  12.0 0.0 copy-done
  12.1 0.0 copy-start.1
  12.1 0.1 dynamic-slice_bitcast_fusion
  12.2 1.4 %collective-permute-done = bf16[128,1280]{1,0:T(8,128)(2,1)S(1)} collective-permute-done((bf16[128,1280]{1,0:T(8,128)(2,1)}, bf16[128,1280]{1,0:T(8,128)(2,1)S(1)}, u32[]{:S(2)}, u32[]{:S(2)}) %collective-permute-start) | collective-permute-done | bytes 327712 | tf_op jit(solution)/shard_map/ppermute | solution.py:19
  13.5 1.0 fusion.3
  14.5 11.6 %all-to-all-start = ((bf16[16,8,1280]{2,1,0:T(8,128)(2,1)}), bf16[16,8,1280]{2,1,0:T(8,128)(2,1)S(1)}, u32[]{:S(2)}, u32[]{:S(2)}) async-start(bf16[16,8,1280]{2,1,0:T(8,128)(2,1)} %fusion.3), calls=%async_computation | async-start | bytes 655360 | tf_op jit(solution)/shard_map/all_to_all | solution.py:117
  26.1 1.9 %collective-permute-start.1 = (bf16[256,1280]{1,0:T(8,128)(2,1)S(1)}, bf16[256,1280]{1,0:T(8,128)(2,1)S(1)}, u32[]{:S(2)}, u32[]{:S(2)}) collective-permute-start(bf16[256,1280]{1,0:T(8,128)(2,1)S(1)} %dynamic-slice_bitcast_fusion), channel_id=1, source_target_pairs={{0,1},{1,0},{2,3},{3,2},{4,5},{5,4},{6,7},{7,6},{8,9},{9,8},{10,11... | collective-permute-start | bytes 1966088 | tf_op jit(solution)/shard_map/ppermute | solution.py:122
  28.1 5.9 %collective-permute-start.2 = (bf16[128,1280]{1,0:T(8,128)(2,1)}, bf16[128,1280]{1,0:T(8,128)(2,1)S(1)}, u32[]{:S(2)}, u32[]{:S(2)}) collective-permute-start(bf16[128,1280]{1,0:T(8,128)(2,1)} %bitcast.138), channel_id=1, source_target_pairs={{0,64},{1,65},{2,66},{3,67},{4,68},{5,69},{6,70},{7,71},{8,72},{9,... | collective-permute-start | bytes 983048 | tf_op jit(solution)/shard_map/ppermute | solution.py:19
  34.0 1.9 %collective-permute-start.3 = (f32[12,128]{1,0:T(8,128)S(1)}, f32[12,128]{1,0:T(8,128)S(1)}, u32[]{:S(2)}, u32[]{:S(2)}) collective-permute-start(f32[12,128]{1,0:T(8,128)S(1)} %pad_maximum_fusion.2), channel_id=1, source_target_pairs={{0,32},{1,33},{2,34},{3,35},{4,36},{5,37},{6,38},{7,39},{8,40},{9,... | collective-permute-start | bytes 18440 | tf_op jit(solution)/shard_map/ppermute | solution.py:19
  36.0 2.5 %all-to-all-done = bf16[16,8,1280]{2,1,0:T(8,128)(2,1)S(1)} async-done(((bf16[16,8,1280]{2,1,0:T(8,128)(2,1)}), bf16[16,8,1280]{2,1,0:T(8,128)(2,1)S(1)}, u32[]{:S(2)}, u32[]{:S(2)}) %all-to-all-start) | async-done | bytes 327712 | tf_op jit(solution)/shard_map/all_to_all | solution.py:117
  38.5 2.4 %all_gather.26 = bf16[128,2560]{1,0:T(8,128)(2,1)S(1)} all-gather(bf16[128,1280]{1,0:T(8,128)(2,1)S(1)} %bitcast.128), channel_id=1, replica_groups=mesh['section'=16,'expert'=16,'tensor'=2] {'tensor'}, dimensions={1}, use_global_device_ids=true | all-gather | bytes 983040 | tf_op jit(solution)/shard_map/all_gather | solution.py:76
  40.9 0.2 fusion.7
  41.1 0.0 copy-start.4
  41.2 0.4 fusion.19
  41.6 0.9 copy-done.4
  42.5 0.4 fusion.30
  42.9 1.9 %all-gather.1 = bf16[256,256]{1,0:T(8,128)(2,1)S(1)} all-gather(bf16[128,256]{1,0:T(8,128)(2,1)S(1)} %fusion.30), channel_id=3, replica_groups=mesh['section'=16,'expert'=16,'tensor'=2] {'tensor'}, dimensions={0}, use_global_device_ids=true | all-gather | bytes 196608 | tf_op jit(solution)/shard_map/all_gather | solution.py:83
  44.8 0.2 fusion.35
  45.0 0.3 fusion
  45.4 3.4 %collective-permute-start.5 = (bf16[8,8,1280]{2,1,0:T(8,128)(2,1)S(1)}, bf16[8,8,1280]{2,1,0:T(8,128)(2,1)S(1)}, u32[]{:S(2)}, u32[]{:S(2)}) collective-permute-start(bf16[8,8,1280]{2,1,0:T(8,128)(2,1)S(1)} %get-tuple-element.29), channel_id=1, source_target_pairs={{0,34},{1,35},{2,32},{3,33},{4,38},{5,39},{6,36},{7,37},{8,42},{9,... | collective-permute-start | bytes 491528 | tf_op jit(solution)/shard_map/ppermute | solution.py:19
  48.8 5.4 %collective-permute-start.4 = (bf16[8,8,1280]{2,1,0:T(8,128)(2,1)S(1)}, bf16[8,8,1280]{2,1,0:T(8,128)(2,1)S(1)}, u32[]{:S(2)}, u32[]{:S(2)}) collective-permute-start(bf16[8,8,1280]{2,1,0:T(8,128)(2,1)S(1)} %get-tuple-element.28), channel_id=1, source_target_pairs={{0,32},{1,33},{2,34},{3,35},{4,36},{5,37},{6,38},{7,39},{8,40},{9,... | collective-permute-start | bytes 491528 | tf_op jit(solution)/shard_map/ppermute | solution.py:19
  54.2 0.1 fusion.63
  54.3 0.1 fusion.50
  54.4 0.1 fusion.51
  54.6 0.1 fusion.56
  54.7 0.1 fusion.57
  54.8 1.7 %collective-permute-done.5 = bf16[8,8,1280]{2,1,0:T(8,128)(2,1)S(1)} collective-permute-done((bf16[8,8,1280]{2,1,0:T(8,128)(2,1)S(1)}, bf16[8,8,1280]{2,1,0:T(8,128)(2,1)S(1)}, u32[]{:S(2)}, u32[]{:S(2)}) %collective-permute-start.5) | collective-permute-done | bytes 163872 | tf_op jit(solution)/shard_map/ppermute | solution.py:19
  56.4 1.3 %collective-permute-done.4 = bf16[8,8,1280]{2,1,0:T(8,128)(2,1)S(1)} collective-permute-done((bf16[8,8,1280]{2,1,0:T(8,128)(2,1)S(1)}, bf16[8,8,1280]{2,1,0:T(8,128)(2,1)S(1)}, u32[]{:S(2)}, u32[]{:S(2)}) %collective-permute-start.4) | collective-permute-done | bytes 163872 | tf_op jit(solution)/shard_map/ppermute | solution.py:19
  57.7 13.9 %all_to_all.20 = bf16[8,8,1280]{2,1,0:T(8,128)(2,1)S(1)} all-to-all(bf16[8,8,1280]{2,1,0:T(8,128)(2,1)S(1)} %add_convert_fusion.1), channel_id=1, replica_groups={{0,24,16,8,4,12,20,28},{2,26,18,10,6,14,22,30},{1,25,17,9,5,13,21,29},{..., dimensions={0} | all-to-all | bytes 327680 | tf_op jit(solution)/shard_map/all_to_all | solution.py:73
  71.7 0.3 add_convert_fusion
  71.9 0.2 fusion.4
  72.2 17.5 %all_to_all.21 = bf16[16,8,1280]{2,1,0:T(8,128)(2,1)S(1)} all-to-all(bf16[16,8,1280]{2,1,0:T(8,128)(2,1)S(1)} %fusion.4), channel_id=1, replica_groups={{0,24,16,8,4,12,20,28,2,26,18,10,6,14,22,30},{1,25,17,9,5,13,21,29,3,27..., dimensions={0} | all-to-all | bytes 655360 | tf_op jit(solution)/shard_map/all_to_all | solution.py:73
  89.6 2.3 %all_gather.29 = bf16[128,2560]{1,0:T(8,128)(2,1)S(1)} all-gather(bf16[128,1280]{1,0:T(8,128)(2,1)S(1)} %bitcast.130), channel_id=1, replica_groups=mesh['section'=16,'expert'=16,'tensor'=2] {'tensor'}, dimensions={1}, use_global_device_ids=true | all-gather | bytes 983040 | tf_op jit(solution)/shard_map/all_gather | solution.py:76
  91.9 0.2 fusion.10
  92.1 0.4 fusion.17
  92.5 0.4 fusion.27
  92.9 1.9 %all-gather.2 = bf16[256,256]{1,0:T(8,128)(2,1)S(1)} all-gather(bf16[128,256]{1,0:T(8,128)(2,1)S(1)} %fusion.27), channel_id=4, replica_groups=mesh['section'=16,'expert'=16,'tensor'=2] {'tensor'}, dimensions={0}, use_global_device_ids=true | all-gather | bytes 196608 | tf_op jit(solution)/shard_map/all_gather | solution.py:83
  94.8 0.2 fusion.33
  95.1 0.3 fusion.6
  95.3 17.1 %all_to_all.22 = bf16[16,8,1280]{2,1,0:T(8,128)(2,1)S(1)} all-to-all(bf16[16,8,1280]{2,1,0:T(8,128)(2,1)S(1)} %fusion.6), channel_id=1, replica_groups={{0,24,16,8,4,12,20,28,2,26,18,10,6,14,22,30},{1,25,17,9,5,13,21,29,3,27..., dimensions={0} | all-to-all | bytes 655360 | tf_op jit(solution)/shard_map/all_to_all | solution.py:73
  112.4 1.0 fusion.5
  (27 shorter events, 0.2 us)
Async XLA Ops:
  0.0 12.1 %copy-start = (bf16[1,256,2560]{2,1,0:T(8,128)(2,1)S(1)}, bf16[1,256,2560]{2,1,0:T(8,128)(2,1)}, u32[]{:S(2)}) copy-start(bf16[1,256,2560]{2,1,0:T(8,128)(2,1)} %param.11) | copy-start | bytes 3932164
  0.0 13.5 %collective-permute-start = (bf16[128,1280]{1,0:T(8,128)(2,1)}, bf16[128,1280]{1,0:T(8,128)(2,1)S(1)}, u32[]{:S(2)}, u32[]{:S(2)}) collective-permute-start(bf16[128,1280]{1,0:T(8,128)(2,1)} %bitcast.137), channel_id=1, source_target_pairs={{0,32},{1,35},{2,34},{3,33},{4,36},{5,39},{6,38},{7,37},{8,40},{9,... | collective-permute-start | bytes 983048 | tf_op jit(solution)/shard_map/ppermute | solution.py:19
  12.1 14.0 %copy-start.1 = (f32[2,1,128,6]{2,1,3,0:T(1,128)S(1)}, f32[2,1,128,6]{2,1,3,0:T(1,128)}, u32[]{:S(2)}) copy-start(f32[2,1,128,6]{2,1,3,0:T(1,128)} %param.13) | copy-start | bytes 18436
  12.1 23.9 %slice-start = ((f32[2,1,128,6]{2,1,3,0:T(1,128)}), f32[1,1,128,6]{2,1,3,0:T(1,128)S(1)}, s32[]{:S(2)}) async-start(f32[2,1,128,6]{2,1,3,0:T(1,128)} %param.13), calls=%async_computation.4 | async-start | bytes 6144 | tf_op jit(solution)/shard_map/slice | solution.py:128
  12.1 23.9 %copy-start.2 = (bf16[1,2560]{1,0:T(2,128)(2,1)S(1)}, bf16[1,2560]{1,0:T(2,128)(2,1)}, u32[]{:S(2)}) copy-start(bf16[1,2560]{1,0:T(2,128)(2,1)} %param.8) | copy-start | bytes 15364
  14.5 24.0 %all-to-all-start = ((bf16[16,8,1280]{2,1,0:T(8,128)(2,1)}), bf16[16,8,1280]{2,1,0:T(8,128)(2,1)S(1)}, u32[]{:S(2)}, u32[]{:S(2)}) async-start(bf16[16,8,1280]{2,1,0:T(8,128)(2,1)} %fusion.3), calls=%async_computation | async-start | bytes 655360 | tf_op jit(solution)/shard_map/all_to_all | solution.py:117
  26.1 18.9 %collective-permute-start.1 = (bf16[256,1280]{1,0:T(8,128)(2,1)S(1)}, bf16[256,1280]{1,0:T(8,128)(2,1)S(1)}, u32[]{:S(2)}, u32[]{:S(2)}) collective-permute-start(bf16[256,1280]{1,0:T(8,128)(2,1)S(1)} %dynamic-slice_bitcast_fusion), channel_id=1, source_target_pairs={{0,1},{1,0},{2,3},{3,2},{4,5},{5,4},{6,7},{7,6},{8,9},{9,8},{10,11... | collective-permute-start | bytes 1966088 | tf_op jit(solution)/shard_map/ppermute | solution.py:122
  28.1 17.3 %collective-permute-start.2 = (bf16[128,1280]{1,0:T(8,128)(2,1)}, bf16[128,1280]{1,0:T(8,128)(2,1)S(1)}, u32[]{:S(2)}, u32[]{:S(2)}) collective-permute-start(bf16[128,1280]{1,0:T(8,128)(2,1)} %bitcast.138), channel_id=1, source_target_pairs={{0,64},{1,65},{2,66},{3,67},{4,68},{5,69},{6,70},{7,71},{8,72},{9,... | collective-permute-start | bytes 983048 | tf_op jit(solution)/shard_map/ppermute | solution.py:19
  34.0 11.3 %collective-permute-start.3 = (f32[12,128]{1,0:T(8,128)S(1)}, f32[12,128]{1,0:T(8,128)S(1)}, u32[]{:S(2)}, u32[]{:S(2)}) collective-permute-start(f32[12,128]{1,0:T(8,128)S(1)} %pad_maximum_fusion.2), channel_id=1, source_target_pairs={{0,32},{1,33},{2,34},{3,35},{4,36},{5,37},{6,38},{7,39},{8,40},{9,... | collective-permute-start | bytes 18440 | tf_op jit(solution)/shard_map/ppermute | solution.py:19
  38.5 2.6 %copy-start.3 = (bf16[1,2560,256]{2,1,0:T(8,128)(2,1)S(1)}, bf16[1,2560,256]{2,1,0:T(8,128)(2,1)}, u32[]{:S(2)}) copy-start(bf16[1,2560,256]{2,1,0:T(8,128)(2,1)} %param.9) | copy-start | bytes 3932164
  41.1 1.3 %copy-start.4 = (bf16[1,2560,256]{2,1,0:T(8,128)(2,1)S(1)}, bf16[1,2560,256]{2,1,0:T(8,128)(2,1)}, u32[]{:S(2)}) copy-start(bf16[1,2560,256]{2,1,0:T(8,128)(2,1)} %param.10) | copy-start | bytes 3932164
  45.4 11.0 %collective-permute-start.5 = (bf16[8,8,1280]{2,1,0:T(8,128)(2,1)S(1)}, bf16[8,8,1280]{2,1,0:T(8,128)(2,1)S(1)}, u32[]{:S(2)}, u32[]{:S(2)}) collective-permute-start(bf16[8,8,1280]{2,1,0:T(8,128)(2,1)S(1)} %get-tuple-element.29), channel_id=1, source_target_pairs={{0,34},{1,35},{2,32},{3,33},{4,38},{5,39},{6,36},{7,37},{8,42},{9,... | collective-permute-start | bytes 491528 | tf_op jit(solution)/shard_map/ppermute | solution.py:19
  48.8 8.9 %collective-permute-start.4 = (bf16[8,8,1280]{2,1,0:T(8,128)(2,1)S(1)}, bf16[8,8,1280]{2,1,0:T(8,128)(2,1)S(1)}, u32[]{:S(2)}, u32[]{:S(2)}) collective-permute-start(bf16[8,8,1280]{2,1,0:T(8,128)(2,1)S(1)} %get-tuple-element.28), channel_id=1, source_target_pairs={{0,32},{1,33},{2,34},{3,35},{4,36},{5,37},{6,38},{7,39},{8,40},{9,... | collective-permute-start | bytes 491528 | tf_op jit(solution)/shard_map/ppermute | solution.py:19

commit v7 on v6

--- a/solution.py
+++ b/solution.py
@@ -97,19 +97,18 @@
         moe_sum = lax.dot_general(table, rows, dims, preferred_element_type=jnp.float32)
         return (tokens.astype(jnp.float32) + moe_sum).astype(jnp.bfloat16)
 
-    ids = route_ids[0, 0].T
     shifted = send(start, 1, (0, 1))
     pairs = [[2 * z, 2 * z + 1] for z in range(window)]
-    both_ids = lax.all_gather(ids, "expert", axis_index_groups=pairs)
-    ids_here = jnp.where(side == core, both_ids[0], both_ids[1])
+    both_ids = lax.all_gather(route_ids, "expert", axis_index_groups=pairs)
+    ids_here = jnp.where(side == core, both_ids[0, 0, 0].T, both_ids[1, 0, 0].T)
     outgoing = slot_rows(shifted, doubled(dispatch_rows(ids_here, window, capacity)))
     down_sent = lax.dynamic_slice_in_dim(w_down[0], (1 - core) * half_width, half_width, 1)
-    outgoing, start, gates, down_sent, down_all, gain = lax.optimization_barrier(
-        (outgoing, start, route_weights, down_sent, w_down[0], norm_gain)
+    outgoing, start, ids, gates, down_sent, down_all, gain = lax.optimization_barrier(
+        (outgoing, start, route_ids, route_weights, down_sent, w_down[0], norm_gain)
     )
     gain_row = gain.astype(jnp.float32)
     down_own = lax.dynamic_slice_in_dim(down_all, core * half_width, half_width, 1)
-    routes = jnp.concatenate([ids.astype(jnp.float32), gates[0, 0].T], axis=0)
+    routes = jnp.concatenate([ids[0, 0].T.astype(jnp.float32), gates[0, 0].T], axis=0)
     orders = [
         [2 * e for e in same_side[0] + same_side[1]],
         [2 * e + 1 for e in same_side[1] + same_side[0]],
@@ -125,7 +124,7 @@
     straight = lax.dynamic_index_in_dim(by_side, side, 0, keepdims=False)
     crossed = lax.dynamic_index_in_dim(by_side, 1 - side, 0, keepdims=False)
     straight, crossed, residual, routes_on, ids, gates = lax.optimization_barrier(
-        (straight, crossed, residual, routes_on, route_ids[1, 0], gates[1, 0])
+        (straight, crossed, residual, routes_on, ids[1, 0], gates[1, 0])
     )
     halves = send(straight, 1).astype(jnp.float32) + send(crossed, 1, (1, 1)).astype(jnp.float32)
     dispatch_1 = doubled(dispatch_rows(ids.T, window, capacity))

time: 114 us -> 114 us (level)
  transfers between devices with their start and end apart: 7 -> 7, of which waited for: 4 -> 4; matrix products, arithmetic and copies ran while one was open for 3% -> 2% of each run, Pallas kernels for 0% -> 0%
where the time goes in v7:
time: 114 us; the launch traced here: 113 us
  blocking collectives  65.1 us (57%)
  starting transfers between devices  33.7 us (30%)
  waiting for transfers between devices  6.79 us (6%)
  matrix products  5.48 us (5%)
    all_to_all x3, blocking collectives, exchange(): lax.all_to_all(chunks, 'expert', 0, 0, tiled=True, axis_index_groups=groups)  48.5 us
    ppermute x5, starting transfers between devices, send(): return lax.ppermute(array, ('section', 'expert', 'tensor'), pairs)  20.2 us
    all_to_all x1, starting transfers between devices, local(): lax.all_to_all(outgoing, ('expert', 'tensor'), 0, 0, tiled=True, axis_ind...  11.6 us
    all_gather x1, blocking collectives, local(): both_ids = lax.all_gather(route_ids, 'expert', axis_index_groups=pairs)  8.16 us
    all_gather x2, blocking collectives, experts(): lax.all_gather(arrived.reshape(slots, half_width), 'tensor', axis=1, tile...  4.66 us
    ppermute x5, waiting for transfers between devices, send(): return lax.ppermute(array, ('section', 'expert', 'tensor'), pairs)  4.25 us
    all_gather x2, blocking collectives, experts(): hidden = lax.all_gather(hidden, 'tensor', axis=0, tiled=False)  3.8 us
    all_to_all x1, waiting for transfers between devices, local(): lax.all_to_all(outgoing, ('expert', 'tensor'), 0, 0, tiled=True, axis_ind...  2.53 us
  transfers between devices with their start and end apart: 7, of which 4 were waited for; matrix products, arithmetic and copies ran while one was open for 2% of the time, Pallas kernels for 0%

profile of v7, /device:TPU:24, one launch (start us, length us, event | category | flops | bytes accessed | tf_op | source)
XLA Modules:
  0.0 113.4 jit_solution(17325069610247626313)
XLA Ops:
  0.0 3.5 %collective-permute-start = (bf16[128,1280]{1,0:T(8,128)(2,1)}, bf16[128,1280]{1,0:T(8,128)(2,1)S(1)}, u32[]{:S(2)}, u32[]{:S(2)}) collective-permute-start(bf16[128,1280]{1,0:T(8,128)(2,1)} %bitcast.140), channel_id=1, source_target_pairs={{0,32},{1,35},{2,34},{3,33},{4,36},{5,39},{6,38},{7,37},{8,40},{9,... | collective-permute-start | bytes 983048 | tf_op jit(solution)/shard_map/ppermute | solution.py:19
  3.6 8.2 %all-gather = s32[4,1,128,6]{2,1,3,0:T(1,128)S(1)} all-gather(s32[2,1,128,6]{2,1,3,0:T(1,128)} %param.12), channel_id=2, replica_groups={{0,2},{4,6},{8,10},{12,14},{16,18},{20,22},{24,26},{28,30},{1,3},{5,7},..., dimensions={0}, use_global_device_ids=true | all-gather | bytes 18432 | tf_op jit(solution)/shard_map/all_gather | solution.py:102
  11.7 0.1 eq.142
  11.8 0.1 convert_reduce_fusion
  11.9 0.1 fusion.52
  12.0 0.1 fusion.59
  12.1 0.0 copy-done
  12.1 0.0 slice-start
  12.2 0.0 copy-start.2
  12.2 0.1 dynamic-slice_bitcast_fusion
  12.2 1.3 %collective-permute-done = bf16[128,1280]{1,0:T(8,128)(2,1)S(1)} collective-permute-done((bf16[128,1280]{1,0:T(8,128)(2,1)}, bf16[128,1280]{1,0:T(8,128)(2,1)S(1)}, u32[]{:S(2)}, u32[]{:S(2)}) %collective-permute-start) | collective-permute-done | bytes 327712 | tf_op jit(solution)/shard_map/ppermute | solution.py:19
  13.5 1.0 fusion.3
  14.5 11.6 %all-to-all-start = ((bf16[16,8,1280]{2,1,0:T(8,128)(2,1)}), bf16[16,8,1280]{2,1,0:T(8,128)(2,1)S(1)}, u32[]{:S(2)}, u32[]{:S(2)}) async-start(bf16[16,8,1280]{2,1,0:T(8,128)(2,1)} %fusion.3), calls=%async_computation | async-start | bytes 655360 | tf_op jit(solution)/shard_map/all_to_all | solution.py:116
  26.1 1.9 %collective-permute-start.1 = (bf16[256,1280]{1,0:T(8,128)(2,1)S(1)}, bf16[256,1280]{1,0:T(8,128)(2,1)S(1)}, u32[]{:S(2)}, u32[]{:S(2)}) collective-permute-start(bf16[256,1280]{1,0:T(8,128)(2,1)S(1)} %dynamic-slice_bitcast_fusion), channel_id=1, source_target_pairs={{0,1},{1,0},{2,3},{3,2},{4,5},{5,4},{6,7},{7,6},{8,9},{9,8},{10,11... | collective-permute-start | bytes 1966088 | tf_op jit(solution)/shard_map/ppermute | solution.py:121
  28.0 5.9 %collective-permute-start.2 = (bf16[128,1280]{1,0:T(8,128)(2,1)}, bf16[128,1280]{1,0:T(8,128)(2,1)S(1)}, u32[]{:S(2)}, u32[]{:S(2)}) collective-permute-start(bf16[128,1280]{1,0:T(8,128)(2,1)} %bitcast.141), channel_id=1, source_target_pairs={{0,64},{1,65},{2,66},{3,67},{4,68},{5,69},{6,70},{7,71},{8,72},{9,... | collective-permute-start | bytes 983048 | tf_op jit(solution)/shard_map/ppermute | solution.py:19
  34.0 1.9 %collective-permute-start.3 = (f32[12,128]{1,0:T(8,128)S(1)}, f32[12,128]{1,0:T(8,128)S(1)}, u32[]{:S(2)}, u32[]{:S(2)}) collective-permute-start(f32[12,128]{1,0:T(8,128)S(1)} %pad_maximum_fusion.2), channel_id=1, source_target_pairs={{0,32},{1,33},{2,34},{3,35},{4,36},{5,37},{6,38},{7,39},{8,40},{9,... | collective-permute-start | bytes 18440 | tf_op jit(solution)/shard_map/ppermute | solution.py:19
  36.0 2.5 %all-to-all-done = bf16[16,8,1280]{2,1,0:T(8,128)(2,1)S(1)} async-done(((bf16[16,8,1280]{2,1,0:T(8,128)(2,1)}), bf16[16,8,1280]{2,1,0:T(8,128)(2,1)S(1)}, u32[]{:S(2)}, u32[]{:S(2)}) %all-to-all-start) | async-done | bytes 327712 | tf_op jit(solution)/shard_map/all_to_all | solution.py:116
  38.5 2.4 %all_gather.26 = bf16[128,2560]{1,0:T(8,128)(2,1)S(1)} all-gather(bf16[128,1280]{1,0:T(8,128)(2,1)S(1)} %bitcast.128), channel_id=1, replica_groups=mesh['section'=16,'expert'=16,'tensor'=2] {'tensor'}, dimensions={1}, use_global_device_ids=true | all-gather | bytes 983040 | tf_op jit(solution)/shard_map/all_gather | solution.py:76
  40.9 0.2 fusion.7
  41.2 0.0 copy-start.5
  41.2 0.4 fusion.19
  41.6 0.9 copy-done.5
  42.5 0.4 fusion.30
  42.9 1.9 %all-gather.1 = bf16[256,256]{1,0:T(8,128)(2,1)S(1)} all-gather(bf16[128,256]{1,0:T(8,128)(2,1)S(1)} %fusion.30), channel_id=3, replica_groups=mesh['section'=16,'expert'=16,'tensor'=2] {'tensor'}, dimensions={0}, use_global_device_ids=true | all-gather | bytes 196608 | tf_op jit(solution)/shard_map/all_gather | solution.py:83
  44.8 0.2 fusion.35
  45.1 0.3 fusion
  45.4 3.3 %collective-permute-start.5 = (bf16[8,8,1280]{2,1,0:T(8,128)(2,1)S(1)}, bf16[8,8,1280]{2,1,0:T(8,128)(2,1)S(1)}, u32[]{:S(2)}, u32[]{:S(2)}) collective-permute-start(bf16[8,8,1280]{2,1,0:T(8,128)(2,1)S(1)} %get-tuple-element.31), channel_id=1, source_target_pairs={{0,34},{1,35},{2,32},{3,33},{4,38},{5,39},{6,36},{7,37},{8,42},{9,... | collective-permute-start | bytes 491528 | tf_op jit(solution)/shard_map/ppermute | solution.py:19
  48.7 5.5 %collective-permute-start.4 = (bf16[8,8,1280]{2,1,0:T(8,128)(2,1)S(1)}, bf16[8,8,1280]{2,1,0:T(8,128)(2,1)S(1)}, u32[]{:S(2)}, u32[]{:S(2)}) collective-permute-start(bf16[8,8,1280]{2,1,0:T(8,128)(2,1)S(1)} %get-tuple-element.30), channel_id=1, source_target_pairs={{0,32},{1,33},{2,34},{3,35},{4,36},{5,37},{6,38},{7,39},{8,40},{9,... | collective-permute-start | bytes 491528 | tf_op jit(solution)/shard_map/ppermute | solution.py:19
  54.2 0.1 fusion.63
  54.3 0.1 fusion.50
  54.4 0.1 fusion.51
  54.6 0.1 fusion.56
  54.7 0.1 fusion.57
  54.8 1.7 %collective-permute-done.5 = bf16[8,8,1280]{2,1,0:T(8,128)(2,1)S(1)} collective-permute-done((bf16[8,8,1280]{2,1,0:T(8,128)(2,1)S(1)}, bf16[8,8,1280]{2,1,0:T(8,128)(2,1)S(1)}, u32[]{:S(2)}, u32[]{:S(2)}) %collective-permute-start.5) | collective-permute-done | bytes 163872 | tf_op jit(solution)/shard_map/ppermute | solution.py:19
  56.4 1.3 %collective-permute-done.4 = bf16[8,8,1280]{2,1,0:T(8,128)(2,1)S(1)} collective-permute-done((bf16[8,8,1280]{2,1,0:T(8,128)(2,1)S(1)}, bf16[8,8,1280]{2,1,0:T(8,128)(2,1)S(1)}, u32[]{:S(2)}, u32[]{:S(2)}) %collective-permute-start.4) | collective-permute-done | bytes 163872 | tf_op jit(solution)/shard_map/ppermute | solution.py:19
  57.7 13.9 %all_to_all.20 = bf16[8,8,1280]{2,1,0:T(8,128)(2,1)S(1)} all-to-all(bf16[8,8,1280]{2,1,0:T(8,128)(2,1)S(1)} %add_convert_fusion.1), channel_id=1, replica_groups={{0,24,16,8,4,12,20,28},{2,26,18,10,6,14,22,30},{1,25,17,9,5,13,21,29},{..., dimensions={0} | all-to-all | bytes 327680 | tf_op jit(solution)/shard_map/all_to_all | solution.py:73
  71.7 0.3 add_convert_fusion
  71.9 0.2 fusion.4
  72.2 17.4 %all_to_all.21 = bf16[16,8,1280]{2,1,0:T(8,128)(2,1)S(1)} all-to-all(bf16[16,8,1280]{2,1,0:T(8,128)(2,1)S(1)} %fusion.4), channel_id=1, replica_groups={{0,24,16,8,4,12,20,28,2,26,18,10,6,14,22,30},{1,25,17,9,5,13,21,29,3,27..., dimensions={0} | all-to-all | bytes 655360 | tf_op jit(solution)/shard_map/all_to_all | solution.py:73
  89.6 2.3 %all_gather.29 = bf16[128,2560]{1,0:T(8,128)(2,1)S(1)} all-gather(bf16[128,1280]{1,0:T(8,128)(2,1)S(1)} %bitcast.130), channel_id=1, replica_groups=mesh['section'=16,'expert'=16,'tensor'=2] {'tensor'}, dimensions={1}, use_global_device_ids=true | all-gather | bytes 983040 | tf_op jit(solution)/shard_map/all_gather | solution.py:76
  91.9 0.2 fusion.10
  92.1 0.4 fusion.17
  92.5 0.4 fusion.27
  92.9 1.9 %all-gather.2 = bf16[256,256]{1,0:T(8,128)(2,1)S(1)} all-gather(bf16[128,256]{1,0:T(8,128)(2,1)S(1)} %fusion.27), channel_id=4, replica_groups=mesh['section'=16,'expert'=16,'tensor'=2] {'tensor'}, dimensions={0}, use_global_device_ids=true | all-gather | bytes 196608 | tf_op jit(solution)/shard_map/all_gather | solution.py:83
  94.8 0.2 fusion.33
  95.1 0.3 fusion.6
  95.3 17.1 %all_to_all.22 = bf16[16,8,1280]{2,1,0:T(8,128)(2,1)S(1)} all-to-all(bf16[16,8,1280]{2,1,0:T(8,128)(2,1)S(1)} %fusion.6), channel_id=1, replica_groups={{0,24,16,8,4,12,20,28,2,26,18,10,6,14,22,30},{1,25,17,9,5,13,21,29,3,27..., dimensions={0} | all-to-all | bytes 655360 | tf_op jit(solution)/shard_map/all_to_all | solution.py:73
  112.4 1.0 fusion.5
  (30 shorter events, 0.2 us)
Async XLA Ops:
  0.0 12.1 %copy-start = (bf16[1,256,2560]{2,1,0:T(8,128)(2,1)S(1)}, bf16[1,256,2560]{2,1,0:T(8,128)(2,1)}, u32[]{:S(2)}) copy-start(bf16[1,256,2560]{2,1,0:T(8,128)(2,1)} %param.11) | copy-start | bytes 3932164
  0.0 14.5 %copy-start.1 = (s32[2,1,128,6]{2,1,3,0:T(1,128)S(1)}, s32[2,1,128,6]{2,1,3,0:T(1,128)}, u32[]{:S(2)}) copy-start(s32[2,1,128,6]{2,1,3,0:T(1,128)} %param.12) | copy-start | bytes 18436
  0.0 13.5 %collective-permute-start = (bf16[128,1280]{1,0:T(8,128)(2,1)}, bf16[128,1280]{1,0:T(8,128)(2,1)S(1)}, u32[]{:S(2)}, u32[]{:S(2)}) collective-permute-start(bf16[128,1280]{1,0:T(8,128)(2,1)} %bitcast.140), channel_id=1, source_target_pairs={{0,32},{1,35},{2,34},{3,33},{4,36},{5,39},{6,38},{7,37},{8,40},{9,... | collective-permute-start | bytes 983048 | tf_op jit(solution)/shard_map/ppermute | solution.py:19
  12.1 21.8 %copy-start.3 = (f32[2,1,128,6]{2,1,3,0:T(1,128)S(1)}, f32[2,1,128,6]{2,1,3,0:T(1,128)}, u32[]{:S(2)}) copy-start(f32[2,1,128,6]{2,1,3,0:T(1,128)} %param.13) | copy-start | bytes 18436
  12.1 23.8 %slice-start = ((s32[2,1,128,6]{2,1,3,0:T(1,128)}), s32[1,1,128,6]{2,1,3,0:T(1,128)S(1)}, s32[]{:S(2)}) async-start(s32[2,1,128,6]{2,1,3,0:T(1,128)} %param.12), calls=%async_computation.4 | async-start | bytes 6144 | tf_op jit(solution)/shard_map/slice | solution.py:127
  12.2 23.8 %copy-start.2 = (bf16[1,2560]{1,0:T(2,128)(2,1)S(1)}, bf16[1,2560]{1,0:T(2,128)(2,1)}, u32[]{:S(2)}) copy-start(bf16[1,2560]{1,0:T(2,128)(2,1)} %param.8) | copy-start | bytes 15364
  14.5 24.0 %all-to-all-start = ((bf16[16,8,1280]{2,1,0:T(8,128)(2,1)}), bf16[16,8,1280]{2,1,0:T(8,128)(2,1)S(1)}, u32[]{:S(2)}, u32[]{:S(2)}) async-start(bf16[16,8,1280]{2,1,0:T(8,128)(2,1)} %fusion.3), calls=%async_computation | async-start | bytes 655360 | tf_op jit(solution)/shard_map/all_to_all | solution.py:116
  26.1 19.0 %collective-permute-start.1 = (bf16[256,1280]{1,0:T(8,128)(2,1)S(1)}, bf16[256,1280]{1,0:T(8,128)(2,1)S(1)}, u32[]{:S(2)}, u32[]{:S(2)}) collective-permute-start(bf16[256,1280]{1,0:T(8,128)(2,1)S(1)} %dynamic-slice_bitcast_fusion), channel_id=1, source_target_pairs={{0,1},{1,0},{2,3},{3,2},{4,5},{5,4},{6,7},{7,6},{8,9},{9,8},{10,11... | collective-permute-start | bytes 1966088 | tf_op jit(solution)/shard_map/ppermute | solution.py:121
  28.0 17.4 %collective-permute-start.2 = (bf16[128,1280]{1,0:T(8,128)(2,1)}, bf16[128,1280]{1,0:T(8,128)(2,1)S(1)}, u32[]{:S(2)}, u32[]{:S(2)}) collective-permute-start(bf16[128,1280]{1,0:T(8,128)(2,1)} %bitcast.141), channel_id=1, source_target_pairs={{0,64},{1,65},{2,66},{3,67},{4,68},{5,69},{6,70},{7,71},{8,72},{9,... | collective-permute-start | bytes 983048 | tf_op jit(solution)/shard_map/ppermute | solution.py:19
  34.0 11.4 %collective-permute-start.3 = (f32[12,128]{1,0:T(8,128)S(1)}, f32[12,128]{1,0:T(8,128)S(1)}, u32[]{:S(2)}, u32[]{:S(2)}) collective-permute-start(f32[12,128]{1,0:T(8,128)S(1)} %pad_maximum_fusion.2), channel_id=1, source_target_pairs={{0,32},{1,33},{2,34},{3,35},{4,36},{5,37},{6,38},{7,39},{8,40},{9,... | collective-permute-start | bytes 18440 | tf_op jit(solution)/shard_map/ppermute | solution.py:19
  38.5 2.6 %copy-start.4 = (bf16[1,2560,256]{2,1,0:T(8,128)(2,1)S(1)}, bf16[1,2560,256]{2,1,0:T(8,128)(2,1)}, u32[]{:S(2)}) copy-start(bf16[1,2560,256]{2,1,0:T(8,128)(2,1)} %param.9) | copy-start | bytes 3932164
  41.2 1.3 %copy-start.5 = (bf16[1,2560,256]{2,1,0:T(8,128)(2,1)S(1)}, bf16[1,2560,256]{2,1,0:T(8,128)(2,1)}, u32[]{:S(2)}) copy-start(bf16[1,2560,256]{2,1,0:T(8,128)(2,1)} %param.10) | copy-start | bytes 3932164
  45.4 11.0 %collective-permute-start.5 = (bf16[8,8,1280]{2,1,0:T(8,128)(2,1)S(1)}, bf16[8,8,1280]{2,1,0:T(8,128)(2,1)S(1)}, u32[]{:S(2)}, u32[]{:S(2)}) collective-permute-start(bf16[8,8,1280]{2,1,0:T(8,128)(2,1)S(1)} %get-tuple-element.31), channel_id=1, source_target_pairs={{0,34},{1,35},{2,32},{3,33},{4,38},{5,39},{6,36},{7,37},{8,42},{9,... | collective-permute-start | bytes 491528 | tf_op jit(solution)/shard_map/ppermute | solution.py:19
  48.7 9.0 %collective-permute-start.4 = (bf16[8,8,1280]{2,1,0:T(8,128)(2,1)S(1)}, bf16[8,8,1280]{2,1,0:T(8,128)(2,1)S(1)}, u32[]{:S(2)}, u32[]{:S(2)}) collective-permute-start(bf16[8,8,1280]{2,1,0:T(8,128)(2,1)S(1)} %get-tuple-element.30), channel_id=1, source_target_pairs={{0,32},{1,33},{2,34},{3,35},{4,36},{5,37},{6,38},{7,39},{8,40},{9,... | collective-permute-start | bytes 491528 | tf_op jit(solution)/shard_map/ppermute | solution.py:19

commit v8 on v7

--- a/solution.py
+++ b/solution.py
@@ -75,8 +75,8 @@
     def experts(arrived, down_own, down_got):
         rows = lax.all_gather(arrived.reshape(slots, half_width), "tensor", axis=1, tiled=True)
         rows = rows.astype(jnp.float32)
-        rms_scale = jnp.sqrt(jnp.mean(rows * rows, axis=1, keepdims=True) + NORM_EPS)
-        normed = (rows / rms_scale * gain_row).astype(jnp.bfloat16)
+        scale = 1.0 / jnp.sqrt(jnp.mean(rows * rows, axis=1, keepdims=True) + NORM_EPS)
+        normed = (rows * scale * gain_row).astype(jnp.bfloat16)
         gate_act = jnp.dot(normed, w_gate[0], preferred_element_type=jnp.float32)
         up_act = jnp.dot(normed, w_up[0], preferred_element_type=jnp.float32)
         hidden = (jax.nn.silu(gate_act) * up_act).astype(jnp.bfloat16)

time: 114 us -> 114 us (level)
  no operation moved by 1% of the time
where the time goes in v8:
time: 114 us; the launch traced here: 113 us
  blocking collectives  65.1 us (57%)
  starting transfers between devices  33.7 us (30%)
  waiting for transfers between devices  6.79 us (6%)
  matrix products  5.42 us (5%)
    all_to_all x3, blocking collectives, exchange(): lax.all_to_all(chunks, 'expert', 0, 0, tiled=True, axis_index_groups=groups)  48.4 us
    ppermute x5, starting transfers between devices, send(): return lax.ppermute(array, ('section', 'expert', 'tensor'), pairs)  20.2 us
    all_to_all x1, starting transfers between devices, local(): lax.all_to_all(outgoing, ('expert', 'tensor'), 0, 0, tiled=True, axis_ind...  11.6 us
    all_gather x1, blocking collectives, local(): both_ids = lax.all_gather(route_ids, 'expert', axis_index_groups=pairs)  8.16 us
    all_gather x2, blocking collectives, experts(): lax.all_gather(arrived.reshape(slots, half_width), 'tensor', axis=1, tile...  4.66 us
    ppermute x5, waiting for transfers between devices, send(): return lax.ppermute(array, ('section', 'expert', 'tensor'), pairs)  4.25 us
    all_gather x2, blocking collectives, experts(): hidden = lax.all_gather(hidden, 'tensor', axis=0, tiled=False)  3.8 us
    all_to_all x1, waiting for transfers between devices, local(): lax.all_to_all(outgoing, ('expert', 'tensor'), 0, 0, tiled=True, axis_ind...  2.53 us
  transfers between devices with their start and end apart: 7, of which 4 were waited for; matrix products, arithmetic and copies ran while one was open for 2% of the time, Pallas kernels for 0%

profile of v8, /device:TPU:24, one launch (start us, length us, event | category | flops | bytes accessed | tf_op | source)
XLA Modules:
  0.0 113.4 jit_solution(4252764781972886041)
XLA Ops:
  0.0 3.5 %collective-permute-start = (bf16[128,1280]{1,0:T(8,128)(2,1)}, bf16[128,1280]{1,0:T(8,128)(2,1)S(1)}, u32[]{:S(2)}, u32[]{:S(2)}) collective-permute-start(bf16[128,1280]{1,0:T(8,128)(2,1)} %bitcast.140), channel_id=1, source_target_pairs={{0,32},{1,35},{2,34},{3,33},{4,36},{5,39},{6,38},{7,37},{8,40},{9,... | collective-permute-start | bytes 983048 | tf_op jit(solution)/shard_map/ppermute | solution.py:19
  3.6 8.2 %all-gather = s32[4,1,128,6]{2,1,3,0:T(1,128)S(1)} all-gather(s32[2,1,128,6]{2,1,3,0:T(1,128)} %param.12), channel_id=2, replica_groups={{0,2},{4,6},{8,10},{12,14},{16,18},{20,22},{24,26},{28,30},{1,3},{5,7},..., dimensions={0}, use_global_device_ids=true | all-gather | bytes 18432 | tf_op jit(solution)/shard_map/all_gather | solution.py:102
  11.7 0.1 eq.142
  11.8 0.1 convert_reduce_fusion
  11.9 0.1 fusion.56
  12.0 0.1 fusion.63
  12.1 0.0 copy-done
  12.1 0.0 copy-start.3
  12.1 0.0 slice-start
  12.2 0.0 copy-start.2
  12.2 0.1 dynamic-slice_bitcast_fusion
  12.2 1.3 %collective-permute-done = bf16[128,1280]{1,0:T(8,128)(2,1)S(1)} collective-permute-done((bf16[128,1280]{1,0:T(8,128)(2,1)}, bf16[128,1280]{1,0:T(8,128)(2,1)S(1)}, u32[]{:S(2)}, u32[]{:S(2)}) %collective-permute-start) | collective-permute-done | bytes 327712 | tf_op jit(solution)/shard_map/ppermute | solution.py:19
  13.5 1.0 fusion.3
  14.5 11.6 %all-to-all-start = ((bf16[16,8,1280]{2,1,0:T(8,128)(2,1)}), bf16[16,8,1280]{2,1,0:T(8,128)(2,1)S(1)}, u32[]{:S(2)}, u32[]{:S(2)}) async-start(bf16[16,8,1280]{2,1,0:T(8,128)(2,1)} %fusion.3), calls=%async_computation | async-start | bytes 655360 | tf_op jit(solution)/shard_map/all_to_all | solution.py:116
  26.1 1.9 %collective-permute-start.1 = (bf16[256,1280]{1,0:T(8,128)(2,1)S(1)}, bf16[256,1280]{1,0:T(8,128)(2,1)S(1)}, u32[]{:S(2)}, u32[]{:S(2)}) collective-permute-start(bf16[256,1280]{1,0:T(8,128)(2,1)S(1)} %dynamic-slice_bitcast_fusion), channel_id=1, source_target_pairs={{0,1},{1,0},{2,3},{3,2},{4,5},{5,4},{6,7},{7,6},{8,9},{9,8},{10,11... | collective-permute-start | bytes 1966088 | tf_op jit(solution)/shard_map/ppermute | solution.py:121
  28.0 5.9 %collective-permute-start.2 = (bf16[128,1280]{1,0:T(8,128)(2,1)}, bf16[128,1280]{1,0:T(8,128)(2,1)S(1)}, u32[]{:S(2)}, u32[]{:S(2)}) collective-permute-start(bf16[128,1280]{1,0:T(8,128)(2,1)} %bitcast.141), channel_id=1, source_target_pairs={{0,64},{1,65},{2,66},{3,67},{4,68},{5,69},{6,70},{7,71},{8,72},{9,... | collective-permute-start | bytes 983048 | tf_op jit(solution)/shard_map/ppermute | solution.py:19
  34.0 1.9 %collective-permute-start.3 = (f32[12,128]{1,0:T(8,128)S(1)}, f32[12,128]{1,0:T(8,128)S(1)}, u32[]{:S(2)}, u32[]{:S(2)}) collective-permute-start(f32[12,128]{1,0:T(8,128)S(1)} %pad_maximum_fusion.2), channel_id=1, source_target_pairs={{0,32},{1,33},{2,34},{3,35},{4,36},{5,37},{6,38},{7,39},{8,40},{9,... | collective-permute-start | bytes 18440 | tf_op jit(solution)/shard_map/ppermute | solution.py:19
  36.0 2.5 %all-to-all-done = bf16[16,8,1280]{2,1,0:T(8,128)(2,1)S(1)} async-done(((bf16[16,8,1280]{2,1,0:T(8,128)(2,1)}), bf16[16,8,1280]{2,1,0:T(8,128)(2,1)S(1)}, u32[]{:S(2)}, u32[]{:S(2)}) %all-to-all-start) | async-done | bytes 327712 | tf_op jit(solution)/shard_map/all_to_all | solution.py:116
  38.5 2.4 %all_gather.26 = bf16[128,2560]{1,0:T(8,128)(2,1)S(1)} all-gather(bf16[128,1280]{1,0:T(8,128)(2,1)S(1)} %bitcast.128), channel_id=1, replica_groups=mesh['section'=16,'expert'=16,'tensor'=2] {'tensor'}, dimensions={1}, use_global_device_ids=true | all-gather | bytes 983040 | tf_op jit(solution)/shard_map/all_gather | solution.py:76
  40.9 0.2 fusion.7
  41.2 0.4 fusion.19
  41.6 0.9 copy-done.5
  42.5 0.4 fusion.30
  42.8 1.9 %all-gather.1 = bf16[256,256]{1,0:T(8,128)(2,1)S(1)} all-gather(bf16[128,256]{1,0:T(8,128)(2,1)S(1)} %fusion.30), channel_id=3, replica_groups=mesh['section'=16,'expert'=16,'tensor'=2] {'tensor'}, dimensions={0}, use_global_device_ids=true | all-gather | bytes 196608 | tf_op jit(solution)/shard_map/all_gather | solution.py:83
  44.7 0.2 fusion.35
  45.0 0.3 fusion
  45.3 3.3 %collective-permute-start.5 = (bf16[8,8,1280]{2,1,0:T(8,128)(2,1)S(1)}, bf16[8,8,1280]{2,1,0:T(8,128)(2,1)S(1)}, u32[]{:S(2)}, u32[]{:S(2)}) collective-permute-start(bf16[8,8,1280]{2,1,0:T(8,128)(2,1)S(1)} %get-tuple-element.31), channel_id=1, source_target_pairs={{0,34},{1,35},{2,32},{3,33},{4,38},{5,39},{6,36},{7,37},{8,42},{9,... | collective-permute-start | bytes 491528 | tf_op jit(solution)/shard_map/ppermute | solution.py:19
  48.7 5.5 %collective-permute-start.4 = (bf16[8,8,1280]{2,1,0:T(8,128)(2,1)S(1)}, bf16[8,8,1280]{2,1,0:T(8,128)(2,1)S(1)}, u32[]{:S(2)}, u32[]{:S(2)}) collective-permute-start(bf16[8,8,1280]{2,1,0:T(8,128)(2,1)S(1)} %get-tuple-element.30), channel_id=1, source_target_pairs={{0,32},{1,33},{2,34},{3,35},{4,36},{5,37},{6,38},{7,39},{8,40},{9,... | collective-permute-start | bytes 491528 | tf_op jit(solution)/shard_map/ppermute | solution.py:19
  54.2 0.1 fusion.67
  54.3 0.1 fusion.54
  54.4 0.1 fusion.55
  54.6 0.1 fusion.60
  54.7 0.1 fusion.61
  54.7 1.6 %collective-permute-done.5 = bf16[8,8,1280]{2,1,0:T(8,128)(2,1)S(1)} collective-permute-done((bf16[8,8,1280]{2,1,0:T(8,128)(2,1)S(1)}, bf16[8,8,1280]{2,1,0:T(8,128)(2,1)S(1)}, u32[]{:S(2)}, u32[]{:S(2)}) %collective-permute-start.5) | collective-permute-done | bytes 163872 | tf_op jit(solution)/shard_map/ppermute | solution.py:19
  56.4 1.3 %collective-permute-done.4 = bf16[8,8,1280]{2,1,0:T(8,128)(2,1)S(1)} collective-permute-done((bf16[8,8,1280]{2,1,0:T(8,128)(2,1)S(1)}, bf16[8,8,1280]{2,1,0:T(8,128)(2,1)S(1)}, u32[]{:S(2)}, u32[]{:S(2)}) %collective-permute-start.4) | collective-permute-done | bytes 163872 | tf_op jit(solution)/shard_map/ppermute | solution.py:19
  57.7 13.9 %all_to_all.20 = bf16[8,8,1280]{2,1,0:T(8,128)(2,1)S(1)} all-to-all(bf16[8,8,1280]{2,1,0:T(8,128)(2,1)S(1)} %add_convert_fusion.1), channel_id=1, replica_groups={{0,24,16,8,4,12,20,28},{2,26,18,10,6,14,22,30},{1,25,17,9,5,13,21,29},{..., dimensions={0} | all-to-all | bytes 327680 | tf_op jit(solution)/shard_map/all_to_all | solution.py:73
  71.6 0.3 add_convert_fusion
  71.9 0.2 fusion.4
  72.1 17.4 %all_to_all.21 = bf16[16,8,1280]{2,1,0:T(8,128)(2,1)S(1)} all-to-all(bf16[16,8,1280]{2,1,0:T(8,128)(2,1)S(1)} %fusion.4), channel_id=1, replica_groups={{0,24,16,8,4,12,20,28,2,26,18,10,6,14,22,30},{1,25,17,9,5,13,21,29,3,27..., dimensions={0} | all-to-all | bytes 655360 | tf_op jit(solution)/shard_map/all_to_all | solution.py:73
  89.6 2.3 %all_gather.29 = bf16[128,2560]{1,0:T(8,128)(2,1)S(1)} all-gather(bf16[128,1280]{1,0:T(8,128)(2,1)S(1)} %bitcast.130), channel_id=1, replica_groups=mesh['section'=16,'expert'=16,'tensor'=2] {'tensor'}, dimensions={1}, use_global_device_ids=true | all-gather | bytes 983040 | tf_op jit(solution)/shard_map/all_gather | solution.py:76
  91.8 0.2 fusion.10
  92.1 0.4 fusion.17
  92.5 0.4 fusion.27
  92.9 1.9 %all-gather.2 = bf16[256,256]{1,0:T(8,128)(2,1)S(1)} all-gather(bf16[128,256]{1,0:T(8,128)(2,1)S(1)} %fusion.27), channel_id=4, replica_groups=mesh['section'=16,'expert'=16,'tensor'=2] {'tensor'}, dimensions={0}, use_global_device_ids=true | all-gather | bytes 196608 | tf_op jit(solution)/shard_map/all_gather | solution.py:83
  94.8 0.2 fusion.33
  95.0 0.3 fusion.6
  95.3 17.1 %all_to_all.22 = bf16[16,8,1280]{2,1,0:T(8,128)(2,1)S(1)} all-to-all(bf16[16,8,1280]{2,1,0:T(8,128)(2,1)S(1)} %fusion.6), channel_id=1, replica_groups={{0,24,16,8,4,12,20,28,2,26,18,10,6,14,22,30},{1,25,17,9,5,13,21,29,3,27..., dimensions={0} | all-to-all | bytes 655360 | tf_op jit(solution)/shard_map/all_to_all | solution.py:73
  112.4 1.0 fusion.5
  (30 shorter events, 0.2 us)
Async XLA Ops:
  0.0 12.1 %copy-start = (bf16[1,256,2560]{2,1,0:T(8,128)(2,1)S(1)}, bf16[1,256,2560]{2,1,0:T(8,128)(2,1)}, u32[]{:S(2)}) copy-start(bf16[1,256,2560]{2,1,0:T(8,128)(2,1)} %param.11) | copy-start | bytes 3932164
  0.0 14.5 %copy-start.1 = (s32[2,1,128,6]{2,1,3,0:T(1,128)S(1)}, s32[2,1,128,6]{2,1,3,0:T(1,128)}, u32[]{:S(2)}) copy-start(s32[2,1,128,6]{2,1,3,0:T(1,128)} %param.12) | copy-start | bytes 18436
  0.0 13.5 %collective-permute-start = (bf16[128,1280]{1,0:T(8,128)(2,1)}, bf16[128,1280]{1,0:T(8,128)(2,1)S(1)}, u32[]{:S(2)}, u32[]{:S(2)}) collective-permute-start(bf16[128,1280]{1,0:T(8,128)(2,1)} %bitcast.140), channel_id=1, source_target_pairs={{0,32},{1,35},{2,34},{3,33},{4,36},{5,39},{6,38},{7,37},{8,40},{9,... | collective-permute-start | bytes 983048 | tf_op jit(solution)/shard_map/ppermute | solution.py:19
  12.1 21.8 %copy-start.3 = (f32[2,1,128,6]{2,1,3,0:T(1,128)S(1)}, f32[2,1,128,6]{2,1,3,0:T(1,128)}, u32[]{:S(2)}) copy-start(f32[2,1,128,6]{2,1,3,0:T(1,128)} %param.13) | copy-start | bytes 18436
  12.1 23.8 %slice-start = ((s32[2,1,128,6]{2,1,3,0:T(1,128)}), s32[1,1,128,6]{2,1,3,0:T(1,128)S(1)}, s32[]{:S(2)}) async-start(s32[2,1,128,6]{2,1,3,0:T(1,128)} %param.12), calls=%async_computation.4 | async-start | bytes 6144 | tf_op jit(solution)/shard_map/slice | solution.py:127
  12.2 23.8 %copy-start.2 = (bf16[1,2560]{1,0:T(2,128)(2,1)S(1)}, bf16[1,2560]{1,0:T(2,128)(2,1)}, u32[]{:S(2)}) copy-start(bf16[1,2560]{1,0:T(2,128)(2,1)} %param.8) | copy-start | bytes 15364
  14.5 24.0 %all-to-all-start = ((bf16[16,8,1280]{2,1,0:T(8,128)(2,1)}), bf16[16,8,1280]{2,1,0:T(8,128)(2,1)S(1)}, u32[]{:S(2)}, u32[]{:S(2)}) async-start(bf16[16,8,1280]{2,1,0:T(8,128)(2,1)} %fusion.3), calls=%async_computation | async-start | bytes 655360 | tf_op jit(solution)/shard_map/all_to_all | solution.py:116
  26.1 18.9 %collective-permute-start.1 = (bf16[256,1280]{1,0:T(8,128)(2,1)S(1)}, bf16[256,1280]{1,0:T(8,128)(2,1)S(1)}, u32[]{:S(2)}, u32[]{:S(2)}) collective-permute-start(bf16[256,1280]{1,0:T(8,128)(2,1)S(1)} %dynamic-slice_bitcast_fusion), channel_id=1, source_target_pairs={{0,1},{1,0},{2,3},{3,2},{4,5},{5,4},{6,7},{7,6},{8,9},{9,8},{10,11... | collective-permute-start | bytes 1966088 | tf_op jit(solution)/shard_map/ppermute | solution.py:121
  28.0 17.3 %collective-permute-start.2 = (bf16[128,1280]{1,0:T(8,128)(2,1)}, bf16[128,1280]{1,0:T(8,128)(2,1)S(1)}, u32[]{:S(2)}, u32[]{:S(2)}) collective-permute-start(bf16[128,1280]{1,0:T(8,128)(2,1)} %bitcast.141), channel_id=1, source_target_pairs={{0,64},{1,65},{2,66},{3,67},{4,68},{5,69},{6,70},{7,71},{8,72},{9,... | collective-permute-start | bytes 983048 | tf_op jit(solution)/shard_map/ppermute | solution.py:19
  34.0 11.3 %collective-permute-start.3 = (f32[12,128]{1,0:T(8,128)S(1)}, f32[12,128]{1,0:T(8,128)S(1)}, u32[]{:S(2)}, u32[]{:S(2)}) collective-permute-start(f32[12,128]{1,0:T(8,128)S(1)} %pad_maximum_fusion.2), channel_id=1, source_target_pairs={{0,32},{1,33},{2,34},{3,35},{4,36},{5,37},{6,38},{7,39},{8,40},{9,... | collective-permute-start | bytes 18440 | tf_op jit(solution)/shard_map/ppermute | solution.py:19
  38.5 2.6 %copy-start.4 = (bf16[1,2560,256]{2,1,0:T(8,128)(2,1)S(1)}, bf16[1,2560,256]{2,1,0:T(8,128)(2,1)}, u32[]{:S(2)}) copy-start(bf16[1,2560,256]{2,1,0:T(8,128)(2,1)} %param.9) | copy-start | bytes 3932164
  41.1 1.3 %copy-start.5 = (bf16[1,2560,256]{2,1,0:T(8,128)(2,1)S(1)}, bf16[1,2560,256]{2,1,0:T(8,128)(2,1)}, u32[]{:S(2)}) copy-start(bf16[1,2560,256]{2,1,0:T(8,128)(2,1)} %param.10) | copy-start | bytes 3932164
  45.3 11.0 %collective-permute-start.5 = (bf16[8,8,1280]{2,1,0:T(8,128)(2,1)S(1)}, bf16[8,8,1280]{2,1,0:T(8,128)(2,1)S(1)}, u32[]{:S(2)}, u32[]{:S(2)}) collective-permute-start(bf16[8,8,1280]{2,1,0:T(8,128)(2,1)S(1)} %get-tuple-element.31), channel_id=1, source_target_pairs={{0,34},{1,35},{2,32},{3,33},{4,38},{5,39},{6,36},{7,37},{8,42},{9,... | collective-permute-start | bytes 491528 | tf_op jit(solution)/shard_map/ppermute | solution.py:19
  48.7 9.0 %collective-permute-start.4 = (bf16[8,8,1280]{2,1,0:T(8,128)(2,1)S(1)}, bf16[8,8,1280]{2,1,0:T(8,128)(2,1)S(1)}, u32[]{:S(2)}, u32[]{:S(2)}) collective-permute-start(bf16[8,8,1280]{2,1,0:T(8,128)(2,1)S(1)} %get-tuple-element.30), channel_id=1, source_target_pairs={{0,32},{1,33},{2,34},{3,35},{4,36},{5,37},{6,38},{7,39},{8,40},{9,... | collective-permute-start | bytes 491528 | tf_op jit(solution)/shard_map/ppermute | solution.py:19
